TPU v7x, 32 devices: a whole 2x2x4 slice. The times are simulated.
32 devices in a mesh: groups: 2 (over x), wide: 16 (over z, y, core).
Axes of the slice: x: 2, y: 2, z: 4, core: 2. Of those that a mesh axis runs over, the one named last changes fastest.
Arguments:
- iterate: float32 [8192, 128], P(('groups', 'wide')), parts along dimension 0, may hold values from -6 to 6
- rhs: float32 [8192, 128], P(('groups', 'wide')), parts along dimension 0, may hold values from -6 to 6
- schur: float32 [32, 384, 384], P(('groups', 'wide')), parts along dimension 0
- near_block: float32 [8192, 256], P(('groups', 'wide')), parts along dimension 0
- u_basis: float32 [32, 32, 4096], P('groups', None, 'wide'), parts along dimension 0, may hold values from -0.375 to 0.375
- v_basis: float32 [32, 32, 4096], P('groups', None, 'wide'), parts along dimension 0, may hold values from -0.375 to 0.375
- tile_rank: int32 [32, 16], P('groups', 'wide'), parts along dimension 0, may hold values from 1 to 32
- send_rows: int32 [32, 3, 128], P(('groups', 'wide')), parts along dimension 0, may hold values from 0 to 255
- send_count: int32 [32, 3], P(('groups', 'wide')), parts along dimension 0, may hold values from 0 to 128, as said below
- precond: float32 [8192], P(('groups', 'wide')), parts along dimension 0, may hold values from 0.1 to 1
Outputs:
- updated: float32 [8192, 128], P(('groups', 'wide')), parts along dimension 0
- residual: float32 [8192, 128], P(('groups', 'wide')), parts along dimension 0
There are 2 independent parts, one for each index of `groups`. A program takes and returns all parts, laid end to end along the dimension named above; each array names one. Nothing has to cross between parts.
Inputs may be any that keep to these rules, and one draw needn't show every extreme that they name: send_count[p, 0] is 0 for p = 0 and send_count[p, 2] is 0 for p = 15; a block is full in every draw.
All inputs are finite; a program needn't handle non-finite values.
Results may differ from a plain program's by a relative error of at most 0.0003.
Values sent between devices are 32-bit elements; how exact they have to be, the bound alone decides.
No kernel may reach another device: no remote copies, remote signals or barrier semaphores. Data moves between devices by JAX's collectives and lax.ppermute only.
A program may use at most 64 MiB of HBM per device.

v0:
```python
import jax
import jax.numpy as jnp
from jax import lax
from jax.sharding import PartitionSpec as P


def shifted(block, axis, distance):
    devices = range(lax.axis_size(axis))
    route = [(i - distance, i) for i in devices if i - distance in devices]
    return lax.ppermute(block, axis, route)


def body(
    iterate, rhs, schur, near_block, u_basis, v_basis, tile_rank, send_rows, send_count, precond
):
    highest = lax.Precision.HIGHEST
    rows_here = iterate.shape[0]
    loads = iterate.shape[1]
    face_rows = send_rows.shape[2]
    slots_all = 3 * face_rows
    tiles = u_basis.shape[0]
    rank_top = u_basis.shape[1]
    rows_local = jnp.arange(rows_here, dtype=jnp.int32)
    slot_ids = jnp.arange(face_rows, dtype=jnp.int32)
    valid = (slot_ids[None, :] < send_count[0][:, None]).reshape(slots_all)
    flat_rows = send_rows[0].reshape(slots_all)
    select = ((flat_rows[:, None] == rows_local[None, :]) & valid[:, None]).astype(jnp.float32)
    outgoing = jnp.dot(select, iterate, precision=highest, preferred_element_type=jnp.float32)
    outgoing = outgoing.reshape(3, face_rows, loads)
    pieces = [None, outgoing[1], None]
    for slot, offset in ((0, -1), (2, 1)):
        pieces[slot] = shifted(outgoing[slot], "wide", offset)
    incoming = jnp.stack(pieces, axis=0)
    forces = jnp.dot(
        schur[0],
        incoming.reshape(slots_all, loads),
        precision=highest,
        preferred_element_type=jnp.float32,
    ).reshape(3, face_rows, loads)
    pieces = [None, forces[1], None]
    for slot, offset in ((0, -1), (2, 1)):
        pieces[slot] = shifted(forces[slot], "wide", -offset)
    returned = jnp.stack(pieces, axis=0)
    fem = lax.dot_general(
        select,
        returned.reshape(slots_all, loads),
        (((0,), (0,)), ((), ())),
        precision=highest,
        preferred_element_type=jnp.float32,
    )
    coeff = jnp.dot(
        v_basis.reshape(tiles * rank_top, rows_here),
        iterate,
        precision=highest,
        preferred_element_type=jnp.float32,
    ).reshape(tiles, rank_top, loads)
    keep = (jnp.arange(rank_top, dtype=jnp.int32)[None, :] < tile_rank).astype(jnp.float32)
    coeff = coeff * keep[:, :, None]
    u_flat = u_basis.reshape(tiles * rank_top, rows_here)
    gathered = lax.all_to_all(coeff, "wide", split_axis=0, concat_axis=0, tiled=True)
    far = lax.dot_general(
        u_flat,
        gathered.reshape(tiles * rank_top, gathered.shape[2]),
        (((0,), (0,)), ((), ())),
        precision=highest,
        preferred_element_type=jnp.float32,
    )
    near = jnp.dot(near_block, iterate, precision=highest, preferred_element_type=jnp.float32)
    residual = rhs - (fem + (far + near))
    updated = iterate + precond[:, None] * residual
    return (updated, residual)


def solution(mesh):
    in_specs = (
        P(("groups", "wide"), None),
        P(("groups", "wide"), None),
        P(("groups", "wide"), None, None),
        P(("groups", "wide"), None),
        P("groups", None, "wide"),
        P("groups", None, "wide"),
        P("groups", "wide"),
        P(("groups", "wide"), None, None),
        P(("groups", "wide"), None),
        P(("groups", "wide")),
    )
    out_specs = (P(("groups", "wide"), None), P(("groups", "wide"), None))
    return jax.shard_map(body, mesh=mesh, in_specs=in_specs, out_specs=out_specs, check_vma=False)
```

profile of v0, /device:TPU:1, one launch (start us, length us, event | category | flops | bytes accessed | tf_op | source)
XLA Modules:
  0.0 29.9 jit_solution(5099675021365020917)
XLA Ops:
  0.6 0.0 copy-start
  0.6 0.0 copy-start.9
  0.7 0.0 copy-start.6
  0.7 0.0 copy-start.2
  0.7 0.7 %copy-done.9 = s32[1,3]{1,0:T(1,128)S(1)} copy-done((s32[1,3]{1,0:T(1,128)S(1)}, s32[1,3]{1,0:T(1,128)}, u32[]{:S(2)}) %copy-start.9) | copy-done | bytes 36
  1.4 0.1 fusion.14
  1.4 0.0 copy-done.6
  1.5 1.3 %fusion.6 = f32[384,128]{1,0:T(8,128)S(1)} fusion(f32[256,128]{1,0:T(8,128)} %param.10, s32[384]{0:T(512)S(1)} %bitcast.41, pred[384]{0:T(512)(128)(4,1)S(1)} %fusion.14), kind=kOutput, calls=%fused_computation.10 | convolution fusion | flops 151191552 | bytes 329600 | tf_op jit(solution)/shard_map/dot_general | solution.py:28
  2.8 0.0 copy-start.1
  2.8 2.1 %collective-permute-start = (f32[128,128]{1,0:T(8,128)S(1)}, f32[128,128]{1,0:T(8,128)S(1)}, u32[]{:S(2)}, u32[]{:S(2)}) collective-permute-start(f32[128,128]{1,0:T(8,128)S(1)} %get-tuple-element.5), channel_id=1, source_target_pairs={{1,0},{2,1},{3,2},{4,3},{5,4},{6,5},{7,6},{8,7},{9,8},{10,9},{11,1... | collective-permute-start | bytes 196616 | tf_op jit(solution)/shard_map/ppermute | solution.py:10
  4.9 0.0 copy-start.8
  4.9 4.5 %collective-permute-start.1 = (f32[128,128]{1,0:T(8,128)S(1)}, f32[128,128]{1,0:T(8,128)S(1)}, u32[]{:S(2)}, u32[]{:S(2)}) collective-permute-start(f32[128,128]{1,0:T(8,128)S(1)} %get-tuple-element.6), channel_id=1, source_target_pairs={{0,1},{1,2},{2,3},{3,4},{4,5},{5,6},{6,7},{7,8},{8,9},{9,10},{10,1... | collective-permute-start | bytes 196616 | tf_op jit(solution)/shard_map/ppermute | solution.py:10
  9.4 0.0 copy-done.8
  9.4 0.1 fusion.13
  9.5 0.0 copy-done.2
  9.5 0.0 copy-done.1
  9.5 1.3 %convolution_multiply_fusion = f32[16,32,128]{2,1,0:T(8,128)} fusion(f32[16,32,256]{2,1,0:T(8,128)S(1)} %copy-done.2, f32[256,128]{1,0:T(8,128)S(1)} %copy-done.1, f32[16,32]{1,0:T(8,128)S(1)} %fusion.13), kind=kOutput, calls=%fused_computation | convolution fusion | flops 201392128 | bytes 919552 | tf_op jit(solution)/shard_map/dot_general | solution.py:51
  10.8 5.8 %all-to-all-start = ((f32[16,32,128]{2,1,0:T(8,128)}), f32[16,32,128]{2,1,0:T(8,128)S(1)}, u32[]{:S(2)}, u32[]{:S(2)}) async-start(f32[16,32,128]{2,1,0:T(8,128)} %convolution_multiply_fusion), calls=%async_computation | async-start | bytes 524288 | tf_op jit(solution)/shard_map/all_to_all | solution.py:60
  16.6 0.0 collective-permute-done
  16.6 0.0 collective-permute-done.1
  16.6 0.0 copy-done
  16.6 0.8 %convolution_bitcast_fusion = f32[384,128]{0,1:T(8,128)S(1)} fusion(f32[384,128]{1,0:T(8,128)S(1)} %bitcast.36, f32[1,384,384]{2,1,0:T(8,128)S(1)} %copy-done), kind=kOutput, calls=%fused_computation.1 | convolution fusion | flops 226492416 | bytes 983040 | tf_op jit(solution)/shard_map/dot_general | solution.py:34
  17.5 3.5 %collective-permute-start.2 = (f32[128,128]{0,1:T(8,128)S(1)}, f32[128,128]{0,1:T(8,128)S(1)}, u32[]{:S(2)}, u32[]{:S(2)}) collective-permute-start(f32[128,128]{0,1:T(8,128)S(1)} %get-tuple-element.2), channel_id=1, source_target_pairs={{0,1},{1,2},{2,3},{3,4},{4,5},{5,6},{6,7},{7,8},{8,9},{9,10},{10,1... | collective-permute-start | bytes 196616 | tf_op jit(solution)/shard_map/ppermute | solution.py:10
  21.0 1.9 %collective-permute-start.3 = (f32[128,128]{0,1:T(8,128)S(1)}, f32[128,128]{0,1:T(8,128)S(1)}, u32[]{:S(2)}, u32[]{:S(2)}) collective-permute-start(f32[128,128]{0,1:T(8,128)S(1)} %get-tuple-element.3), channel_id=1, source_target_pairs={{1,0},{2,1},{3,2},{4,3},{5,4},{6,5},{7,6},{8,7},{9,8},{10,9},{11,1... | collective-permute-start | bytes 196616 | tf_op jit(solution)/shard_map/ppermute | solution.py:10
  23.0 0.0 collective-permute-done.2
  23.0 3.8 %collective-permute-done.3 = f32[128,128]{0,1:T(8,128)S(1)} collective-permute-done((f32[128,128]{0,1:T(8,128)S(1)}, f32[128,128]{0,1:T(8,128)S(1)}, u32[]{:S(2)}, u32[]{:S(2)}) %collective-permute-start.3) | collective-permute-done | bytes 65568 | tf_op jit(solution)/shard_map/ppermute | solution.py:10
  26.7 0.0 copy-start.3
  26.7 0.1 copy.13
  26.9 0.6 %fusion.4 = f32[256,128]{1,0:T(8,128)S(1)} fusion(f32[384,128]{1,0:T(8,128)S(1)} %bitcast.35, s32[384]{0:T(512)S(1)} %bitcast.42, pred[384]{0:T(512)(128)(4,1)S(1)} %fusion.14), kind=kOutput, calls=%fused_computation.9 | convolution fusion | flops 151191552 | bytes 329600 | tf_op jit(solution)/shard_map/dot_general | solution.py:44
  27.5 0.0 copy-start.4
  27.5 0.0 copy-start.5
  27.5 0.0 copy-start.7
  27.6 0.0 all-to-all-done
  27.6 0.2 copy-done.3
  27.8 1.0 %convolution_bitcast_fusion.1 = f32[256,128]{1,0:T(8,128)S(1)} fusion(f32[16,32,128]{2,1,0:T(8,128)S(1)} %all-to-all-done, f32[16,32,256]{2,1,0:T(8,128)S(1)} %copy-done.3), kind=kOutput, calls=%fused_computation.5 | convolution fusion | flops 201326592 | bytes 917504 | tf_op jit(solution)/shard_map/dot_general | solution.py:61
  28.8 0.0 copy-done.4
  28.8 0.0 copy-done.5
  28.8 0.0 copy-done.7
  28.8 1.1 %multiply_add_fusion = (f32[256,128]{1,0:T(8,128)}, f32[256,128]{1,0:T(8,128)}) fusion(f32[256,128]{1,0:T(8,128)S(1)} %copy-done.1, f32[256]{0:T(256)S(1)} %copy-done.7, f32[256,128]{1,0:T(8,128)S(1)} %copy-done.5, f32[256,128]{1,0:T(8,128)S(1)} %fusion.4, f32[256,128]{1,0:T(8,128)S(1)} %convolution_bitcast_fusion.1, f32[256,256]{1,0:T(8,128)S(1)} %copy-done.4), kind=kOutput, calls=%fused_computation.18 | convolution fusion | flops 100827136 | bytes 1049600 | tf_op jit(solution)/shard_map/dot_general | solution.py:68
  (5 shorter events, 0.1 us)
Async XLA Ops:
  0.6 16.0 %copy-start = (f32[1,384,384]{2,1,0:T(8,128)S(1)}, f32[1,384,384]{2,1,0:T(8,128)}, u32[]{:S(2)}) copy-start(f32[1,384,384]{2,1,0:T(8,128)} %param.12) | copy-start | bytes 1769476
  0.6 0.7 %copy-start.9 = (s32[1,3]{1,0:T(1,128)S(1)}, s32[1,3]{1,0:T(1,128)}, u32[]{:S(2)}) copy-start(s32[1,3]{1,0:T(1,128)} %param.18) | copy-start | bytes 40
  0.7 0.8 %copy-start.6 = (s32[1,3,128]{2,0,1:T(1,128)S(1)}, s32[1,3,128]{2,0,1:T(1,128)}, u32[]{:S(2)}) copy-start(s32[1,3,128]{2,0,1:T(1,128)} %param.17) | copy-start | bytes 4612
  0.7 8.8 %copy-start.2 = (f32[16,32,256]{2,1,0:T(8,128)S(1)}, f32[16,32,256]{2,1,0:T(8,128)}, u32[]{:S(2)}) copy-start(f32[16,32,256]{2,1,0:T(8,128)} %param.15) | copy-start | bytes 1572868
  2.8 6.7 %copy-start.1 = (f32[256,128]{1,0:T(8,128)S(1)}, f32[256,128]{1,0:T(8,128)}, u32[]{:S(2)}) copy-start(f32[256,128]{1,0:T(8,128)} %param.10) | copy-start | bytes 393220
  2.8 13.8 %collective-permute-start = (f32[128,128]{1,0:T(8,128)S(1)}, f32[128,128]{1,0:T(8,128)S(1)}, u32[]{:S(2)}, u32[]{:S(2)}) collective-permute-start(f32[128,128]{1,0:T(8,128)S(1)} %get-tuple-element.5), channel_id=1, source_target_pairs={{1,0},{2,1},{3,2},{4,3},{5,4},{6,5},{7,6},{8,7},{9,8},{10,9},{11,1... | collective-permute-start | bytes 196616 | tf_op jit(solution)/shard_map/ppermute | solution.py:10
  4.9 4.5 %copy-start.8 = (s32[16,1]{0,1:T(1,128)S(1)}, s32[16,1]{0,1:T(1,128)}, u32[]{:S(2)}) copy-start(s32[16,1]{0,1:T(1,128)} %param.16) | copy-start | bytes 196
  4.9 11.7 %collective-permute-start.1 = (f32[128,128]{1,0:T(8,128)S(1)}, f32[128,128]{1,0:T(8,128)S(1)}, u32[]{:S(2)}, u32[]{:S(2)}) collective-permute-start(f32[128,128]{1,0:T(8,128)S(1)} %get-tuple-element.6), channel_id=1, source_target_pairs={{0,1},{1,2},{2,3},{3,4},{4,5},{5,6},{6,7},{7,8},{8,9},{9,10},{10,1... | collective-permute-start | bytes 196616 | tf_op jit(solution)/shard_map/ppermute | solution.py:10
  10.8 16.8 %all-to-all-start = ((f32[16,32,128]{2,1,0:T(8,128)}), f32[16,32,128]{2,1,0:T(8,128)S(1)}, u32[]{:S(2)}, u32[]{:S(2)}) async-start(f32[16,32,128]{2,1,0:T(8,128)} %convolution_multiply_fusion), calls=%async_computation | async-start | bytes 524288 | tf_op jit(solution)/shard_map/all_to_all | solution.py:60
  17.5 5.5 %collective-permute-start.2 = (f32[128,128]{0,1:T(8,128)S(1)}, f32[128,128]{0,1:T(8,128)S(1)}, u32[]{:S(2)}, u32[]{:S(2)}) collective-permute-start(f32[128,128]{0,1:T(8,128)S(1)} %get-tuple-element.2), channel_id=1, source_target_pairs={{0,1},{1,2},{2,3},{3,4},{4,5},{5,6},{6,7},{7,8},{8,9},{9,10},{10,1... | collective-permute-start | bytes 196616 | tf_op jit(solution)/shard_map/ppermute | solution.py:10
  21.0 5.7 %collective-permute-start.3 = (f32[128,128]{0,1:T(8,128)S(1)}, f32[128,128]{0,1:T(8,128)S(1)}, u32[]{:S(2)}, u32[]{:S(2)}) collective-permute-start(f32[128,128]{0,1:T(8,128)S(1)} %get-tuple-element.3), channel_id=1, source_target_pairs={{1,0},{2,1},{3,2},{4,3},{5,4},{6,5},{7,6},{8,7},{9,8},{10,9},{11,1... | collective-permute-start | bytes 196616 | tf_op jit(solution)/shard_map/ppermute | solution.py:10
  26.7 1.0 %copy-start.3 = (f32[16,32,256]{2,1,0:T(8,128)S(1)}, f32[16,32,256]{2,1,0:T(8,128)}, u32[]{:S(2)}) copy-start(f32[16,32,256]{2,1,0:T(8,128)} %param.14) | copy-start | bytes 1572868
  27.5 1.2 %copy-start.4 = (f32[256,256]{1,0:T(8,128)S(1)}, f32[256,256]{1,0:T(8,128)}, u32[]{:S(2)}) copy-start(f32[256,256]{1,0:T(8,128)} %param.13) | copy-start | bytes 786436
  27.5 1.2 %copy-start.5 = (f32[256,128]{1,0:T(8,128)S(1)}, f32[256,128]{1,0:T(8,128)}, u32[]{:S(2)}) copy-start(f32[256,128]{1,0:T(8,128)} %param.11) | copy-start | bytes 393220
  27.5 1.2 %copy-start.7 = (f32[256]{0:T(256)S(1)}, f32[256]{0:T(256)}, u32[]{:S(2)}) copy-start(f32[256]{0:T(256)} %param.19) | copy-start | bytes 3076
where the time goes:
time: 30.2 us; the launch traced here: 29.9 us
  starting transfers between devices  17.8 us (59%)
  matrix products  6.11 us (20%)
  waiting for transfers between devices  3.78 us (13%)
  local copies, waits for them, and re-layouts  1.1 us (4%)
  between operations  0.86 us (3%)
    ppermute x4, starting transfers between devices, shifted(): return lax.ppermute(block, axis, route)  12.1 us
    all_to_all x1, starting transfers between devices, body(): lax.all_to_all(coeff, 'wide', split_axis=0, concat_axis=0, tiled=True)  5.78 us
    ppermute x4, waiting for transfers between devices, shifted(): return lax.ppermute(block, axis, route)  3.77 us
    dot_general x1, matrix products, body(): jnp.dot(select, iterate, precision=highest, preferred_element_type=jnp.fl...  1.3 us
    dot_general x1, matrix products, body(): jnp.dot(v_basis.reshape(tiles * rank_top, rows_here), iterate, precision=...  1.28 us
    dot_general x1, matrix products, body(): jnp.dot(near_block, iterate, precision=highest, preferred_element_type=jn...  1.08 us
    dot_general x1, matrix products, body(): lax.dot_general(u_flat, gathered.reshape(tiles * rank_top, gathered.shape...  0.99 us
    unnamed x20, local copies, waits for them, and re-layouts  0.94 us
  transfers between devices with their start and end apart: 5, of which 1 were waited for; matrix products, arithmetic and copies ran while one was open for 10% of the time, Pallas kernels for 0%

commit v1 on v0

v1 whole, which is shorter than its diff:
```python
import functools

import jax
import jax.numpy as jnp
from jax import lax
from jax.experimental import pallas as pl
from jax.experimental.pallas import tpu as pltpu
from jax.sharding import PartitionSpec as P

VMEM = pl.BlockSpec(memory_space=pltpu.VMEM)
SMEM = pl.BlockSpec(memory_space=pltpu.SMEM)
f32 = jnp.float32
bf16 = jnp.bfloat16


def halves(a):
    hi = a.astype(bf16)
    return hi, (a - hi.astype(f32)).astype(bf16)


def dot(a, b):
    return jnp.dot(a, b, preferred_element_type=f32)


def wide_halves(a):
    return jnp.concatenate(halves(a), axis=1)


def product(a, b_wide):
    n = b_wide.shape[1] // 2
    hi, lo = halves(a)
    both = dot(hi, b_wide)
    return both[:, :n] + (both[:, n:] + dot(lo, b_wide[:, :n]))


def face_slot(spot, odd):
    return 1 if spot == 1 else jnp.where(odd == spot // 2, 2, 0)


def live_rows(rows_ref, count_ref, slot):
    rows = rows_ref[pl.ds(slot, 1), :]
    lane = lax.broadcasted_iota(jnp.int32, rows.shape, 1)
    return jnp.where(lane < count_ref[slot], rows, -1)


def send_kernel(rank_ref, count_ref, odd_ref, x_ref, v_ref, rows_ref, coeff_ref, a_ref, m_ref, b_ref):
    loads = x_ref.shape[1]
    n_rows = x_ref.shape[0]
    x_wide = wide_halves(x_ref[...])
    odd = odd_ref[0]
    for spot, out_ref in enumerate((a_ref, m_ref, b_ref)):
        rows = live_rows(rows_ref, count_ref, face_slot(spot, odd))
        local = lax.broadcasted_iota(jnp.int32, (n_rows, rows.shape[1]), 0)
        select = (local == rows).astype(f32).T.astype(bf16)
        both = dot(select, x_wide)
        out_ref[...] = both[:, :loads] + both[:, loads:]
    tiles, top, _ = v_ref.shape
    step = max(1, min(tiles, 256 // top))

    @pl.loop(0, tiles // step, unroll=tiles <= 32)
    def _(s):
        first = s * step
        part = v_ref[pl.ds(first, step)].reshape(step * top, n_rows)
        out = product(part, x_wide).reshape(step, top, loads)
        k = lax.broadcasted_iota(jnp.int32, (top, loads), 0)
        for t in range(step):
            coeff_ref[first + t] = jnp.where(k < rank_ref[first + t], out[t], 0.0)


def schur_kernel(odd_ref, a_ref, m_ref, b_ref, schur_ref, fa_ref, fm_ref, fb_ref):
    odd = odd_ref[0]
    face = a_ref.shape[0]
    is_odd = odd == 1
    a, b = a_ref[...], b_ref[...]
    first = jnp.where(is_odd, b, a)
    last = jnp.where(is_odd, a, b)
    incoming = wide_halves(jnp.concatenate([first, m_ref[...], last], axis=0))
    starts = (jnp.where(is_odd, 2 * face, 0), face, jnp.where(is_odd, 0, 2 * face))
    for start, out_ref in zip(starts, (fa_ref, fm_ref, fb_ref)):
        start = pl.multiple_of(start, face)
        out_ref[...] = product(schur_ref[pl.ds(start, face), :], incoming)


def base_kernel(count_ref, odd_ref, rhs_ref, near_ref, x_ref, rows_ref, fa_ref, fm_ref, fb_ref, u_ref, base_ref, hi_ref, lo_ref):
    n_rows, loads = x_ref.shape
    odd = odd_ref[0]
    total = rhs_ref[...] - product(near_ref[...], wide_halves(x_ref[...]))
    for spot, f_ref in enumerate((fa_ref, fm_ref, fb_ref)):
        rows = live_rows(rows_ref, count_ref, face_slot(spot, odd))
        local = lax.broadcasted_iota(jnp.int32, (n_rows, rows.shape[1]), 0)
        both = dot((local == rows).astype(f32).astype(bf16), wide_halves(f_ref[...]))
        total = total - (both[:, :loads] + both[:, loads:])
    base_ref[...] = total
    ut = u_ref[...].T
    hi_ref[...], lo_ref[...] = halves(ut)


def final_kernel(coeff_ref, hi_ref, lo_ref, base_ref, x_ref, p_ref, up_ref, res_ref):
    loads = x_ref.shape[1]
    c_wide = wide_halves(coeff_ref[...])
    both = dot(hi_ref[...], c_wide)
    far = both[:, :loads] + (both[:, loads:] + dot(lo_ref[...], c_wide[:, :loads]))
    res = base_ref[...] - far
    res_ref[...] = res
    scale = jnp.broadcast_to(p_ref[...], (8, p_ref.shape[1])).T[:, :1]
    up_ref[...] = x_ref[...] + scale * res


def call(kernel, outs, specs, name):
    return pl.pallas_call(
        kernel,
        out_shape=tuple(jax.ShapeDtypeStruct(s, t) for s, t in outs),
        in_specs=specs,
        out_specs=tuple(VMEM for _ in outs),
        compiler_params=pltpu.CompilerParams(vmem_limit_bytes=40 * 2**20),
        name=name,
    )


def body(iterate, rhs, schur, near_block, u_basis, v_basis, tile_rank, send_rows, send_count, precond):
    n_rows, loads = iterate.shape
    face = send_rows.shape[2]
    tiles, top, _ = u_basis.shape
    size = lax.axis_size("wide")
    odd = jnp.reshape(lax.axis_index("wide") % 2, (1,)).astype(jnp.int32)
    inside = [(i, i ^ 1) for i in range(size) if i ^ 1 < size]
    across = [(i, j) for i in range(size) for j in [i - 1 if i % 2 == 0 else i + 1] if 0 <= j < size]
    rank = tile_rank.reshape(tiles)
    count = send_count.reshape(3)
    rows = send_rows.reshape(3, face)
    block = ((face, loads), f32)

    coeff, out_a, out_m, out_b = call(
        send_kernel, [((tiles, top, loads), f32), block, block, block], [SMEM] * 3 + [VMEM] * 3, "send"
    )(rank, count, odd, iterate, v_basis, rows)
    gathered = lax.all_to_all(coeff, "wide", split_axis=0, concat_axis=0, tiled=True)
    in_a = lax.ppermute(out_a, "wide", inside)
    in_b = lax.ppermute(out_b, "wide", across)
    f_a, f_m, f_b = call(schur_kernel, [block] * 3, [SMEM] + [VMEM] * 4, "schur")(
        odd, in_a, out_m, in_b, schur.reshape(3 * face, 3 * face)
    )
    back_a = lax.ppermute(f_a, "wide", inside)
    back_b = lax.ppermute(f_b, "wide", across)
    base, u_hi, u_lo = call(
        base_kernel,
        [((n_rows, loads), f32), ((n_rows, tiles * top), bf16), ((n_rows, tiles * top), bf16)],
        [SMEM] * 2 + [VMEM] * 8,
        "base",
    )(count, odd, rhs, near_block, iterate, rows, back_a, f_m, back_b, u_basis.reshape(tiles * top, n_rows))
    return call(final_kernel, [((n_rows, loads), f32)] * 2, [VMEM] * 6, "final")(
        gathered.reshape(tiles * top, loads), u_hi, u_lo, base, iterate, precond.reshape(1, n_rows)
    )


def solution(mesh):
    rows = P(("groups", "wide"), None)
    block = P(("groups", "wide"), None, None)
    basis = P("groups", None, "wide")
    in_specs = (rows, rows, block, rows, basis, basis, P("groups", "wide"), block, rows, P(("groups", "wide")))
    return jax.shard_map(body, mesh=mesh, in_specs=in_specs, out_specs=(rows, rows), check_vma=False)
```

time: 30.2 us -> 31.2 us (1.033)
  the two profiles are of different devices: /device:TPU:1 before, /device:TPU:19 now
where the time goes in v1:
time: 31.2 us; the launch traced here: 30.9 us
  starting transfers between devices  14.9 us (48%)
  waiting for transfers between devices  7.35 us (24%)
  local copies, waits for them, and re-layouts  3.98 us (13%)
  Pallas kernels  3.91 us (13%)
  between operations  0.73 us (2%)
    all_to_all x1, starting transfers between devices, body(): lax.all_to_all(coeff, 'wide', split_axis=0, concat_axis=0, tiled=True)  6.63 us
    ppermute x1, waiting for transfers between devices, body(): back_b = lax.ppermute(f_b, 'wide', across)  4.35 us
    unnamed x23, local copies, waits for them, and re-layouts  3.98 us
    ppermute x1, starting transfers between devices, body(): in_b = lax.ppermute(out_b, 'wide', across)  3.11 us
    ppermute x1, waiting for transfers between devices, body(): in_b = lax.ppermute(out_b, 'wide', across)  3 us
    ppermute x1, starting transfers between devices, body(): back_a = lax.ppermute(f_a, 'wide', inside)  2.84 us
    ppermute x1, starting transfers between devices, body(): back_b = lax.ppermute(f_b, 'wide', across)  1.91 us
    pallas_call x1, Pallas kernels, body(): call(send_kernel, [((tiles, top, loads), f32), block, block, block], [SME...  1.65 us
  transfers between devices with their start and end apart: 5, of which 2 were waited for; matrix products, arithmetic and copies ran while one was open for 0% of the time, Pallas kernels for 4%

profile of v1, /device:TPU:19, one launch (start us, length us, event | category | flops | bytes accessed | tf_op | source)
XLA Modules:
  0.0 30.9 jit_solution(13278924771669269450)
XLA Ops:
  0.6 0.0 copy-start.10
  0.6 0.7 %copy-done.10 = s32[1,3,128]{2,0,1:T(1,128)S(1)} copy-done((s32[1,3,128]{2,0,1:T(1,128)S(1)}, s32[1,3,128]{2,0,1:T(1,128)}, u32[]{:S(2)}) %copy-start.10) | copy-done | bytes 1560
  1.3 0.0 copy-start.7
  1.3 0.0 copy-start.9
  1.3 0.7 %copy-done.7 = s32[1,3]{1,0:T(1,128)S(1)} copy-done((s32[1,3]{1,0:T(1,128)S(1)}, s32[1,3]{1,0:T(1,128)}, u32[]{:S(2)}) %copy-start.7) | copy-done | bytes 36
  2.0 0.0 copy-done.9
  2.0 0.0 copy-start
  2.0 0.9 %copy-done = f32[256,128]{1,0:T(8,128)S(1)} copy-done((f32[256,128]{1,0:T(8,128)S(1)}, f32[256,128]{1,0:T(8,128)}, u32[]{:S(2)}) %copy-start) | copy-done | bytes 131096
  2.9 0.0 copy-start.3
  2.9 1.0 %copy-done.3 = f32[16,32,256]{2,1,0:T(8,128)S(1)} copy-done((f32[16,32,256]{2,1,0:T(8,128)S(1)}, f32[16,32,256]{2,1,0:T(8,128)}, u32[]{:S(2)}) %copy-start.3) | copy-done | bytes 524312
  3.9 0.0 copy-start.2
  3.9 1.6 %send.1 = (f32[16,32,128]{2,1,0:T(8,128)}, f32[128,128]{1,0:T(8,128)S(1)}, f32[128,128]{1,0:T(8,128)S(1)}, f32[128,128]{1,0:T(8,128)S(1)}) custom-call(s32[16]{0:T(128)S(1)} %bitcast.18, s32[3]{0:T(128)S(1)} %bitcast.15, s32[1]{0:T(128)} %bitcast.2.odd_ref, f32[256,128]{1,0:T(8,128)S(1)} %copy-done, f32[16,32,256]{2,1,0:T(8,128)S(1)} %copy-done.3, ...), custom_call_target="tpu_custom_call" | custom-call | tf_op jit(solution)/shard_map/send/pallas_call | solution.py:133
  5.6 0.0 copy-start.5
  5.6 6.6 %all-to-all-start = ((f32[16,32,128]{2,1,0:T(8,128)}), f32[16,32,128]{2,1,0:T(8,128)S(1)}, u32[]{:S(2)}, u32[]{:S(2)}) async-start(f32[16,32,128]{2,1,0:T(8,128)} %get-tuple-element.12), calls=%async_computation | async-start | bytes 524288 | tf_op jit(solution)/shard_map/all_to_all | solution.py:136
  12.2 0.0 copy-start.4
  12.2 0.4 %collective-permute-start = (f32[128,128]{1,0:T(8,128)S(1)}, f32[128,128]{1,0:T(8,128)S(1)}, u32[]{:S(2)}, u32[]{:S(2)}) collective-permute-start(f32[128,128]{1,0:T(8,128)S(1)} %get-tuple-element.13), channel_id=1, source_target_pairs={{0,1},{1,0},{2,3},{3,2},{4,5},{5,4},{6,7},{7,6},{8,9},{9,8},{10,11... | collective-permute-start | bytes 196616 | tf_op jit(solution)/shard_map/ppermute | solution.py:137
  12.7 3.1 %collective-permute-start.1 = (f32[128,128]{1,0:T(8,128)S(1)}, f32[128,128]{1,0:T(8,128)S(1)}, u32[]{:S(2)}, u32[]{:S(2)}) collective-permute-start(f32[128,128]{1,0:T(8,128)S(1)} %get-tuple-element.15), channel_id=1, source_target_pairs={{1,2},{2,1},{3,4},{4,3},{5,6},{6,5},{7,8},{8,7},{9,10},{10,9},{11,... | collective-permute-start | bytes 196616 | tf_op jit(solution)/shard_map/ppermute | solution.py:138
  15.8 0.0 collective-permute-done.a_ref
  15.8 3.0 %collective-permute-done.1.b_ref = f32[128,128]{1,0:T(8,128)S(1)} collective-permute-done((f32[128,128]{1,0:T(8,128)S(1)}, f32[128,128]{1,0:T(8,128)S(1)}, u32[]{:S(2)}, u32[]{:S(2)}) %collective-permute-start.1) | collective-permute-done | bytes 65568 | tf_op jit(solution)/shard_map/ppermute | solution.py:138
  18.8 0.0 copy-done.2
  18.8 0.0 copy-start.1
  18.8 0.0 copy-start.6
  18.8 0.3 %schur.1 = (f32[128,128]{1,0:T(8,128)S(1)}, f32[128,128]{1,0:T(8,128)S(1)}, f32[128,128]{1,0:T(8,128)S(1)}) custom-call(s32[1]{0:T(128)} %bitcast.2.odd_ref, f32[128,128]{1,0:T(8,128)S(1)} %collective-permute-done.a_ref, f32[128,128]{1,0:T(8,128)S(1)} %get-tuple-element.14.m_ref, f32[128,128]{1,0:T(8,128)S(1)} %collective-permute-done.1.b_ref, ...), custom_call_target="tpu_custom_call" | custom-call | tf_op jit(solution)/shard_map/schur/pallas_call | solution.py:139
  19.1 2.8 %collective-permute-start.2 = (f32[128,128]{1,0:T(8,128)S(1)}, f32[128,128]{1,0:T(8,128)S(1)}, u32[]{:S(2)}, u32[]{:S(2)}) collective-permute-start(f32[128,128]{1,0:T(8,128)S(1)} %get-tuple-element.16), channel_id=1, source_target_pairs={{0,1},{1,0},{2,3},{3,2},{4,5},{5,4},{6,7},{7,6},{8,9},{9,8},{10,11... | collective-permute-start | bytes 196616 | tf_op jit(solution)/shard_map/ppermute | solution.py:142
  22.0 1.9 %collective-permute-start.3 = (f32[128,128]{1,0:T(8,128)S(1)}, f32[128,128]{1,0:T(8,128)S(1)}, u32[]{:S(2)}, u32[]{:S(2)}) collective-permute-start(f32[128,128]{1,0:T(8,128)S(1)} %get-tuple-element.18), channel_id=1, source_target_pairs={{1,2},{2,1},{3,4},{4,3},{5,6},{6,5},{7,8},{8,7},{9,10},{10,9},{11,... | collective-permute-start | bytes 196616 | tf_op jit(solution)/shard_map/ppermute | solution.py:143
  23.9 0.0 collective-permute-done.2.fa_ref
  23.9 4.3 %collective-permute-done.3.fb_ref = f32[128,128]{1,0:T(8,128)S(1)} collective-permute-done((f32[128,128]{1,0:T(8,128)S(1)}, f32[128,128]{1,0:T(8,128)S(1)}, u32[]{:S(2)}, u32[]{:S(2)}) %collective-permute-start.3) | collective-permute-done | bytes 65568 | tf_op jit(solution)/shard_map/ppermute | solution.py:143
  28.3 0.0 copy-done.5
  28.3 0.0 copy-done.4
  28.3 0.0 copy-done.1
  28.3 0.0 copy-done.6
  28.3 0.9 %base.1 = (f32[256,128]{1,0:T(8,128)S(1)}, bf16[256,512]{1,0:T(8,128)(2,1)S(1)}, bf16[256,512]{1,0:T(8,128)(2,1)S(1)}) custom-call(s32[3]{0:T(128)S(1)} %bitcast.16, s32[1]{0:T(128)} %bitcast.2.odd_ref, f32[256,128]{1,0:T(8,128)S(1)} %copy-done.6, f32[256,256]{1,0:T(8,128)S(1)} %copy-done.5, f32[256,128]{1,0:T(8,128)S(1)} %copy-done.1, ...), custom_call_target="tpu_custom_call" | custom-call | tf_op jit(solution)/shard_map/base/pallas_call | solution.py:144
  29.2 0.0 all-to-all-done
  29.2 0.0 copy-start.8
  29.2 0.7 %copy-done.8 = f32[256]{0:T(256)S(1)} copy-done((f32[256]{0:T(256)S(1)}, f32[256]{0:T(256)}, u32[]{:S(2)}) %copy-start.8) | copy-done | bytes 1048
  29.9 1.0 %final.1 = (f32[256,128]{1,0:T(8,128)}, f32[256,128]{1,0:T(8,128)}) custom-call(f32[512,128]{1,0:T(8,128)S(1)} %bitcast.10, bf16[256,512]{1,0:T(8,128)(2,1)S(1)} %get-tuple-element.19.hi_ref, bf16[256,512]{1,0:T(8,128)(2,1)S(1)} %get-tuple-element.20.lo_ref, f32[256,128]{1,0:T(8,128)S(1)} %get-tuple-element.21.base_ref, f32[256,128]{1,0:T(8,128)S(1)} %copy-done.1, ...), custom_call_target="tpu_custom_call" | custom-call | tf_op jit(solution)/shard_map/final/pallas_call | solution.py:150
  (1 shorter events, 0.0 us)
Async XLA Ops:
  0.6 0.7 %copy-start.10 = (s32[1,3,128]{2,0,1:T(1,128)S(1)}, s32[1,3,128]{2,0,1:T(1,128)}, u32[]{:S(2)}) copy-start(s32[1,3,128]{2,0,1:T(1,128)} %param.17) | copy-start | bytes 4612
  1.3 0.7 %copy-start.7 = (s32[1,3]{1,0:T(1,128)S(1)}, s32[1,3]{1,0:T(1,128)}, u32[]{:S(2)}) copy-start(s32[1,3]{1,0:T(1,128)} %param.18) | copy-start | bytes 40
  1.3 0.7 %copy-start.9 = (s32[16,1]{0,1:T(1,128)S(1)}, s32[16,1]{0,1:T(1,128)}, u32[]{:S(2)}) copy-start(s32[16,1]{0,1:T(1,128)} %param.16) | copy-start | bytes 196
  2.0 0.9 %copy-start = (f32[256,128]{1,0:T(8,128)S(1)}, f32[256,128]{1,0:T(8,128)}, u32[]{:S(2)}) copy-start(f32[256,128]{1,0:T(8,128)} %x_ref.5) | copy-start | bytes 393220
  2.9 1.0 %copy-start.3 = (f32[16,32,256]{2,1,0:T(8,128)S(1)}, f32[16,32,256]{2,1,0:T(8,128)}, u32[]{:S(2)}) copy-start(f32[16,32,256]{2,1,0:T(8,128)} %v_ref.1) | copy-start | bytes 1572868
  3.9 14.9 %copy-start.2 = (f32[1,384,384]{2,1,0:T(8,128)S(1)}, f32[1,384,384]{2,1,0:T(8,128)}, u32[]{:S(2)}) copy-start(f32[1,384,384]{2,1,0:T(8,128)} %param.12) | copy-start | bytes 1769476
  5.6 22.7 %copy-start.5 = (f32[256,256]{1,0:T(8,128)S(1)}, f32[256,256]{1,0:T(8,128)}, u32[]{:S(2)}) copy-start(f32[256,256]{1,0:T(8,128)} %near_ref.1) | copy-start | bytes 786436
  5.6 23.6 %all-to-all-start = ((f32[16,32,128]{2,1,0:T(8,128)}), f32[16,32,128]{2,1,0:T(8,128)S(1)}, u32[]{:S(2)}, u32[]{:S(2)}) async-start(f32[16,32,128]{2,1,0:T(8,128)} %get-tuple-element.12), calls=%async_computation | async-start | bytes 524288 | tf_op jit(solution)/shard_map/all_to_all | solution.py:136
  12.2 16.0 %copy-start.4 = (f32[16,32,256]{2,1,0:T(8,128)S(1)}, f32[16,32,256]{2,1,0:T(8,128)}, u32[]{:S(2)}) copy-start(f32[16,32,256]{2,1,0:T(8,128)} %param.14) | copy-start | bytes 1572868
  12.2 3.6 %collective-permute-start = (f32[128,128]{1,0:T(8,128)S(1)}, f32[128,128]{1,0:T(8,128)S(1)}, u32[]{:S(2)}, u32[]{:S(2)}) collective-permute-start(f32[128,128]{1,0:T(8,128)S(1)} %get-tuple-element.13), channel_id=1, source_target_pairs={{0,1},{1,0},{2,3},{3,2},{4,5},{5,4},{6,7},{7,6},{8,9},{9,8},{10,11... | collective-permute-start | bytes 196616 | tf_op jit(solution)/shard_map/ppermute | solution.py:137
  12.7 6.1 %collective-permute-start.1 = (f32[128,128]{1,0:T(8,128)S(1)}, f32[128,128]{1,0:T(8,128)S(1)}, u32[]{:S(2)}, u32[]{:S(2)}) collective-permute-start(f32[128,128]{1,0:T(8,128)S(1)} %get-tuple-element.15), channel_id=1, source_target_pairs={{1,2},{2,1},{3,4},{4,3},{5,6},{6,5},{7,8},{8,7},{9,10},{10,9},{11,... | collective-permute-start | bytes 196616 | tf_op jit(solution)/shard_map/ppermute | solution.py:138
  18.8 9.5 %copy-start.1 = (f32[256,128]{1,0:T(8,128)S(1)}, f32[256,128]{1,0:T(8,128)}, u32[]{:S(2)}) copy-start(f32[256,128]{1,0:T(8,128)} %x_ref.5) | copy-start | bytes 393220
  18.8 9.5 %copy-start.6 = (f32[256,128]{1,0:T(8,128)S(1)}, f32[256,128]{1,0:T(8,128)}, u32[]{:S(2)}) copy-start(f32[256,128]{1,0:T(8,128)} %rhs_ref.1) | copy-start | bytes 393220
  19.1 4.8 %collective-permute-start.2 = (f32[128,128]{1,0:T(8,128)S(1)}, f32[128,128]{1,0:T(8,128)S(1)}, u32[]{:S(2)}, u32[]{:S(2)}) collective-permute-start(f32[128,128]{1,0:T(8,128)S(1)} %get-tuple-element.16), channel_id=1, source_target_pairs={{0,1},{1,0},{2,3},{3,2},{4,5},{5,4},{6,7},{7,6},{8,9},{9,8},{10,11... | collective-permute-start | bytes 196616 | tf_op jit(solution)/shard_map/ppermute | solution.py:142
  22.0 6.3 %collective-permute-start.3 = (f32[128,128]{1,0:T(8,128)S(1)}, f32[128,128]{1,0:T(8,128)S(1)}, u32[]{:S(2)}, u32[]{:S(2)}) collective-permute-start(f32[128,128]{1,0:T(8,128)S(1)} %get-tuple-element.18), channel_id=1, source_target_pairs={{1,2},{2,1},{3,4},{4,3},{5,6},{6,5},{7,8},{8,7},{9,10},{10,9},{11,... | collective-permute-start | bytes 196616 | tf_op jit(solution)/shard_map/ppermute | solution.py:143
  29.2 0.7 %copy-start.8 = (f32[256]{0:T(256)S(1)}, f32[256]{0:T(256)}, u32[]{:S(2)}) copy-start(f32[256]{0:T(256)} %param.19) | copy-start | bytes 3076

commit v2 on v1

v2 whole, which is shorter than its diff:
```python
import jax
import jax.numpy as jnp
from jax import lax
from jax.experimental import pallas as pl
from jax.experimental.pallas import tpu as pltpu
from jax.sharding import PartitionSpec as P

VMEM = pl.BlockSpec(memory_space=pltpu.VMEM)
HBM = pl.BlockSpec(memory_space=pltpu.HBM)
f32 = jnp.float32
bf16 = jnp.bfloat16


def halves(a):
    hi = a.astype(bf16)
    return hi, (a - hi.astype(f32)).astype(bf16)


def dot(a, b):
    return jnp.dot(a, b, preferred_element_type=f32)


def wide_halves(a):
    return jnp.concatenate(halves(a), axis=1)


def fold(both):
    n = both.shape[1] // 2
    return both[:, :n] + both[:, n:]


def split_product(hi, lo, b_wide):
    n = b_wide.shape[1] // 2
    both = dot(hi, b_wide)
    return both[:, :n] + (both[:, n:] + dot(lo, b_wide[:, :n]))


def product(a, b_wide):
    return split_product(*halves(a), b_wide)


def is_odd():
    return lax.axis_index("wide") % 2 == 1


def send_kernel(x_hbm, v_hbm, rows_hbm, count_hbm, rank_hbm, schur_hbm, u_hbm, near_hbm, rhs_hbm, p_hbm,
                coeff_hbm, a_ref, m_ref, b_ref, sel_ref, x_ref, schur_ref, u_ref, near_ref, rhs_ref, p_ref,
                v_ref, rows_ref, count_ref, rank_ref, coeff_ref, sems, out_sems):
    n_rows, loads = x_ref.shape
    face = rows_ref.shape[2]
    tiles, top, _ = v_ref.shape
    pairs = (
        (x_hbm, x_ref), (rank_hbm, rank_ref), (v_hbm, v_ref), (rows_hbm, rows_ref), (count_hbm, count_ref),
        (schur_hbm, schur_ref), (u_hbm, u_ref), (near_hbm, near_ref), (rhs_hbm, rhs_ref), (p_hbm, p_ref),
    )
    moves = [pltpu.make_async_copy(src, dst, sems.at[i]) for i, (src, dst) in enumerate(pairs)]
    for move in moves:
        move.start()
    moves[0].wait()
    x_wide = wide_halves(x_ref[...])
    for move in moves[1:3]:
        move.wait()
    step = max(1, min(tiles, 256 // top))
    k = lax.broadcasted_iota(jnp.int32, (top, loads), 0)

    def out_move(s):
        span = pl.ds(s * step, step)
        return pltpu.make_async_copy(coeff_ref.at[span], coeff_hbm.at[span], out_sems.at[s])

    for s in range(tiles // step):
        part = v_ref[s * step : (s + 1) * step].reshape(step * top, n_rows)
        out = product(part, x_wide).reshape(step, top, loads)
        for t in range(step):
            coeff_ref[s * step + t] = jnp.where(k < rank_ref[s * step + t], out[t], 0.0)
        out_move(s).start()
    for move in moves[3:5]:
        move.wait()
    odd = is_odd()
    slots = (jnp.where(odd, 0, 2), 1, jnp.where(odd, 2, 0))
    lane = lax.broadcasted_iota(jnp.int32, (1, face), 1)
    across = lax.broadcasted_iota(jnp.int32, (face, n_rows), 1).astype(f32)
    down = lax.broadcasted_iota(jnp.int32, (n_rows, face), 0)
    for spot, out_ref in enumerate((a_ref, m_ref, b_ref)):
        rows = jnp.where(lane < count_ref[slots[spot]], rows_ref[slots[spot]], -1)
        sel_ref[:, spot * face : (spot + 1) * face] = (down == rows).astype(f32).astype(bf16)
        column = jnp.broadcast_to(rows.astype(f32), (face, face)).T[:, :1]
        select = (across == column).astype(f32).astype(bf16)
        out_ref[...] = fold(dot(select, x_wide))
    for s in range(tiles // step):
        out_move(s).wait()
    for move in moves[5:]:
        move.wait()


def place(odd, spot, face):
    if spot == 1:
        return face
    return pl.multiple_of(jnp.where(odd == (spot == 0), 2 * face, 0), face)


def across_kernel(a_ref, m_ref, b_ref, schur_ref, pay_ref, part_ref):
    odd = is_odd()
    face = a_ref.shape[0]
    known = jnp.concatenate([wide_halves(a_ref[...]), wide_halves(m_ref[...])], axis=0)
    pay_ref[:face] = b_ref[...]
    for spot in (2, 0, 1):
        rows = pl.ds(place(odd, spot, face), face)
        block = jnp.concatenate(
            [schur_ref[rows, pl.ds(place(odd, 0, face), face)], schur_ref[rows, face : 2 * face]], axis=1
        )
        out = product(block, known)
        if spot == 2:
            pay_ref[face : 2 * face] = out
            pay_ref[2 * face :] = schur_ref[rows, pl.ds(place(odd, 2, face), face)]
        else:
            part_ref[spot * face : (spot + 1) * face] = out


def base_kernel(rhs_ref, near_ref, x_ref, sel_ref, part_ref, u_ref, p_ref, base_ref, hi_ref, lo_ref, scale_ref):
    n_rows, loads = x_ref.shape
    face = part_ref.shape[0] // 2
    total = rhs_ref[...] - product(near_ref[...], wide_halves(x_ref[...]))
    base_ref[...] = total - fold(dot(sel_ref[:, face : 2 * face], wide_halves(part_ref[face:])))
    hi_ref[...], lo_ref[...] = halves(u_ref[...].T)
    scale_ref[...] = jnp.broadcast_to(p_ref[...], (loads, n_rows)).T


def force_kernel(got_ref, part_ref, schur_ref, _, fa_ref):
    odd = is_odd()
    face = fa_ref.shape[0]
    block = schur_ref[pl.ds(place(odd, 0, face), face), pl.ds(place(odd, 2, face), face)]
    fa_ref[...] = part_ref[:face] + product(block, wide_halves(got_ref[:face]))


def own_kernel(got_ref, out_b_ref, schur_ref, sel_ref, base_ref, next_ref):
    odd = is_odd()
    face = out_b_ref.shape[0]
    block = schur_ref[face : 2 * face, pl.ds(place(odd, 2, face), face)]
    own = product(block, wide_halves(got_ref[:face]))
    back = got_ref[face : 2 * face] + product(got_ref[2 * face :], wide_halves(out_b_ref[...]))
    both = jnp.concatenate([wide_halves(own), wide_halves(back)], axis=0)
    next_ref[...] = base_ref[...] - fold(dot(sel_ref[:, face:], both))


def pair_kernel(back_ref, sel_ref, base_ref, next_ref):
    face = back_ref.shape[0]
    next_ref[...] = base_ref[...] - fold(dot(sel_ref[:, :face], wide_halves(back_ref[...])))


def final_kernel(coeff_ref, hi_ref, lo_ref, base_ref, x_ref, scale_ref, up_ref, res_ref):
    res = base_ref[...] - split_product(hi_ref[...], lo_ref[...], wide_halves(coeff_ref[...]))
    res_ref[...] = res
    up_ref[...] = x_ref[...] + scale_ref[...] * res


def call(kernel, name, outs, operands, in_specs=None, out_specs=None, scratch=(), spaces=None):
    return pl.pallas_call(
        kernel,
        out_shape=tuple(
            space(s, t) for space, (s, t) in zip(spaces or [pltpu.VMEM] * len(outs), outs)
        ),
        in_specs=in_specs or [VMEM] * len(operands),
        out_specs=tuple(out_specs or [VMEM] * len(outs)),
        scratch_shapes=list(scratch),
        compiler_params=pltpu.CompilerParams(vmem_limit_bytes=40 * 2**20),
        name=name,
    )(*operands)


def body(iterate, rhs, schur, near_block, u_basis, v_basis, tile_rank, send_rows, send_count, precond):
    n_rows, loads = iterate.shape
    face = send_rows.shape[2]
    tiles, top, _ = u_basis.shape
    size = lax.axis_size("wide")
    inside = [(i, i ^ 1) for i in range(size) if i ^ 1 < size]
    across = [(i, j) for i in range(size) for j in [i - 1 if i % 2 == 0 else i + 1] if 0 <= j < size]
    schur = schur.reshape(3 * face, 3 * face)
    block = ((face, loads), f32)
    field = ((n_rows, loads), f32)
    factor = ((n_rows, tiles * top), bf16)
    steps = tiles // max(1, min(tiles, 256 // top))

    arrays = (
        iterate,
        v_basis,
        send_rows.reshape(3, 1, face),
        send_count.reshape(3),
        tile_rank.reshape(tiles),
        schur,
        u_basis.reshape(tiles * top, n_rows),
        near_block,
        rhs,
        precond.reshape(1, n_rows),
    )
    square = lambda a: (a.shape, a.dtype)
    coeff, out_a, out_m, out_b, sel, x, schur, u, near, rhs, p = call(
        send_kernel,
        "send",
        [((tiles, top, loads), f32), block, block, block, ((n_rows, 3 * face), bf16), field]
        + [square(arrays[i]) for i in (5, 6, 7, 8, 9)],
        [pltpu.with_memory_space_constraint(a, pltpu.HBM) for a in arrays],
        [HBM] * len(arrays),
        [HBM] + [VMEM] * 10,
        [
            pltpu.VMEM((tiles, top, n_rows), f32),
            pltpu.VMEM((3, 1, face), jnp.int32),
            pltpu.SMEM((3,), jnp.int32),
            pltpu.SMEM((tiles,), jnp.int32),
            pltpu.VMEM((tiles, top, loads), f32),
            pltpu.SemaphoreType.DMA((len(arrays),)),
            pltpu.SemaphoreType.DMA((steps,)),
        ],
        [pltpu.HBM] + [pltpu.VMEM] * 10,
    )
    gathered = lax.all_to_all(coeff, "wide", split_axis=0, concat_axis=0, tiled=True)
    in_a = lax.ppermute(out_a, "wide", inside)
    pay, part = call(
        across_kernel, "across", [((3 * face, loads), f32), ((2 * face, loads), f32)], (in_a, out_m, out_b, schur)
    )
    got = lax.ppermute(pay, "wide", across)
    base, u_hi, u_lo, scale = call(
        base_kernel,
        "base",
        [field, factor, factor, field],
        (rhs, near, x, sel, part, u, p),
    )
    (f_a,) = call(force_kernel, "force", [block], (got, part, schur, base))
    back = lax.ppermute(f_a, "wide", inside)
    (base,) = call(own_kernel, "own", [field], (got, out_b, schur, sel, base))
    (base,) = call(pair_kernel, "pair", [field], (back, sel, base))
    return call(
        final_kernel,
        "final",
        [field, field],
        (gathered.reshape(tiles * top, loads), u_hi, u_lo, base, x, scale),
        spaces=[jax.ShapeDtypeStruct] * 2,
    )


def solution(mesh):
    rows = P(("groups", "wide"), None)
    block = P(("groups", "wide"), None, None)
    basis = P("groups", None, "wide")
    in_specs = (rows, rows, block, rows, basis, basis, P("groups", "wide"), block, rows, P(("groups", "wide")))
    return jax.shard_map(body, mesh=mesh, in_specs=in_specs, out_specs=(rows, rows), check_vma=False)
```

time: 31.2 us -> 23.8 us (0.76)
  starting transfers between devices: 14.9 us -> 10.3 us
  local copies, waits for them, and re-layouts: 3.98 us -> 0 us
  waiting for transfers between devices: 7.35 us -> 7.95 us
  Pallas kernels: 3.91 us -> 4.44 us
    ppermute x3 -> x2, starting transfers between devices: 7.86 us -> 3.41 us  [the longest x1 3.34 us: body(): got = lax.ppermute(pay, 'wide', across)]
    unnamed x23 -> x0, local copies, waits for them, and re-layouts: 3.98 us -> none
    ppermute x1, waiting for transfers between devices: 0.01 us -> 0.9 us  [body(): in_a = lax.ppermute(out_a, 'wide', inside)]
    pallas_call x4 -> x7, Pallas kernels: 3.91 us -> 4.44 us  [call(): pl.pallas_call(kernel, out_shape=tuple((space(s, t) for space, (s, t) in...]
    ppermute x3 -> x2, waiting for transfers between devices: 7.35 us -> 7.05 us  [the longest x1 6.19 us: body(): got = lax.ppermute(pay, 'wide', across)]
  transfers between devices with their start and end apart: 5 -> 4, of which waited for: 2 -> 3; matrix products, arithmetic and copies ran while one was open for 0% -> 0% of each run, Pallas kernels for 4% -> 5%
where the time goes in v2:
time: 23.8 us; the launch traced here: 23.4 us
  starting transfers between devices  10.3 us (43%)
  waiting for transfers between devices  7.95 us (33%)
  Pallas kernels  4.44 us (19%)
  between operations  0.7 us (3%)
    all_to_all x1, starting transfers between devices, body(): lax.all_to_all(coeff, 'wide', split_axis=0, concat_axis=0, tiled=True)  6.51 us
    ppermute x1, waiting for transfers between devices, body(): got = lax.ppermute(pay, 'wide', across)  6.19 us
    pallas_call x7, Pallas kernels, call(): pl.pallas_call(kernel, out_shape=tuple((space(s, t) for space, (s, t) in...  4.44 us
    ppermute x1, starting transfers between devices, body(): got = lax.ppermute(pay, 'wide', across)  3.34 us
    ppermute x1, waiting for transfers between devices, body(): in_a = lax.ppermute(out_a, 'wide', inside)  0.9 us
    ppermute x1, waiting for transfers between devices, body(): back = lax.ppermute(f_a, 'wide', inside)  0.86 us
  transfers between devices with their start and end apart: 4, of which 3 were waited for; matrix products, arithmetic and copies ran while one was open for 0% of the time, Pallas kernels for 5%

profile of v2, /device:TPU:19, one launch (start us, length us, event | category | flops | bytes accessed | tf_op | source)
XLA Modules:
  0.0 23.4 jit_solution(1812567738796248167)
XLA Ops:
  0.6 2.2 %send.1 = (f32[16,32,128]{2,1,0:T(8,128)}, f32[128,128]{1,0:T(8,128)S(1)}, f32[128,128]{1,0:T(8,128)S(1)}, f32[128,128]{1,0:T(8,128)S(1)}, bf16[256,384]{1,0:T(8...) custom-call(f32[256,128]{1,0:T(8,128)} %x_hbm.1, ...), custom_call_target="tpu_custom_call" | custom-call | tf_op jit(solution)/shard_map/send/pallas_call | solution.py:157
  2.8 6.5 %all-to-all-start = ((f32[16,32,128]{2,1,0:T(8,128)}), f32[16,32,128]{2,1,0:T(8,128)S(1)}, u32[]{:S(2)}, u32[]{:S(2)}) async-start(f32[16,32,128]{2,1,0:T(8,128)} %get-tuple-element.19), calls=%async_computation | async-start | bytes 524288 | tf_op jit(solution)/shard_map/all_to_all | solution.py:215
  9.3 0.4 %collective-permute-start = (f32[128,128]{1,0:T(8,128)S(1)}, f32[128,128]{1,0:T(8,128)S(1)}, u32[]{:S(2)}, u32[]{:S(2)}) collective-permute-start(f32[128,128]{1,0:T(8,128)S(1)} %get-tuple-element.24), channel_id=1, source_target_pairs={{0,1},{1,0},{2,3},{3,2},{4,5},{5,4},{6,7},{7,6},{8,9},{9,8},{10,11... | collective-permute-start | bytes 196616 | tf_op jit(solution)/shard_map/ppermute | solution.py:216
  9.7 0.9 %collective-permute-done.a_ref = f32[128,128]{1,0:T(8,128)S(1)} collective-permute-done((f32[128,128]{1,0:T(8,128)S(1)}, f32[128,128]{1,0:T(8,128)S(1)}, u32[]{:S(2)}, u32[]{:S(2)}) %collective-permute-start) | collective-permute-done | bytes 65568 | tf_op jit(solution)/shard_map/ppermute | solution.py:216
  10.6 0.3 %across.1 = (f32[384,128]{1,0:T(8,128)S(1)}, f32[256,128]{1,0:T(8,128)S(1)}) custom-call(f32[128,128]{1,0:T(8,128)S(1)} %collective-permute-done.a_ref, f32[128,128]{1,0:T(8,128)S(1)} %get-tuple-element.25.m_ref, f32[128,128]{1,0:T(8,128)S(1)} %get-tuple-element.26.b_ref.out_b_ref, f32[384,384]{1,0:T(8,128)S(1)} %get-tuple-element.27.schur_ref), custom_call_target="tpu_custom_call" | custom-call | tf_op jit(solution)/shard_map/across/pallas_call | solution.py:157
  10.9 3.3 %collective-permute-start.1 = (f32[384,128]{1,0:T(8,128)S(1)}, f32[384,128]{1,0:T(8,128)S(1)}, u32[]{:S(2)}, u32[]{:S(2)}) collective-permute-start(f32[384,128]{1,0:T(8,128)S(1)} %get-tuple-element.33), channel_id=1, source_target_pairs={{1,2},{2,1},{3,4},{4,3},{5,6},{6,5},{7,8},{8,7},{9,10},{10,9},{11,... | collective-permute-start | bytes 589832 | tf_op jit(solution)/shard_map/ppermute | solution.py:220
  14.2 0.3 %base.1 = (f32[256,128]{1,0:T(8,128)S(1)}, bf16[256,512]{1,0:T(8,128)(2,1)S(1)}, bf16[256,512]{1,0:T(8,128)(2,1)S(1)}, f32[256,128]{1,0:T(8,128)S(1)}) custom-call(f32[256,128]{1,0:T(8,128)S(1)} %get-tuple-element.20.rhs_ref, f32[256,256]{1,0:T(8,128)S(1)} %get-tuple-element.21.near_ref, f32[256,128]{1,0:T(8,128)S(1)} %get-tuple-element.22.x_ref, ...), custom_call_target="tpu_custom_call" | custom-call | tf_op jit(solution)/shard_map/base/pallas_call | solution.py:157
  14.5 6.2 %collective-permute-done.1.got_ref = f32[384,128]{1,0:T(8,128)S(1)} collective-permute-done((f32[384,128]{1,0:T(8,128)S(1)}, f32[384,128]{1,0:T(8,128)S(1)}, u32[]{:S(2)}, u32[]{:S(2)}) %collective-permute-start.1) | collective-permute-done | bytes 196640 | tf_op jit(solution)/shard_map/ppermute | solution.py:220
  20.7 0.2 force.1
  20.9 0.1 collective-permute-start.2
  20.9 0.4 %own.1.base_ref = f32[256,128]{1,0:T(8,128)S(1)} custom-call(f32[384,128]{1,0:T(8,128)S(1)} %collective-permute-done.1.got_ref, f32[128,128]{1,0:T(8,128)S(1)} %get-tuple-element.26.b_ref.out_b_ref, f32[384,384]{1,0:T(8,128)S(1)} %get-tuple-element.27.schur_ref, bf16[256,384]{1,0:T(8,128)(2,1)S(1)} %get-tuple-element.23.sel_ref, ...), custom_call_target="tpu_custom_call" | custom-call | tf_op jit(solution)/shard_map/own/pallas_call | solution.py:157
  21.3 0.9 %collective-permute-done.2.back_ref = f32[128,128]{1,0:T(8,128)S(1)} collective-permute-done((f32[128,128]{1,0:T(8,128)S(1)}, f32[128,128]{1,0:T(8,128)S(1)}, u32[]{:S(2)}, u32[]{:S(2)}) %collective-permute-start.2) | collective-permute-done | bytes 65568 | tf_op jit(solution)/shard_map/ppermute | solution.py:228
  22.2 0.2 pair.1.base_ref
  22.4 0.0 all-to-all-done
  22.4 1.0 %final.1 = (f32[256,128]{1,0:T(8,128)}, f32[256,128]{1,0:T(8,128)}) custom-call(f32[512,128]{1,0:T(8,128)S(1)} %bitcast.7, bf16[256,512]{1,0:T(8,128)(2,1)S(1)} %get-tuple-element.31.hi_ref, bf16[256,512]{1,0:T(8,128)(2,1)S(1)} %get-tuple-element.32.lo_ref, f32[256,128]{1,0:T(8,128)S(1)} %pair.1.base_ref, f32[256,128]{1,0:T(8,128)S(1)} %get-tuple-element.22.x_ref, ...), custom_call_target="tpu_custom_call" | custom-call | tf_op jit(solution)/shard_map/final/pallas_call | solution.py:157
Async XLA Ops:
  2.8 19.5 %all-to-all-start = ((f32[16,32,128]{2,1,0:T(8,128)}), f32[16,32,128]{2,1,0:T(8,128)S(1)}, u32[]{:S(2)}, u32[]{:S(2)}) async-start(f32[16,32,128]{2,1,0:T(8,128)} %get-tuple-element.19), calls=%async_computation | async-start | bytes 524288 | tf_op jit(solution)/shard_map/all_to_all | solution.py:215
  9.3 1.3 %collective-permute-start = (f32[128,128]{1,0:T(8,128)S(1)}, f32[128,128]{1,0:T(8,128)S(1)}, u32[]{:S(2)}, u32[]{:S(2)}) collective-permute-start(f32[128,128]{1,0:T(8,128)S(1)} %get-tuple-element.24), channel_id=1, source_target_pairs={{0,1},{1,0},{2,3},{3,2},{4,5},{5,4},{6,7},{7,6},{8,9},{9,8},{10,11... | collective-permute-start | bytes 196616 | tf_op jit(solution)/shard_map/ppermute | solution.py:216
  10.9 9.8 %collective-permute-start.1 = (f32[384,128]{1,0:T(8,128)S(1)}, f32[384,128]{1,0:T(8,128)S(1)}, u32[]{:S(2)}, u32[]{:S(2)}) collective-permute-start(f32[384,128]{1,0:T(8,128)S(1)} %get-tuple-element.33), channel_id=1, source_target_pairs={{1,2},{2,1},{3,4},{4,3},{5,6},{6,5},{7,8},{8,7},{9,10},{10,9},{11,... | collective-permute-start | bytes 589832 | tf_op jit(solution)/shard_map/ppermute | solution.py:220
  20.9 1.3 %collective-permute-start.2 = (f32[128,128]{1,0:T(8,128)S(1)}, f32[128,128]{1,0:T(8,128)S(1)}, u32[]{:S(2)}, u32[]{:S(2)}) collective-permute-start(f32[128,128]{1,0:T(8,128)S(1)} %force.1), channel_id=1, source_target_pairs={{0,1},{1,0},{2,3},{3,2},{4,5},{5,4},{6,7},{7,6},{8,9},{9,8},{10,11... | collective-permute-start | bytes 196616 | tf_op jit(solution)/shard_map/ppermute | solution.py:228

commit v3 on v2

--- a/solution.py
+++ b/solution.py
@@ -142,18 +142,18 @@
     next_ref[...] = base_ref[...] - fold(dot(sel_ref[:, face:], both))
 
 
-def pair_kernel(back_ref, sel_ref, base_ref, next_ref):
+def far_kernel(coeff_ref, hi_ref, lo_ref, base_ref, next_ref):
+    next_ref[...] = base_ref[...] - split_product(hi_ref[...], lo_ref[...], wide_halves(coeff_ref[...]))
+
+
+def final_kernel(back_ref, sel_ref, base_ref, x_ref, scale_ref, up_ref, res_ref):
     face = back_ref.shape[0]
-    next_ref[...] = base_ref[...] - fold(dot(sel_ref[:, :face], wide_halves(back_ref[...])))
-
-
-def final_kernel(coeff_ref, hi_ref, lo_ref, base_ref, x_ref, scale_ref, up_ref, res_ref):
-    res = base_ref[...] - split_product(hi_ref[...], lo_ref[...], wide_halves(coeff_ref[...]))
+    res = base_ref[...] - fold(dot(sel_ref[:, :face], wide_halves(back_ref[...])))
     res_ref[...] = res
     up_ref[...] = x_ref[...] + scale_ref[...] * res
 
 
-def call(kernel, name, outs, operands, in_specs=None, out_specs=None, scratch=(), spaces=None):
+def call(kernel, name, outs, operands, in_specs=None, out_specs=None, scratch=(), spaces=None, cost=0):
     return pl.pallas_call(
         kernel,
         out_shape=tuple(
@@ -163,6 +163,7 @@
         out_specs=tuple(out_specs or [VMEM] * len(outs)),
         scratch_shapes=list(scratch),
         compiler_params=pltpu.CompilerParams(vmem_limit_bytes=40 * 2**20),
+        cost_estimate=pl.CostEstimate(flops=cost, bytes_accessed=0, transcendentals=0) if cost else None,
         name=name,
     )(*operands)
 
@@ -215,7 +216,7 @@
     gathered = lax.all_to_all(coeff, "wide", split_axis=0, concat_axis=0, tiled=True)
     in_a = lax.ppermute(out_a, "wide", inside)
     pay, part = call(
-        across_kernel, "across", [((3 * face, loads), f32), ((2 * face, loads), f32)], (in_a, out_m, out_b, schur)
+        across_kernel, "across", [((3 * face, loads), f32), ((2 * face, loads), f32)], (in_a, out_m, out_b, schur), cost=10000000000
     )
     got = lax.ppermute(pay, "wide", across)
     base, u_hi, u_lo, scale = call(
@@ -224,16 +225,12 @@
         [field, factor, factor, field],
         (rhs, near, x, sel, part, u, p),
     )
-    (f_a,) = call(force_kernel, "force", [block], (got, part, schur, base))
+    (f_a,) = call(force_kernel, "force", [block], (got, part, schur, base), cost=0)
     back = lax.ppermute(f_a, "wide", inside)
     (base,) = call(own_kernel, "own", [field], (got, out_b, schur, sel, base))
-    (base,) = call(pair_kernel, "pair", [field], (back, sel, base))
+    (base,) = call(far_kernel, "far", [field], (gathered.reshape(tiles * top, loads), u_hi, u_lo, base))
     return call(
-        final_kernel,
-        "final",
-        [field, field],
-        (gathered.reshape(tiles * top, loads), u_hi, u_lo, base, x, scale),
-        spaces=[jax.ShapeDtypeStruct] * 2,
+        final_kernel, "final", [field, field], (back, sel, base, x, scale), spaces=[jax.ShapeDtypeStruct] * 2
     )
 
 

time: 23.8 us -> 23 us (0.966)
  the two profiles are of different devices: /device:TPU:19 before, /device:TPU:9 now
where the time goes in v3:
time: 23 us; the launch traced here: 22.7 us
  starting transfers between devices  10.2 us (44%)
  waiting for transfers between devices  7.34 us (32%)
  Pallas kernels  4.44 us (19%)
  between operations  0.7 us (3%)
    ppermute x1, waiting for transfers between devices, body(): got = lax.ppermute(pay, 'wide', across)  6.79 us
    all_to_all x1, starting transfers between devices, body(): lax.all_to_all(coeff, 'wide', split_axis=0, concat_axis=0, tiled=True)  6.05 us
    pallas_call x7, Pallas kernels, call(): pl.pallas_call(kernel, out_shape=tuple((space(s, t) for space, (s, t) in...  4.44 us
    ppermute x1, starting transfers between devices, body(): got = lax.ppermute(pay, 'wide', across)  3.34 us
    ppermute x1, starting transfers between devices, body(): in_a = lax.ppermute(out_a, 'wide', inside)  0.74 us
    ppermute x1, waiting for transfers between devices, body(): back = lax.ppermute(f_a, 'wide', inside)  0.54 us
  transfers between devices with their start and end apart: 4, of which 2 were waited for; matrix products, arithmetic and copies ran while one was open for 0% of the time, Pallas kernels for 6%

profile of v3, /device:TPU:9, one launch (start us, length us, event | category | flops | bytes accessed | tf_op | source)
XLA Modules:
  0.0 22.7 jit_solution(11398754367861385570)
XLA Ops:
  0.6 2.2 %send.1 = (f32[16,32,128]{2,1,0:T(8,128)}, f32[128,128]{1,0:T(8,128)S(1)}, f32[128,128]{1,0:T(8,128)S(1)}, f32[128,128]{1,0:T(8,128)S(1)}, bf16[256,384]{1,0:T(8...) custom-call(f32[256,128]{1,0:T(8,128)} %x_hbm.1, ...), custom_call_target="tpu_custom_call" | custom-call | tf_op jit(solution)/shard_map/send/pallas_call | solution.py:157
  2.8 0.7 %collective-permute-start = (f32[128,128]{1,0:T(8,128)S(1)}, f32[128,128]{1,0:T(8,128)S(1)}, u32[]{:S(2)}, u32[]{:S(2)}) collective-permute-start(f32[128,128]{1,0:T(8,128)S(1)} %get-tuple-element.19), channel_id=1, source_target_pairs={{0,1},{1,0},{2,3},{3,2},{4,5},{5,4},{6,7},{7,6},{8,9},{9,8},{10,11... | collective-permute-start | bytes 196616 | tf_op jit(solution)/shard_map/ppermute | solution.py:217
  3.6 6.0 %all-to-all-start = ((f32[16,32,128]{2,1,0:T(8,128)}), f32[16,32,128]{2,1,0:T(8,128)S(1)}, u32[]{:S(2)}, u32[]{:S(2)}) async-start(f32[16,32,128]{2,1,0:T(8,128)} %get-tuple-element.32), calls=%async_computation | async-start | bytes 524288 | tf_op jit(solution)/shard_map/all_to_all | solution.py:216
  9.6 0.0 collective-permute-done.a_ref
  9.6 0.3 %across.1 = (f32[384,128]{1,0:T(8,128)S(1)}, f32[256,128]{1,0:T(8,128)S(1)}) custom-call(f32[128,128]{1,0:T(8,128)S(1)} %collective-permute-done.a_ref, f32[128,128]{1,0:T(8,128)S(1)} %get-tuple-element.20.m_ref, f32[128,128]{1,0:T(8,128)S(1)} %get-tuple-element.21.b_ref.out_b_ref, f32[384,384]{1,0:T(8,128)S(1)} %get-tuple-element.22.schur_ref), custom_call_target="tpu_custom_call" | custom-call | flops 10000000000 | tf_op jit(solution)/shard_map/across/pallas_call | solution.py:157
  9.9 3.3 %collective-permute-start.1 = (f32[384,128]{1,0:T(8,128)S(1)}, f32[384,128]{1,0:T(8,128)S(1)}, u32[]{:S(2)}, u32[]{:S(2)}) collective-permute-start(f32[384,128]{1,0:T(8,128)S(1)} %get-tuple-element.23), channel_id=1, source_target_pairs={{1,2},{2,1},{3,4},{4,3},{5,6},{6,5},{7,8},{8,7},{9,10},{10,9},{11,... | collective-permute-start | bytes 589832 | tf_op jit(solution)/shard_map/ppermute | solution.py:221
  13.2 0.3 %base.1 = (f32[256,128]{1,0:T(8,128)S(1)}, bf16[256,512]{1,0:T(8,128)(2,1)S(1)}, bf16[256,512]{1,0:T(8,128)(2,1)S(1)}, f32[256,128]{1,0:T(8,128)S(1)}) custom-call(f32[256,128]{1,0:T(8,128)S(1)} %get-tuple-element.25.rhs_ref, f32[256,256]{1,0:T(8,128)S(1)} %get-tuple-element.26.near_ref, f32[256,128]{1,0:T(8,128)S(1)} %get-tuple-element.27.x_ref, ...), custom_call_target="tpu_custom_call" | custom-call | tf_op jit(solution)/shard_map/base/pallas_call | solution.py:157
  13.5 6.8 %collective-permute-done.1.got_ref = f32[384,128]{1,0:T(8,128)S(1)} collective-permute-done((f32[384,128]{1,0:T(8,128)S(1)}, f32[384,128]{1,0:T(8,128)S(1)}, u32[]{:S(2)}, u32[]{:S(2)}) %collective-permute-start.1) | collective-permute-done | bytes 196640 | tf_op jit(solution)/shard_map/ppermute | solution.py:221
  20.3 0.2 force.1
  20.5 0.1 collective-permute-start.2
  20.6 0.4 %own.1.base_ref = f32[256,128]{1,0:T(8,128)S(1)} custom-call(f32[384,128]{1,0:T(8,128)S(1)} %collective-permute-done.1.got_ref, f32[128,128]{1,0:T(8,128)S(1)} %get-tuple-element.21.b_ref.out_b_ref, f32[384,384]{1,0:T(8,128)S(1)} %get-tuple-element.22.schur_ref, bf16[256,384]{1,0:T(8,128)(2,1)S(1)} %get-tuple-element.28.sel_ref, ...), custom_call_target="tpu_custom_call" | custom-call | tf_op jit(solution)/shard_map/own/pallas_call | solution.py:157
  20.9 0.0 all-to-all-done
  21.0 0.3 %far.1.base_ref = f32[256,128]{1,0:T(8,128)S(1)} custom-call(f32[512,128]{1,0:T(8,128)S(1)} %bitcast.7, bf16[256,512]{1,0:T(8,128)(2,1)S(1)} %get-tuple-element.33.hi_ref, bf16[256,512]{1,0:T(8,128)(2,1)S(1)} %get-tuple-element.34.lo_ref, f32[256,128]{1,0:T(8,128)S(1)} %own.1.base_ref), custom_call_target="tpu_custom_call" | custom-call | tf_op jit(solution)/shard_map/far/pallas_call | solution.py:157
  21.3 0.5 %collective-permute-done.2.back_ref = f32[128,128]{1,0:T(8,128)S(1)} collective-permute-done((f32[128,128]{1,0:T(8,128)S(1)}, f32[128,128]{1,0:T(8,128)S(1)}, u32[]{:S(2)}, u32[]{:S(2)}) %collective-permute-start.2) | collective-permute-done | bytes 65568 | tf_op jit(solution)/shard_map/ppermute | solution.py:229
  21.8 0.9 %final.1 = (f32[256,128]{1,0:T(8,128)}, f32[256,128]{1,0:T(8,128)}) custom-call(f32[128,128]{1,0:T(8,128)S(1)} %collective-permute-done.2.back_ref, bf16[256,384]{1,0:T(8,128)(2,1)S(1)} %get-tuple-element.28.sel_ref, f32[256,128]{1,0:T(8,128)S(1)} %far.1.base_ref, f32[256,128]{1,0:T(8,128)S(1)} %get-tuple-element.27.x_ref, ...), custom_call_target="tpu_custom_call" | custom-call | tf_op jit(solution)/shard_map/final/pallas_call | solution.py:157
Async XLA Ops:
  2.8 6.8 %collective-permute-start = (f32[128,128]{1,0:T(8,128)S(1)}, f32[128,128]{1,0:T(8,128)S(1)}, u32[]{:S(2)}, u32[]{:S(2)}) collective-permute-start(f32[128,128]{1,0:T(8,128)S(1)} %get-tuple-element.19), channel_id=1, source_target_pairs={{0,1},{1,0},{2,3},{3,2},{4,5},{5,4},{6,7},{7,6},{8,9},{9,8},{10,11... | collective-permute-start | bytes 196616 | tf_op jit(solution)/shard_map/ppermute | solution.py:217
  3.6 17.4 %all-to-all-start = ((f32[16,32,128]{2,1,0:T(8,128)}), f32[16,32,128]{2,1,0:T(8,128)S(1)}, u32[]{:S(2)}, u32[]{:S(2)}) async-start(f32[16,32,128]{2,1,0:T(8,128)} %get-tuple-element.32), calls=%async_computation | async-start | bytes 524288 | tf_op jit(solution)/shard_map/all_to_all | solution.py:216
  9.9 10.4 %collective-permute-start.1 = (f32[384,128]{1,0:T(8,128)S(1)}, f32[384,128]{1,0:T(8,128)S(1)}, u32[]{:S(2)}, u32[]{:S(2)}) collective-permute-start(f32[384,128]{1,0:T(8,128)S(1)} %get-tuple-element.23), channel_id=1, source_target_pairs={{1,2},{2,1},{3,4},{4,3},{5,6},{6,5},{7,8},{8,7},{9,10},{10,9},{11,... | collective-permute-start | bytes 589832 | tf_op jit(solution)/shard_map/ppermute | solution.py:221
  20.5 1.3 %collective-permute-start.2 = (f32[128,128]{1,0:T(8,128)S(1)}, f32[128,128]{1,0:T(8,128)S(1)}, u32[]{:S(2)}, u32[]{:S(2)}) collective-permute-start(f32[128,128]{1,0:T(8,128)S(1)} %force.1), channel_id=1, source_target_pairs={{0,1},{1,0},{2,3},{3,2},{4,5},{5,4},{6,7},{7,6},{8,9},{9,8},{10,11... | collective-permute-start | bytes 196616 | tf_op jit(solution)/shard_map/ppermute | solution.py:229

commit v4 on v3

--- a/solution.py
+++ b/solution.py
@@ -116,30 +116,28 @@
             part_ref[spot * face : (spot + 1) * face] = out
 
 
-def base_kernel(rhs_ref, near_ref, x_ref, sel_ref, part_ref, u_ref, p_ref, base_ref, hi_ref, lo_ref, scale_ref):
+def force_kernel(got_ref, part_ref, schur_ref, fa_ref):
+    odd = is_odd()
+    face = fa_ref.shape[0]
+    got_ref = got_ref.at[odd.astype(jnp.int32)]
+    block = schur_ref[pl.ds(place(odd, 0, face), face), pl.ds(place(odd, 2, face), face)]
+    fa_ref[...] = part_ref[:face] + product(block, wide_halves(got_ref[:face]))
+
+
+def local_kernel(got_ref, part_ref, out_b_ref, schur_ref, sel_ref, rhs_ref, near_ref, x_ref, u_ref, p_ref,
+                 base_ref, hi_ref, lo_ref, scale_ref):
+    odd = is_odd()
     n_rows, loads = x_ref.shape
-    face = part_ref.shape[0] // 2
-    total = rhs_ref[...] - product(near_ref[...], wide_halves(x_ref[...]))
-    base_ref[...] = total - fold(dot(sel_ref[:, face : 2 * face], wide_halves(part_ref[face:])))
+    face = out_b_ref.shape[0]
+    got_ref = got_ref.at[odd.astype(jnp.int32)]
+    block = schur_ref[face : 2 * face, pl.ds(place(odd, 2, face), face)]
+    own = part_ref[face:] + product(block, wide_halves(got_ref[:face]))
+    back = got_ref[face : 2 * face] + product(got_ref[2 * face :], wide_halves(out_b_ref[...]))
+    both = jnp.concatenate([wide_halves(own), wide_halves(back)], axis=0)
+    near = product(near_ref[...], wide_halves(x_ref[...]))
+    base_ref[...] = rhs_ref[...] - near - fold(dot(sel_ref[:, face:], both))
     hi_ref[...], lo_ref[...] = halves(u_ref[...].T)
     scale_ref[...] = jnp.broadcast_to(p_ref[...], (loads, n_rows)).T
-
-
-def force_kernel(got_ref, part_ref, schur_ref, _, fa_ref):
-    odd = is_odd()
-    face = fa_ref.shape[0]
-    block = schur_ref[pl.ds(place(odd, 0, face), face), pl.ds(place(odd, 2, face), face)]
-    fa_ref[...] = part_ref[:face] + product(block, wide_halves(got_ref[:face]))
-
-
-def own_kernel(got_ref, out_b_ref, schur_ref, sel_ref, base_ref, next_ref):
-    odd = is_odd()
-    face = out_b_ref.shape[0]
-    block = schur_ref[face : 2 * face, pl.ds(place(odd, 2, face), face)]
-    own = product(block, wide_halves(got_ref[:face]))
-    back = got_ref[face : 2 * face] + product(got_ref[2 * face :], wide_halves(out_b_ref[...]))
-    both = jnp.concatenate([wide_halves(own), wide_halves(back)], axis=0)
-    next_ref[...] = base_ref[...] - fold(dot(sel_ref[:, face:], both))
 
 
 def far_kernel(coeff_ref, hi_ref, lo_ref, base_ref, next_ref):
@@ -173,8 +171,11 @@
     face = send_rows.shape[2]
     tiles, top, _ = u_basis.shape
     size = lax.axis_size("wide")
+    parts = lax.axis_size("groups")
     inside = [(i, i ^ 1) for i in range(size) if i ^ 1 < size]
-    across = [(i, j) for i in range(size) for j in [i - 1 if i % 2 == 0 else i + 1] if 0 <= j < size]
+    across = [[g * size + i - 1, g * size + i] for g in range(parts) for i in range(2, size, 2)]
+    for g in range(0, parts, 2):
+        across += [[g * size + size - 1, (g + 1) * size + size - 1], [(g + 1) * size, g * size]]
     schur = schur.reshape(3 * face, 3 * face)
     block = ((face, loads), f32)
     field = ((n_rows, loads), f32)
@@ -218,16 +219,15 @@
     pay, part = call(
         across_kernel, "across", [((3 * face, loads), f32), ((2 * face, loads), f32)], (in_a, out_m, out_b, schur), cost=10000000000
     )
-    got = lax.ppermute(pay, "wide", across)
+    got = lax.all_gather(pay, ("groups", "wide"), axis_index_groups=across)
+    (f_a,) = call(force_kernel, "force", [block], (got, part, schur))
+    back = lax.ppermute(f_a, "wide", inside)
     base, u_hi, u_lo, scale = call(
-        base_kernel,
-        "base",
+        local_kernel,
+        "local",
         [field, factor, factor, field],
-        (rhs, near, x, sel, part, u, p),
-    )
-    (f_a,) = call(force_kernel, "force", [block], (got, part, schur, base), cost=0)
-    back = lax.ppermute(f_a, "wide", inside)
-    (base,) = call(own_kernel, "own", [field], (got, out_b, schur, sel, base))
+        (got, part, out_b, schur, sel, rhs, near, x, u, p),
+    )
     (base,) = call(far_kernel, "far", [field], (gathered.reshape(tiles * top, loads), u_hi, u_lo, base))
     return call(
         final_kernel, "final", [field, field], (back, sel, base, x, scale), spaces=[jax.ShapeDtypeStruct] * 2

time: 23 us -> 22.5 us (0.978)
  the two profiles are of different devices: /device:TPU:9 before, /device:TPU:19 now
where the time goes in v4:
time: 22.5 us; the launch traced here: 22.3 us
  starting transfers between devices  8.84 us (39%)
  blocking collectives  8.38 us (37%)
  Pallas kernels  4.23 us (19%)
  between operations  0.68 us (3%)
    all_gather x1, blocking collectives, body(): got = lax.all_gather(pay, ('groups', 'wide'), axis_index_groups=across)  8.38 us
    all_to_all x1, starting transfers between devices, body(): lax.all_to_all(coeff, 'wide', split_axis=0, concat_axis=0, tiled=True)  5.94 us
    pallas_call x6, Pallas kernels, call(): pl.pallas_call(kernel, out_shape=tuple((space(s, t) for space, (s, t) in...  4.23 us
    ppermute x1, starting transfers between devices, body(): back = lax.ppermute(f_a, 'wide', inside)  2.16 us
    ppermute x1, starting transfers between devices, body(): in_a = lax.ppermute(out_a, 'wide', inside)  0.74 us
  transfers between devices with their start and end apart: 3, of which 1 were waited for; matrix products, arithmetic and copies ran while one was open for 0% of the time, Pallas kernels for 5%

profile of v4, /device:TPU:19, one launch (start us, length us, event | category | flops | bytes accessed | tf_op | source)
XLA Modules:
  0.0 22.3 jit_solution(6968569151312241854)
XLA Ops:
  0.6 2.2 %send.1 = (f32[16,32,128]{2,1,0:T(8,128)}, f32[128,128]{1,0:T(8,128)S(1)}, f32[128,128]{1,0:T(8,128)S(1)}, f32[128,128]{1,0:T(8,128)S(1)}, bf16[256,384]{1,0:T(8...) custom-call(f32[256,128]{1,0:T(8,128)} %x_hbm.1, ...), custom_call_target="tpu_custom_call" | custom-call | tf_op jit(solution)/shard_map/send/pallas_call | solution.py:155
  2.8 0.7 %collective-permute-start = (f32[128,128]{1,0:T(8,128)S(1)}, f32[128,128]{1,0:T(8,128)S(1)}, u32[]{:S(2)}, u32[]{:S(2)}) collective-permute-start(f32[128,128]{1,0:T(8,128)S(1)} %get-tuple-element.19), channel_id=1, source_target_pairs={{0,1},{1,0},{2,3},{3,2},{4,5},{5,4},{6,7},{7,6},{8,9},{9,8},{10,11... | collective-permute-start | bytes 196616 | tf_op jit(solution)/shard_map/ppermute | solution.py:218
  3.6 5.9 %all-to-all-start = ((f32[16,32,128]{2,1,0:T(8,128)}), f32[16,32,128]{2,1,0:T(8,128)S(1)}, u32[]{:S(2)}, u32[]{:S(2)}) async-start(f32[16,32,128]{2,1,0:T(8,128)} %get-tuple-element.26), calls=%async_computation | async-start | bytes 524288 | tf_op jit(solution)/shard_map/all_to_all | solution.py:217
  9.5 0.0 collective-permute-done.a_ref
  9.5 0.3 %across.1 = (f32[384,128]{1,0:T(8,128)S(1)}, f32[256,128]{1,0:T(8,128)S(1)}) custom-call(f32[128,128]{1,0:T(8,128)S(1)} %collective-permute-done.a_ref, f32[128,128]{1,0:T(8,128)S(1)} %get-tuple-element.20.m_ref, f32[128,128]{1,0:T(8,128)S(1)} %get-tuple-element.21.b_ref.out_b_ref, f32[384,384]{1,0:T(8,128)S(1)} %get-tuple-element.22.schur_ref), custom_call_target="tpu_custom_call" | custom-call | flops 10000000000 | tf_op jit(solution)/shard_map/across/pallas_call | solution.py:155
  9.8 8.4 %all-gather = f32[768,128]{1,0:T(8,128)S(1)} all-gather(f32[384,128]{1,0:T(8,128)S(1)} %get-tuple-element.23), channel_id=2, replica_groups={{1,2},{3,4},{5,6},{7,8},{9,10},{11,12},{13,14},{17,18},{19,20},{21,22},..., dimensions={0}, use_global_device_ids=true | all-gather | bytes 589824 | tf_op jit(solution)/shard_map/all_gather | solution.py:222
  18.2 0.2 force.1
  18.3 2.2 %collective-permute-start.1 = (f32[128,128]{1,0:T(8,128)S(1)}, f32[128,128]{1,0:T(8,128)S(1)}, u32[]{:S(2)}, u32[]{:S(2)}) collective-permute-start(f32[128,128]{1,0:T(8,128)S(1)} %force.1), channel_id=1, source_target_pairs={{0,1},{1,0},{2,3},{3,2},{4,5},{5,4},{6,7},{7,6},{8,9},{9,8},{10,11... | collective-permute-start | bytes 196616 | tf_op jit(solution)/shard_map/ppermute | solution.py:224
  20.5 0.4 %local.1 = (f32[256,128]{1,0:T(8,128)S(1)}, bf16[256,512]{1,0:T(8,128)(2,1)S(1)}, bf16[256,512]{1,0:T(8,128)(2,1)S(1)}, f32[256,128]{1,0:T(8,128)S(1)}) custom-call(f32[2,384,128]{2,1,0:T(8,128)S(1)} %bitcast.9, f32[256,128]{1,0:T(8,128)S(1)} %get-tuple-element.24.part_ref, f32[128,128]{1,0:T(8,128)S(1)} %get-tuple-element.21.b_ref.out_b_ref, ...), custom_call_target="tpu_custom_call" | custom-call | tf_op jit(solution)/shard_map/local/pallas_call | solution.py:155
  20.9 0.0 all-to-all-done
  21.0 0.3 %far.1.base_ref = f32[256,128]{1,0:T(8,128)S(1)} custom-call(f32[512,128]{1,0:T(8,128)S(1)} %bitcast.10, bf16[256,512]{1,0:T(8,128)(2,1)S(1)} %get-tuple-element.32.hi_ref, bf16[256,512]{1,0:T(8,128)(2,1)S(1)} %get-tuple-element.33.lo_ref, f32[256,128]{1,0:T(8,128)S(1)} %get-tuple-element.34.base_ref), custom_call_target="tpu_custom_call" | custom-call | tf_op jit(solution)/shard_map/far/pallas_call | solution.py:155
  21.3 0.1 collective-permute-done.1.back_ref
  21.4 0.9 %final.1 = (f32[256,128]{1,0:T(8,128)}, f32[256,128]{1,0:T(8,128)}) custom-call(f32[128,128]{1,0:T(8,128)S(1)} %collective-permute-done.1.back_ref, bf16[256,384]{1,0:T(8,128)(2,1)S(1)} %get-tuple-element.25.sel_ref, f32[256,128]{1,0:T(8,128)S(1)} %far.1.base_ref, f32[256,128]{1,0:T(8,128)S(1)} %get-tuple-element.29.x_ref, ...), custom_call_target="tpu_custom_call" | custom-call | tf_op jit(solution)/shard_map/final/pallas_call | solution.py:155
Async XLA Ops:
  2.8 6.7 %collective-permute-start = (f32[128,128]{1,0:T(8,128)S(1)}, f32[128,128]{1,0:T(8,128)S(1)}, u32[]{:S(2)}, u32[]{:S(2)}) collective-permute-start(f32[128,128]{1,0:T(8,128)S(1)} %get-tuple-element.19), channel_id=1, source_target_pairs={{0,1},{1,0},{2,3},{3,2},{4,5},{5,4},{6,7},{7,6},{8,9},{9,8},{10,11... | collective-permute-start | bytes 196616 | tf_op jit(solution)/shard_map/ppermute | solution.py:218
  3.6 17.4 %all-to-all-start = ((f32[16,32,128]{2,1,0:T(8,128)}), f32[16,32,128]{2,1,0:T(8,128)S(1)}, u32[]{:S(2)}, u32[]{:S(2)}) async-start(f32[16,32,128]{2,1,0:T(8,128)} %get-tuple-element.26), calls=%async_computation | async-start | bytes 524288 | tf_op jit(solution)/shard_map/all_to_all | solution.py:217
  18.3 3.1 %collective-permute-start.1 = (f32[128,128]{1,0:T(8,128)S(1)}, f32[128,128]{1,0:T(8,128)S(1)}, u32[]{:S(2)}, u32[]{:S(2)}) collective-permute-start(f32[128,128]{1,0:T(8,128)S(1)} %force.1), channel_id=1, source_target_pairs={{0,1},{1,0},{2,3},{3,2},{4,5},{5,4},{6,7},{7,6},{8,9},{9,8},{10,11... | collective-permute-start | bytes 196616 | tf_op jit(solution)/shard_map/ppermute | solution.py:224

commit v5 on v2

--- a/solution.py
+++ b/solution.py
@@ -1,3 +1,5 @@
+import math
+
 import jax
 import jax.numpy as jnp
 from jax import lax
@@ -41,6 +43,10 @@
 
 def is_odd():
     return lax.axis_index("wide") % 2 == 1
+
+
+def tiles_at_once(tiles, top):
+    return math.gcd(tiles, max(1, 256 // top))
 
 
 def send_kernel(x_hbm, v_hbm, rows_hbm, count_hbm, rank_hbm, schur_hbm, u_hbm, near_hbm, rhs_hbm, p_hbm,
@@ -60,7 +66,7 @@
     x_wide = wide_halves(x_ref[...])
     for move in moves[1:3]:
         move.wait()
-    step = max(1, min(tiles, 256 // top))
+    step = tiles_at_once(tiles, top)
     k = lax.broadcasted_iota(jnp.int32, (top, loads), 0)
 
     def out_move(s):
@@ -98,11 +104,12 @@
     return pl.multiple_of(jnp.where(odd == (spot == 0), 2 * face, 0), face)
 
 
-def across_kernel(a_ref, m_ref, b_ref, schur_ref, pay_ref, part_ref):
+def across_kernel(a_ref, m_ref, schur_ref, pay_ref, part_ref):
     odd = is_odd()
     face = a_ref.shape[0]
+    last = pl.ds(place(odd, 2, face), face)
     known = jnp.concatenate([wide_halves(a_ref[...]), wide_halves(m_ref[...])], axis=0)
-    pay_ref[:face] = b_ref[...]
+    pay_ref[face:] = schur_ref[last, last]
     for spot in (2, 0, 1):
         rows = pl.ds(place(odd, spot, face), face)
         block = jnp.concatenate(
@@ -110,41 +117,39 @@
         )
         out = product(block, known)
         if spot == 2:
-            pay_ref[face : 2 * face] = out
-            pay_ref[2 * face :] = schur_ref[rows, pl.ds(place(odd, 2, face), face)]
+            pay_ref[:face] = out
         else:
             part_ref[spot * face : (spot + 1) * face] = out
 
 
-def base_kernel(rhs_ref, near_ref, x_ref, sel_ref, part_ref, u_ref, p_ref, base_ref, hi_ref, lo_ref, scale_ref):
+def base_kernel(rhs_ref, near_ref, x_ref, u_ref, p_ref, _, base_ref, hi_ref, lo_ref, scale_ref):
     n_rows, loads = x_ref.shape
-    face = part_ref.shape[0] // 2
-    total = rhs_ref[...] - product(near_ref[...], wide_halves(x_ref[...]))
-    base_ref[...] = total - fold(dot(sel_ref[:, face : 2 * face], wide_halves(part_ref[face:])))
+    base_ref[...] = rhs_ref[...] - product(near_ref[...], wide_halves(x_ref[...]))
     hi_ref[...], lo_ref[...] = halves(u_ref[...].T)
     scale_ref[...] = jnp.broadcast_to(p_ref[...], (loads, n_rows)).T
 
 
-def force_kernel(got_ref, part_ref, schur_ref, _, fa_ref):
+def force_kernel(got_ref, part_ref, schur_ref, fa_ref):
     odd = is_odd()
     face = fa_ref.shape[0]
     block = schur_ref[pl.ds(place(odd, 0, face), face), pl.ds(place(odd, 2, face), face)]
-    fa_ref[...] = part_ref[:face] + product(block, wide_halves(got_ref[:face]))
-
-
-def own_kernel(got_ref, out_b_ref, schur_ref, sel_ref, base_ref, next_ref):
-    odd = is_odd()
-    face = out_b_ref.shape[0]
+    fa_ref[...] = part_ref[:face] + product(block, wide_halves(got_ref[...]))
+
+
+def own_kernel(got_ref, part_ref, schur_ref, sel_ref, base_ref, next_ref):
+    odd = is_odd()
+    face = got_ref.shape[0]
     block = schur_ref[face : 2 * face, pl.ds(place(odd, 2, face), face)]
-    own = product(block, wide_halves(got_ref[:face]))
-    back = got_ref[face : 2 * face] + product(got_ref[2 * face :], wide_halves(out_b_ref[...]))
-    both = jnp.concatenate([wide_halves(own), wide_halves(back)], axis=0)
-    next_ref[...] = base_ref[...] - fold(dot(sel_ref[:, face:], both))
-
-
-def pair_kernel(back_ref, sel_ref, base_ref, next_ref):
+    own = part_ref[face:] + product(block, wide_halves(got_ref[...]))
+    next_ref[...] = base_ref[...] - fold(dot(sel_ref[:, face : 2 * face], wide_halves(own)))
+
+
+def back_kernel(pay_ref, out_b_ref, back_ref, sel_ref, base_ref, next_ref):
     face = back_ref.shape[0]
-    next_ref[...] = base_ref[...] - fold(dot(sel_ref[:, :face], wide_halves(back_ref[...])))
+    b = pay_ref[:face] + product(pay_ref[face:], wide_halves(out_b_ref[...]))
+    a = dot(sel_ref[:, :face], wide_halves(back_ref[...]))
+    b = dot(sel_ref[:, 2 * face :], wide_halves(b))
+    next_ref[...] = base_ref[...] - fold(a + b)
 
 
 def final_kernel(coeff_ref, hi_ref, lo_ref, base_ref, x_ref, scale_ref, up_ref, res_ref):
@@ -172,13 +177,15 @@
     face = send_rows.shape[2]
     tiles, top, _ = u_basis.shape
     size = lax.axis_size("wide")
+    parts = lax.axis_size("groups")
     inside = [(i, i ^ 1) for i in range(size) if i ^ 1 < size]
-    across = [(i, j) for i in range(size) for j in [i - 1 if i % 2 == 0 else i + 1] if 0 <= j < size]
+    across = [(g * size + i, g * size + (i - 1 if i % 2 == 0 else i + 1)) for g in range(parts) for i in range(1, size - 1)]
+    across += [(g * size + i, (g + 1) % parts * size + i) for g in range(parts) for i in (0, size - 1)]
     schur = schur.reshape(3 * face, 3 * face)
     block = ((face, loads), f32)
     field = ((n_rows, loads), f32)
     factor = ((n_rows, tiles * top), bf16)
-    steps = tiles // max(1, min(tiles, 256 // top))
+    steps = tiles // tiles_at_once(tiles, top)
 
     arrays = (
         iterate,
@@ -214,20 +221,18 @@
     )
     gathered = lax.all_to_all(coeff, "wide", split_axis=0, concat_axis=0, tiled=True)
     in_a = lax.ppermute(out_a, "wide", inside)
+    got = lax.ppermute(out_b, ("groups", "wide"), across)
     pay, part = call(
-        across_kernel, "across", [((3 * face, loads), f32), ((2 * face, loads), f32)], (in_a, out_m, out_b, schur)
-    )
-    got = lax.ppermute(pay, "wide", across)
+        across_kernel, "across", [((2 * face, loads), f32)] * 2, (in_a, out_m, schur)
+    )
+    sums = lax.ppermute(pay, ("groups", "wide"), across)
     base, u_hi, u_lo, scale = call(
-        base_kernel,
-        "base",
-        [field, factor, factor, field],
-        (rhs, near, x, sel, part, u, p),
-    )
-    (f_a,) = call(force_kernel, "force", [block], (got, part, schur, base))
+        base_kernel, "base", [field, factor, factor, field], (rhs, near, x, u, p, part)
+    )
+    (f_a,) = call(force_kernel, "force", [block], (got, part, schur))
     back = lax.ppermute(f_a, "wide", inside)
-    (base,) = call(own_kernel, "own", [field], (got, out_b, schur, sel, base))
-    (base,) = call(pair_kernel, "pair", [field], (back, sel, base))
+    (base,) = call(own_kernel, "own", [field], (got, part, schur, sel, base))
+    (base,) = call(back_kernel, "back", [field], (sums, out_b, back, sel, base))
     return call(
         final_kernel,
         "final",

time: 23.8 us -> 21.6 us (0.908)
  waiting for transfers between devices: 7.95 us -> 1.9 us
  starting transfers between devices: 10.3 us -> 14.1 us
    ppermute x1, starting transfers between devices: 0.07 us -> 4.8 us  [body(): back = lax.ppermute(f_a, 'wide', inside)]
    ppermute x1 -> x2, waiting for transfers between devices: 6.19 us -> 1.59 us  [the longest x1 1.59 us: body(): got = lax.ppermute(out_b, ('groups', 'wide'), across)]
    ppermute x1 -> x2, starting transfers between devices: 3.34 us -> 2.39 us  [the longest x1 1.22 us: body(): got = lax.ppermute(out_b, ('groups', 'wide'), across)]
    ppermute x1, waiting for transfers between devices: 0.9 us -> 0.01 us  [body(): in_a = lax.ppermute(out_a, 'wide', inside)]
    ppermute x1, waiting for transfers between devices: 0.86 us -> 0.3 us  [body(): back = lax.ppermute(f_a, 'wide', inside)]
  transfers between devices with their start and end apart: 4 -> 5, of which waited for: 3 -> 2; matrix products, arithmetic and copies ran while one was open for 0% -> 0% of each run, Pallas kernels for 5% -> 7%
where the time goes in v5:
time: 21.6 us; the launch traced here: 21.2 us
  starting transfers between devices  14.1 us (65%)
  Pallas kernels  4.59 us (21%)
  waiting for transfers between devices  1.9 us (9%)
  between operations  0.68 us (3%)
    all_to_all x1, starting transfers between devices, body(): lax.all_to_all(coeff, 'wide', split_axis=0, concat_axis=0, tiled=True)  6.51 us
    ppermute x1, starting transfers between devices, body(): back = lax.ppermute(f_a, 'wide', inside)  4.8 us
    pallas_call x7, Pallas kernels, call(): pl.pallas_call(kernel, out_shape=tuple((space(s, t) for space, (s, t) in...  4.59 us
    ppermute x1, waiting for transfers between devices, body(): got = lax.ppermute(out_b, ('groups', 'wide'), across)  1.59 us
    ppermute x1, starting transfers between devices, body(): got = lax.ppermute(out_b, ('groups', 'wide'), across)  1.22 us
    ppermute x1, starting transfers between devices, body(): sums = lax.ppermute(pay, ('groups', 'wide'), across)  1.17 us
  transfers between devices with their start and end apart: 5, of which 2 were waited for; matrix products, arithmetic and copies ran while one was open for 0% of the time, Pallas kernels for 7%

profile of v5, /device:TPU:19, one launch (start us, length us, event | category | flops | bytes accessed | tf_op | source)
XLA Modules:
  0.0 21.2 jit_solution(9383862732267945196)
XLA Ops:
  0.6 2.2 %send.1 = (f32[16,32,128]{2,1,0:T(8,128)}, f32[128,128]{1,0:T(8,128)S(1)}, f32[128,128]{1,0:T(8,128)S(1)}, f32[128,128]{1,0:T(8,128)S(1)}, bf16[256,384]{1,0:T(8...) custom-call(f32[256,128]{1,0:T(8,128)} %x_hbm.1, ...), custom_call_target="tpu_custom_call" | custom-call | tf_op jit(solution)/shard_map/send/pallas_call | solution.py:162
  2.8 6.5 %all-to-all-start = ((f32[16,32,128]{2,1,0:T(8,128)}), f32[16,32,128]{2,1,0:T(8,128)S(1)}, u32[]{:S(2)}, u32[]{:S(2)}) async-start(f32[16,32,128]{2,1,0:T(8,128)} %get-tuple-element.19), calls=%async_computation | async-start | bytes 524288 | tf_op jit(solution)/shard_map/all_to_all | solution.py:222
  9.3 0.4 %collective-permute-start = (f32[128,128]{1,0:T(8,128)S(1)}, f32[128,128]{1,0:T(8,128)S(1)}, u32[]{:S(2)}, u32[]{:S(2)}) collective-permute-start(f32[128,128]{1,0:T(8,128)S(1)} %get-tuple-element.25), channel_id=1, source_target_pairs={{0,1},{1,0},{2,3},{3,2},{4,5},{5,4},{6,7},{7,6},{8,9},{9,8},{10,11... | collective-permute-start | bytes 196616 | tf_op jit(solution)/shard_map/ppermute | solution.py:223
  9.7 1.2 %collective-permute-start.2 = (f32[128,128]{1,0:T(8,128)S(1)}, f32[128,128]{1,0:T(8,128)S(1)}, u32[]{:S(2)}, u32[]{:S(2)}) collective-permute-start(f32[128,128]{1,0:T(8,128)S(1)} %get-tuple-element.32.out_b_ref), channel_id=1, source_target_pairs={{1,2},{2,1},{3,4},{4,3},{5,6},{6,5},{7,8},{8,7},{9,10},{10,9},{11,... | collective-permute-start | bytes 196616 | tf_op jit(solution)/shard_map/ppermute | solution.py:224
  10.9 0.0 collective-permute-done.a_ref
  10.9 0.3 %across.1 = (f32[256,128]{1,0:T(8,128)S(1)}, f32[256,128]{1,0:T(8,128)S(1)}) custom-call(f32[128,128]{1,0:T(8,128)S(1)} %collective-permute-done.a_ref, f32[128,128]{1,0:T(8,128)S(1)} %get-tuple-element.26.m_ref, f32[384,384]{1,0:T(8,128)S(1)} %get-tuple-element.27.schur_ref), custom_call_target="tpu_custom_call" | custom-call | tf_op jit(solution)/shard_map/across/pallas_call | solution.py:162
  11.2 1.2 %collective-permute-start.1 = (f32[256,128]{1,0:T(8,128)S(1)}, f32[256,128]{1,0:T(8,128)S(1)}, u32[]{:S(2)}, u32[]{:S(2)}) collective-permute-start(f32[256,128]{1,0:T(8,128)S(1)} %get-tuple-element.31), channel_id=1, source_target_pairs={{1,2},{2,1},{3,4},{4,3},{5,6},{6,5},{7,8},{8,7},{9,10},{10,9},{11,... | collective-permute-start | bytes 393224 | tf_op jit(solution)/shard_map/ppermute | solution.py:228
  12.4 1.6 %collective-permute-done.2.got_ref = f32[128,128]{1,0:T(8,128)S(1)} collective-permute-done((f32[128,128]{1,0:T(8,128)S(1)}, f32[128,128]{1,0:T(8,128)S(1)}, u32[]{:S(2)}, u32[]{:S(2)}) %collective-permute-start.2) | collective-permute-done | bytes 65568 | tf_op jit(solution)/shard_map/ppermute | solution.py:224
  13.9 0.2 force.1
  14.1 4.8 %collective-permute-start.3 = (f32[128,128]{1,0:T(8,128)S(1)}, f32[128,128]{1,0:T(8,128)S(1)}, u32[]{:S(2)}, u32[]{:S(2)}) collective-permute-start(f32[128,128]{1,0:T(8,128)S(1)} %force.1), channel_id=1, source_target_pairs={{0,1},{1,0},{2,3},{3,2},{4,5},{5,4},{6,7},{7,6},{8,9},{9,8},{10,11... | collective-permute-start | bytes 196616 | tf_op jit(solution)/shard_map/ppermute | solution.py:233
  18.9 0.2 %base.1 = (f32[256,128]{1,0:T(8,128)S(1)}, bf16[256,512]{1,0:T(8,128)(2,1)S(1)}, bf16[256,512]{1,0:T(8,128)(2,1)S(1)}, f32[256,128]{1,0:T(8,128)S(1)}) custom-call(f32[256,128]{1,0:T(8,128)S(1)} %get-tuple-element.20.rhs_ref, f32[256,256]{1,0:T(8,128)S(1)} %get-tuple-element.21.near_ref, f32[256,128]{1,0:T(8,128)S(1)} %get-tuple-element.22.x_ref, ...), custom_call_target="tpu_custom_call" | custom-call | tf_op jit(solution)/shard_map/base/pallas_call | solution.py:162
  19.2 0.3 %own.1.base_ref = f32[256,128]{1,0:T(8,128)S(1)} custom-call(f32[128,128]{1,0:T(8,128)S(1)} %collective-permute-done.2.got_ref, f32[256,128]{1,0:T(8,128)S(1)} %get-tuple-element.28._.part_ref, f32[384,384]{1,0:T(8,128)S(1)} %get-tuple-element.27.schur_ref, bf16[256,384]{1,0:T(8,128)(2,1)S(1)} %get-tuple-element.33.sel_ref, ...), custom_call_target="tpu_custom_call" | custom-call | tf_op jit(solution)/shard_map/own/pallas_call | solution.py:162
  19.5 0.3 %collective-permute-done.3.back_ref = f32[128,128]{1,0:T(8,128)S(1)} collective-permute-done((f32[128,128]{1,0:T(8,128)S(1)}, f32[128,128]{1,0:T(8,128)S(1)}, u32[]{:S(2)}, u32[]{:S(2)}) %collective-permute-start.3) | collective-permute-done | bytes 65568 | tf_op jit(solution)/shard_map/ppermute | solution.py:233
  19.8 0.0 collective-permute-done.1.pay_ref
  19.8 0.4 %back.1.base_ref = f32[256,128]{1,0:T(8,128)S(1)} custom-call(f32[256,128]{1,0:T(8,128)S(1)} %collective-permute-done.1.pay_ref, f32[128,128]{1,0:T(8,128)S(1)} %get-tuple-element.32.out_b_ref, f32[128,128]{1,0:T(8,128)S(1)} %collective-permute-done.3.back_ref, bf16[256,384]{1,0:T(8,128)(2,1)S(1)} %get-tuple-element.33.sel_ref, f32[256,128]{1,0:T(8,128)S(1)} %own.1.base_ref), custom_call_target="tpu_custom_call" | custom-call | tf_op jit(solution)/shard_map/back/pallas_call | solution.py:162
  20.2 0.0 all-to-all-done
  20.2 1.0 %final.1 = (f32[256,128]{1,0:T(8,128)}, f32[256,128]{1,0:T(8,128)}) custom-call(f32[512,128]{1,0:T(8,128)S(1)} %bitcast.7, bf16[256,512]{1,0:T(8,128)(2,1)S(1)} %get-tuple-element.29.hi_ref, bf16[256,512]{1,0:T(8,128)(2,1)S(1)} %get-tuple-element.30.lo_ref, f32[256,128]{1,0:T(8,128)S(1)} %back.1.base_ref, f32[256,128]{1,0:T(8,128)S(1)} %get-tuple-element.22.x_ref, ...), custom_call_target="tpu_custom_call" | custom-call | tf_op jit(solution)/shard_map/final/pallas_call | solution.py:162
Async XLA Ops:
  2.8 17.4 %all-to-all-start = ((f32[16,32,128]{2,1,0:T(8,128)}), f32[16,32,128]{2,1,0:T(8,128)S(1)}, u32[]{:S(2)}, u32[]{:S(2)}) async-start(f32[16,32,128]{2,1,0:T(8,128)} %get-tuple-element.19), calls=%async_computation | async-start | bytes 524288 | tf_op jit(solution)/shard_map/all_to_all | solution.py:222
  9.3 1.6 %collective-permute-start = (f32[128,128]{1,0:T(8,128)S(1)}, f32[128,128]{1,0:T(8,128)S(1)}, u32[]{:S(2)}, u32[]{:S(2)}) collective-permute-start(f32[128,128]{1,0:T(8,128)S(1)} %get-tuple-element.25), channel_id=1, source_target_pairs={{0,1},{1,0},{2,3},{3,2},{4,5},{5,4},{6,7},{7,6},{8,9},{9,8},{10,11... | collective-permute-start | bytes 196616 | tf_op jit(solution)/shard_map/ppermute | solution.py:223
  9.7 4.2 %collective-permute-start.2 = (f32[128,128]{1,0:T(8,128)S(1)}, f32[128,128]{1,0:T(8,128)S(1)}, u32[]{:S(2)}, u32[]{:S(2)}) collective-permute-start(f32[128,128]{1,0:T(8,128)S(1)} %get-tuple-element.32.out_b_ref), channel_id=1, source_target_pairs={{1,2},{2,1},{3,4},{4,3},{5,6},{6,5},{7,8},{8,7},{9,10},{10,9},{11,... | collective-permute-start | bytes 196616 | tf_op jit(solution)/shard_map/ppermute | solution.py:224
  11.2 8.7 %collective-permute-start.1 = (f32[256,128]{1,0:T(8,128)S(1)}, f32[256,128]{1,0:T(8,128)S(1)}, u32[]{:S(2)}, u32[]{:S(2)}) collective-permute-start(f32[256,128]{1,0:T(8,128)S(1)} %get-tuple-element.31), channel_id=1, source_target_pairs={{1,2},{2,1},{3,4},{4,3},{5,6},{6,5},{7,8},{8,7},{9,10},{10,9},{11,... | collective-permute-start | bytes 393224 | tf_op jit(solution)/shard_map/ppermute | solution.py:228
  14.1 5.7 %collective-permute-start.3 = (f32[128,128]{1,0:T(8,128)S(1)}, f32[128,128]{1,0:T(8,128)S(1)}, u32[]{:S(2)}, u32[]{:S(2)}) collective-permute-start(f32[128,128]{1,0:T(8,128)S(1)} %force.1), channel_id=1, source_target_pairs={{0,1},{1,0},{2,3},{3,2},{4,5},{5,4},{6,7},{7,6},{8,9},{9,8},{10,11... | collective-permute-start | bytes 196616 | tf_op jit(solution)/shard_map/ppermute | solution.py:233

commit v6 on v5

--- a/solution.py
+++ b/solution.py
@@ -45,6 +45,18 @@
     return lax.axis_index("wide") % 2 == 1
 
 
+def lead(size):
+    pairs = size // 2
+    return (2 * (pairs // 2 + math.isqrt(pairs) // 2) + 1) % size
+
+
+def turned(hbm, ref, by):
+    rest = hbm.shape[0] - by
+    if by == 0:
+        return [(hbm, ref)]
+    return [(hbm.at[pl.ds(by, rest)], ref.at[pl.ds(0, rest)]), (hbm.at[pl.ds(0, by)], ref.at[pl.ds(rest, by)])]
+
+
 def tiles_at_once(tiles, top):
     return math.gcd(tiles, max(1, 256 // top))
 
@@ -55,16 +67,17 @@
     n_rows, loads = x_ref.shape
     face = rows_ref.shape[2]
     tiles, top, _ = v_ref.shape
-    pairs = (
-        (x_hbm, x_ref), (rank_hbm, rank_ref), (v_hbm, v_ref), (rows_hbm, rows_ref), (count_hbm, count_ref),
-        (schur_hbm, schur_ref), (u_hbm, u_ref), (near_hbm, near_ref), (rhs_hbm, rhs_ref), (p_hbm, p_ref),
-    )
-    moves = [pltpu.make_async_copy(src, dst, sems.at[i]) for i, (src, dst) in enumerate(pairs)]
+    first = lead(tiles)
+    early = [(x_hbm, x_ref), (rank_hbm, rank_ref)] + turned(v_hbm, v_ref, first)
+    middle = [(rows_hbm, rows_ref), (count_hbm, count_ref)]
+    late = [(schur_hbm, schur_ref)] + turned(u_hbm, u_ref, first * top)
+    late += [(near_hbm, near_ref), (rhs_hbm, rhs_ref), (p_hbm, p_ref)]
+    moves = [pltpu.make_async_copy(src, dst, sems.at[i]) for i, (src, dst) in enumerate(early + middle + late)]
     for move in moves:
         move.start()
     moves[0].wait()
     x_wide = wide_halves(x_ref[...])
-    for move in moves[1:3]:
+    for move in moves[1 : len(early)]:
         move.wait()
     step = tiles_at_once(tiles, top)
     k = lax.broadcasted_iota(jnp.int32, (top, loads), 0)
@@ -77,9 +90,10 @@
         part = v_ref[s * step : (s + 1) * step].reshape(step * top, n_rows)
         out = product(part, x_wide).reshape(step, top, loads)
         for t in range(step):
-            coeff_ref[s * step + t] = jnp.where(k < rank_ref[s * step + t], out[t], 0.0)
+            at = s * step + t
+            coeff_ref[at] = jnp.where(k < rank_ref[(at + first) % tiles], out[t], 0.0)
         out_move(s).start()
-    for move in moves[3:5]:
+    for move in moves[len(early) : -len(late)]:
         move.wait()
     odd = is_odd()
     slots = (jnp.where(odd, 0, 2), 1, jnp.where(odd, 2, 0))
@@ -94,7 +108,7 @@
         out_ref[...] = fold(dot(select, x_wide))
     for s in range(tiles // step):
         out_move(s).wait()
-    for move in moves[5:]:
+    for move in moves[-len(late) :]:
         move.wait()
 
 
@@ -214,12 +228,13 @@
             pltpu.SMEM((3,), jnp.int32),
             pltpu.SMEM((tiles,), jnp.int32),
             pltpu.VMEM((tiles, top, loads), f32),
-            pltpu.SemaphoreType.DMA((len(arrays),)),
+            pltpu.SemaphoreType.DMA((len(arrays) + 2,)),
             pltpu.SemaphoreType.DMA((steps,)),
         ],
         [pltpu.HBM] + [pltpu.VMEM] * 10,
     )
-    gathered = lax.all_to_all(coeff, "wide", split_axis=0, concat_axis=0, tiled=True)
+    order = [(i + lead(size)) % size for i in range(size)]
+    gathered = lax.all_to_all(coeff, "wide", split_axis=0, concat_axis=0, tiled=True, axis_index_groups=[order])
     in_a = lax.ppermute(out_a, "wide", inside)
     got = lax.ppermute(out_b, ("groups", "wide"), across)
     pay, part = call(

time: 21.6 us -> 19.8 us (0.917)
  starting transfers between devices: 14.1 us -> 10.8 us
  waiting for transfers between devices: 1.9 us -> 3.3 us
    all_to_all x1, starting transfers between devices: 6.51 us -> 4.69 us  [body(): lax.all_to_all(coeff, 'wide', split_axis=0, concat_axis=0, tiled=True, ax...]
    ppermute x1, starting transfers between devices: 1.22 us -> 0.34 us  [body(): got = lax.ppermute(out_b, ('groups', 'wide'), across)]
    ppermute x1, waiting for transfers between devices: 1.59 us -> 2.43 us  [body(): got = lax.ppermute(out_b, ('groups', 'wide'), across)]
    ppermute x1, waiting for transfers between devices: 0.01 us -> 0.56 us  [body(): in_a = lax.ppermute(out_a, 'wide', inside)]
    ppermute x1, starting transfers between devices: 4.8 us -> 4.52 us  [body(): back = lax.ppermute(f_a, 'wide', inside)]
    ppermute x1, starting transfers between devices: 1.17 us -> 0.92 us  [body(): sums = lax.ppermute(pay, ('groups', 'wide'), across)]
  transfers between devices with their start and end apart: 5 -> 5, of which waited for: 2 -> 3; matrix products, arithmetic and copies ran while one was open for 0% -> 0% of each run, Pallas kernels for 7% -> 7%
where the time goes in v6:
time: 19.8 us; the launch traced here: 19.4 us
  starting transfers between devices  10.8 us (55%)
  Pallas kernels  4.63 us (23%)
  waiting for transfers between devices  3.3 us (17%)
  between operations  0.68 us (3%)
    all_to_all x1, starting transfers between devices, body(): lax.all_to_all(coeff, 'wide', split_axis=0, concat_axis=0, tiled=True, ax...  4.69 us
    pallas_call x7, Pallas kernels, call(): pl.pallas_call(kernel, out_shape=tuple((space(s, t) for space, (s, t) in...  4.63 us
    ppermute x1, starting transfers between devices, body(): back = lax.ppermute(f_a, 'wide', inside)  4.52 us
    ppermute x1, waiting for transfers between devices, body(): got = lax.ppermute(out_b, ('groups', 'wide'), across)  2.43 us
    ppermute x1, starting transfers between devices, body(): sums = lax.ppermute(pay, ('groups', 'wide'), across)  0.92 us
    ppermute x1, waiting for transfers between devices, body(): in_a = lax.ppermute(out_a, 'wide', inside)  0.56 us
  transfers between devices with their start and end apart: 5, of which 3 were waited for; matrix products, arithmetic and copies ran while one was open for 0% of the time, Pallas kernels for 7%

profile of v6, /device:TPU:19, one launch (start us, length us, event | category | flops | bytes accessed | tf_op | source)
XLA Modules:
  0.0 19.4 jit_solution(18422058271967863048)
XLA Ops:
  0.6 2.2 %send.1 = (f32[16,32,128]{2,1,0:T(8,128)}, f32[128,128]{1,0:T(8,128)S(1)}, f32[128,128]{1,0:T(8,128)S(1)}, f32[128,128]{1,0:T(8,128)S(1)}, bf16[256,384]{1,0:T(8...) custom-call(f32[256,128]{1,0:T(8,128)} %x_hbm.1, ...), custom_call_target="tpu_custom_call" | custom-call | tf_op jit(solution)/shard_map/send/pallas_call | solution.py:176
  2.9 4.7 %all-to-all-start = ((f32[16,32,128]{2,1,0:T(8,128)}), f32[16,32,128]{2,1,0:T(8,128)S(1)}, u32[]{:S(2)}, u32[]{:S(2)}) async-start(f32[16,32,128]{2,1,0:T(8,128)} %get-tuple-element.19), calls=%async_computation | async-start | bytes 524288 | tf_op jit(solution)/shard_map/all_to_all | solution.py:237
  7.6 0.4 %collective-permute-start = (f32[128,128]{1,0:T(8,128)S(1)}, f32[128,128]{1,0:T(8,128)S(1)}, u32[]{:S(2)}, u32[]{:S(2)}) collective-permute-start(f32[128,128]{1,0:T(8,128)S(1)} %get-tuple-element.25), channel_id=1, source_target_pairs={{0,1},{1,0},{2,3},{3,2},{4,5},{5,4},{6,7},{7,6},{8,9},{9,8},{10,11... | collective-permute-start | bytes 196616 | tf_op jit(solution)/shard_map/ppermute | solution.py:238
  7.9 0.3 %collective-permute-start.2 = (f32[128,128]{1,0:T(8,128)S(1)}, f32[128,128]{1,0:T(8,128)S(1)}, u32[]{:S(2)}, u32[]{:S(2)}) collective-permute-start(f32[128,128]{1,0:T(8,128)S(1)} %get-tuple-element.32.out_b_ref), channel_id=1, source_target_pairs={{1,2},{2,1},{3,4},{4,3},{5,6},{6,5},{7,8},{8,7},{9,10},{10,9},{11,... | collective-permute-start | bytes 196616 | tf_op jit(solution)/shard_map/ppermute | solution.py:239
  8.3 0.6 %collective-permute-done.a_ref = f32[128,128]{1,0:T(8,128)S(1)} collective-permute-done((f32[128,128]{1,0:T(8,128)S(1)}, f32[128,128]{1,0:T(8,128)S(1)}, u32[]{:S(2)}, u32[]{:S(2)}) %collective-permute-start) | collective-permute-done | bytes 65568 | tf_op jit(solution)/shard_map/ppermute | solution.py:238
  8.8 0.3 %across.1 = (f32[256,128]{1,0:T(8,128)S(1)}, f32[256,128]{1,0:T(8,128)S(1)}) custom-call(f32[128,128]{1,0:T(8,128)S(1)} %collective-permute-done.a_ref, f32[128,128]{1,0:T(8,128)S(1)} %get-tuple-element.26.m_ref, f32[384,384]{1,0:T(8,128)S(1)} %get-tuple-element.27.schur_ref), custom_call_target="tpu_custom_call" | custom-call | tf_op jit(solution)/shard_map/across/pallas_call | solution.py:176
  9.1 0.9 %collective-permute-start.1 = (f32[256,128]{1,0:T(8,128)S(1)}, f32[256,128]{1,0:T(8,128)S(1)}, u32[]{:S(2)}, u32[]{:S(2)}) collective-permute-start(f32[256,128]{1,0:T(8,128)S(1)} %get-tuple-element.31), channel_id=1, source_target_pairs={{1,2},{2,1},{3,4},{4,3},{5,6},{6,5},{7,8},{8,7},{9,10},{10,9},{11,... | collective-permute-start | bytes 393224 | tf_op jit(solution)/shard_map/ppermute | solution.py:243
  10.0 2.4 %collective-permute-done.2.got_ref = f32[128,128]{1,0:T(8,128)S(1)} collective-permute-done((f32[128,128]{1,0:T(8,128)S(1)}, f32[128,128]{1,0:T(8,128)S(1)}, u32[]{:S(2)}, u32[]{:S(2)}) %collective-permute-start.2) | collective-permute-done | bytes 65568 | tf_op jit(solution)/shard_map/ppermute | solution.py:239
  12.4 0.2 force.1
  12.6 4.5 %collective-permute-start.3 = (f32[128,128]{1,0:T(8,128)S(1)}, f32[128,128]{1,0:T(8,128)S(1)}, u32[]{:S(2)}, u32[]{:S(2)}) collective-permute-start(f32[128,128]{1,0:T(8,128)S(1)} %force.1), channel_id=1, source_target_pairs={{0,1},{1,0},{2,3},{3,2},{4,5},{5,4},{6,7},{7,6},{8,9},{9,8},{10,11... | collective-permute-start | bytes 196616 | tf_op jit(solution)/shard_map/ppermute | solution.py:248
  17.1 0.2 %base.1 = (f32[256,128]{1,0:T(8,128)S(1)}, bf16[256,512]{1,0:T(8,128)(2,1)S(1)}, bf16[256,512]{1,0:T(8,128)(2,1)S(1)}, f32[256,128]{1,0:T(8,128)S(1)}) custom-call(f32[256,128]{1,0:T(8,128)S(1)} %get-tuple-element.20.rhs_ref, f32[256,256]{1,0:T(8,128)S(1)} %get-tuple-element.21.near_ref, f32[256,128]{1,0:T(8,128)S(1)} %get-tuple-element.22.x_ref, ...), custom_call_target="tpu_custom_call" | custom-call | tf_op jit(solution)/shard_map/base/pallas_call | solution.py:176
  17.4 0.3 %own.1.base_ref = f32[256,128]{1,0:T(8,128)S(1)} custom-call(f32[128,128]{1,0:T(8,128)S(1)} %collective-permute-done.2.got_ref, f32[256,128]{1,0:T(8,128)S(1)} %get-tuple-element.28._.part_ref, f32[384,384]{1,0:T(8,128)S(1)} %get-tuple-element.27.schur_ref, bf16[256,384]{1,0:T(8,128)(2,1)S(1)} %get-tuple-element.33.sel_ref, ...), custom_call_target="tpu_custom_call" | custom-call | tf_op jit(solution)/shard_map/own/pallas_call | solution.py:176
  17.7 0.3 %collective-permute-done.3.back_ref = f32[128,128]{1,0:T(8,128)S(1)} collective-permute-done((f32[128,128]{1,0:T(8,128)S(1)}, f32[128,128]{1,0:T(8,128)S(1)}, u32[]{:S(2)}, u32[]{:S(2)}) %collective-permute-start.3) | collective-permute-done | bytes 65568 | tf_op jit(solution)/shard_map/ppermute | solution.py:248
  18.0 0.0 collective-permute-done.1.pay_ref
  18.0 0.4 %back.1.base_ref = f32[256,128]{1,0:T(8,128)S(1)} custom-call(f32[256,128]{1,0:T(8,128)S(1)} %collective-permute-done.1.pay_ref, f32[128,128]{1,0:T(8,128)S(1)} %get-tuple-element.32.out_b_ref, f32[128,128]{1,0:T(8,128)S(1)} %collective-permute-done.3.back_ref, bf16[256,384]{1,0:T(8,128)(2,1)S(1)} %get-tuple-element.33.sel_ref, f32[256,128]{1,0:T(8,128)S(1)} %own.1.base_ref), custom_call_target="tpu_custom_call" | custom-call | tf_op jit(solution)/shard_map/back/pallas_call | solution.py:176
  18.4 0.0 all-to-all-done
  18.4 1.0 %final.1 = (f32[256,128]{1,0:T(8,128)}, f32[256,128]{1,0:T(8,128)}) custom-call(f32[512,128]{1,0:T(8,128)S(1)} %bitcast.7, bf16[256,512]{1,0:T(8,128)(2,1)S(1)} %get-tuple-element.29.hi_ref, bf16[256,512]{1,0:T(8,128)(2,1)S(1)} %get-tuple-element.30.lo_ref, f32[256,128]{1,0:T(8,128)S(1)} %back.1.base_ref, f32[256,128]{1,0:T(8,128)S(1)} %get-tuple-element.22.x_ref, ...), custom_call_target="tpu_custom_call" | custom-call | tf_op jit(solution)/shard_map/final/pallas_call | solution.py:176
Async XLA Ops:
  2.9 15.5 %all-to-all-start = ((f32[16,32,128]{2,1,0:T(8,128)}), f32[16,32,128]{2,1,0:T(8,128)S(1)}, u32[]{:S(2)}, u32[]{:S(2)}) async-start(f32[16,32,128]{2,1,0:T(8,128)} %get-tuple-element.19), calls=%async_computation | async-start | bytes 524288 | tf_op jit(solution)/shard_map/all_to_all | solution.py:237
  7.6 1.3 %collective-permute-start = (f32[128,128]{1,0:T(8,128)S(1)}, f32[128,128]{1,0:T(8,128)S(1)}, u32[]{:S(2)}, u32[]{:S(2)}) collective-permute-start(f32[128,128]{1,0:T(8,128)S(1)} %get-tuple-element.25), channel_id=1, source_target_pairs={{0,1},{1,0},{2,3},{3,2},{4,5},{5,4},{6,7},{7,6},{8,9},{9,8},{10,11... | collective-permute-start | bytes 196616 | tf_op jit(solution)/shard_map/ppermute | solution.py:238
  7.9 4.5 %collective-permute-start.2 = (f32[128,128]{1,0:T(8,128)S(1)}, f32[128,128]{1,0:T(8,128)S(1)}, u32[]{:S(2)}, u32[]{:S(2)}) collective-permute-start(f32[128,128]{1,0:T(8,128)S(1)} %get-tuple-element.32.out_b_ref), channel_id=1, source_target_pairs={{1,2},{2,1},{3,4},{4,3},{5,6},{6,5},{7,8},{8,7},{9,10},{10,9},{11,... | collective-permute-start | bytes 196616 | tf_op jit(solution)/shard_map/ppermute | solution.py:239
  9.1 9.0 %collective-permute-start.1 = (f32[256,128]{1,0:T(8,128)S(1)}, f32[256,128]{1,0:T(8,128)S(1)}, u32[]{:S(2)}, u32[]{:S(2)}) collective-permute-start(f32[256,128]{1,0:T(8,128)S(1)} %get-tuple-element.31), channel_id=1, source_target_pairs={{1,2},{2,1},{3,4},{4,3},{5,6},{6,5},{7,8},{8,7},{9,10},{10,9},{11,... | collective-permute-start | bytes 393224 | tf_op jit(solution)/shard_map/ppermute | solution.py:243
  12.6 5.4 %collective-permute-start.3 = (f32[128,128]{1,0:T(8,128)S(1)}, f32[128,128]{1,0:T(8,128)S(1)}, u32[]{:S(2)}, u32[]{:S(2)}) collective-permute-start(f32[128,128]{1,0:T(8,128)S(1)} %force.1), channel_id=1, source_target_pairs={{0,1},{1,0},{2,3},{3,2},{4,5},{5,4},{6,7},{7,6},{8,9},{9,8},{10,11... | collective-permute-start | bytes 196616 | tf_op jit(solution)/shard_map/ppermute | solution.py:248

commit v7 on v6

--- a/solution.py
+++ b/solution.py
@@ -158,16 +158,16 @@
     next_ref[...] = base_ref[...] - fold(dot(sel_ref[:, face : 2 * face], wide_halves(own)))
 
 
-def back_kernel(pay_ref, out_b_ref, back_ref, sel_ref, base_ref, next_ref):
+def far_kernel(coeff_ref, hi_ref, lo_ref, base_ref, next_ref):
+    next_ref[...] = base_ref[...] - split_product(hi_ref[...], lo_ref[...], wide_halves(coeff_ref[...]))
+
+
+def final_kernel(pay_ref, out_b_ref, back_ref, sel_ref, base_ref, x_ref, scale_ref, up_ref, res_ref):
     face = back_ref.shape[0]
+    a = dot(sel_ref[:, :face], wide_halves(back_ref[...]))
     b = pay_ref[:face] + product(pay_ref[face:], wide_halves(out_b_ref[...]))
-    a = dot(sel_ref[:, :face], wide_halves(back_ref[...]))
     b = dot(sel_ref[:, 2 * face :], wide_halves(b))
-    next_ref[...] = base_ref[...] - fold(a + b)
-
-
-def final_kernel(coeff_ref, hi_ref, lo_ref, base_ref, x_ref, scale_ref, up_ref, res_ref):
-    res = base_ref[...] - split_product(hi_ref[...], lo_ref[...], wide_halves(coeff_ref[...]))
+    res = base_ref[...] - fold(a + b)
     res_ref[...] = res
     up_ref[...] = x_ref[...] + scale_ref[...] * res
 
@@ -247,12 +247,12 @@
     (f_a,) = call(force_kernel, "force", [block], (got, part, schur))
     back = lax.ppermute(f_a, "wide", inside)
     (base,) = call(own_kernel, "own", [field], (got, part, schur, sel, base))
-    (base,) = call(back_kernel, "back", [field], (sums, out_b, back, sel, base))
+    (base,) = call(far_kernel, "far", [field], (gathered.reshape(tiles * top, loads), u_hi, u_lo, base))
     return call(
         final_kernel,
         "final",
         [field, field],
-        (gathered.reshape(tiles * top, loads), u_hi, u_lo, base, x, scale),
+        (sums, out_b, back, sel, base, x, scale),
         spaces=[jax.ShapeDtypeStruct] * 2,
     )
 

time: 19.8 us -> 19.4 us (0.980)
  waiting for transfers between devices: 3.3 us -> 3 us
    ppermute x1, waiting for transfers between devices: 0.3 us -> 0.01 us  [body(): back = lax.ppermute(f_a, 'wide', inside)]
  transfers between devices with their start and end apart: 5 -> 5, of which waited for: 3 -> 2; matrix products, arithmetic and copies ran while one was open for 0% -> 0% of each run, Pallas kernels for 7% -> 7%
where the time goes in v7:
time: 19.4 us; the launch traced here: 19.2 us
  starting transfers between devices  10.8 us (56%)
  Pallas kernels  4.63 us (24%)
  waiting for transfers between devices  3 us (15%)
  between operations  0.7 us (4%)
    all_to_all x1, starting transfers between devices, body(): lax.all_to_all(coeff, 'wide', split_axis=0, concat_axis=0, tiled=True, ax...  4.69 us
    pallas_call x7, Pallas kernels, call(): pl.pallas_call(kernel, out_shape=tuple((space(s, t) for space, (s, t) in...  4.63 us
    ppermute x1, starting transfers between devices, body(): back = lax.ppermute(f_a, 'wide', inside)  4.52 us
    ppermute x1, waiting for transfers between devices, body(): got = lax.ppermute(out_b, ('groups', 'wide'), across)  2.43 us
    ppermute x1, starting transfers between devices, body(): sums = lax.ppermute(pay, ('groups', 'wide'), across)  0.92 us
    ppermute x1, waiting for transfers between devices, body(): in_a = lax.ppermute(out_a, 'wide', inside)  0.56 us
  transfers between devices with their start and end apart: 5, of which 2 were waited for; matrix products, arithmetic and copies ran while one was open for 0% of the time, Pallas kernels for 7%

profile of v7, /device:TPU:19, one launch (start us, length us, event | category | flops | bytes accessed | tf_op | source)
XLA Modules:
  0.0 19.2 jit_solution(12092955472483843711)
XLA Ops:
  0.6 2.2 %send.1 = (f32[16,32,128]{2,1,0:T(8,128)}, f32[128,128]{1,0:T(8,128)S(1)}, f32[128,128]{1,0:T(8,128)S(1)}, f32[128,128]{1,0:T(8,128)S(1)}, bf16[256,384]{1,0:T(8...) custom-call(f32[256,128]{1,0:T(8,128)} %x_hbm.1, ...), custom_call_target="tpu_custom_call" | custom-call | tf_op jit(solution)/shard_map/send/pallas_call | solution.py:176
  2.9 4.7 %all-to-all-start = ((f32[16,32,128]{2,1,0:T(8,128)}), f32[16,32,128]{2,1,0:T(8,128)S(1)}, u32[]{:S(2)}, u32[]{:S(2)}) async-start(f32[16,32,128]{2,1,0:T(8,128)} %get-tuple-element.26), calls=%async_computation | async-start | bytes 524288 | tf_op jit(solution)/shard_map/all_to_all | solution.py:237
  7.6 0.4 %collective-permute-start = (f32[128,128]{1,0:T(8,128)S(1)}, f32[128,128]{1,0:T(8,128)S(1)}, u32[]{:S(2)}, u32[]{:S(2)}) collective-permute-start(f32[128,128]{1,0:T(8,128)S(1)} %get-tuple-element.19), channel_id=1, source_target_pairs={{0,1},{1,0},{2,3},{3,2},{4,5},{5,4},{6,7},{7,6},{8,9},{9,8},{10,11... | collective-permute-start | bytes 196616 | tf_op jit(solution)/shard_map/ppermute | solution.py:238
  7.9 0.3 %collective-permute-start.2 = (f32[128,128]{1,0:T(8,128)S(1)}, f32[128,128]{1,0:T(8,128)S(1)}, u32[]{:S(2)}, u32[]{:S(2)}) collective-permute-start(f32[128,128]{1,0:T(8,128)S(1)} %get-tuple-element.23.out_b_ref), channel_id=1, source_target_pairs={{1,2},{2,1},{3,4},{4,3},{5,6},{6,5},{7,8},{8,7},{9,10},{10,9},{11,... | collective-permute-start | bytes 196616 | tf_op jit(solution)/shard_map/ppermute | solution.py:239
  8.3 0.6 %collective-permute-done.a_ref = f32[128,128]{1,0:T(8,128)S(1)} collective-permute-done((f32[128,128]{1,0:T(8,128)S(1)}, f32[128,128]{1,0:T(8,128)S(1)}, u32[]{:S(2)}, u32[]{:S(2)}) %collective-permute-start) | collective-permute-done | bytes 65568 | tf_op jit(solution)/shard_map/ppermute | solution.py:238
  8.8 0.3 %across.1 = (f32[256,128]{1,0:T(8,128)S(1)}, f32[256,128]{1,0:T(8,128)S(1)}) custom-call(f32[128,128]{1,0:T(8,128)S(1)} %collective-permute-done.a_ref, f32[128,128]{1,0:T(8,128)S(1)} %get-tuple-element.20.m_ref, f32[384,384]{1,0:T(8,128)S(1)} %get-tuple-element.21.schur_ref), custom_call_target="tpu_custom_call" | custom-call | tf_op jit(solution)/shard_map/across/pallas_call | solution.py:176
  9.1 0.9 %collective-permute-start.1 = (f32[256,128]{1,0:T(8,128)S(1)}, f32[256,128]{1,0:T(8,128)S(1)}, u32[]{:S(2)}, u32[]{:S(2)}) collective-permute-start(f32[256,128]{1,0:T(8,128)S(1)} %get-tuple-element.22), channel_id=1, source_target_pairs={{1,2},{2,1},{3,4},{4,3},{5,6},{6,5},{7,8},{8,7},{9,10},{10,9},{11,... | collective-permute-start | bytes 393224 | tf_op jit(solution)/shard_map/ppermute | solution.py:243
  10.0 2.4 %collective-permute-done.2.got_ref = f32[128,128]{1,0:T(8,128)S(1)} collective-permute-done((f32[128,128]{1,0:T(8,128)S(1)}, f32[128,128]{1,0:T(8,128)S(1)}, u32[]{:S(2)}, u32[]{:S(2)}) %collective-permute-start.2) | collective-permute-done | bytes 65568 | tf_op jit(solution)/shard_map/ppermute | solution.py:239
  12.4 0.2 force.1
  12.6 4.5 %collective-permute-start.3 = (f32[128,128]{1,0:T(8,128)S(1)}, f32[128,128]{1,0:T(8,128)S(1)}, u32[]{:S(2)}, u32[]{:S(2)}) collective-permute-start(f32[128,128]{1,0:T(8,128)S(1)} %force.1), channel_id=1, source_target_pairs={{0,1},{1,0},{2,3},{3,2},{4,5},{5,4},{6,7},{7,6},{8,9},{9,8},{10,11... | collective-permute-start | bytes 196616 | tf_op jit(solution)/shard_map/ppermute | solution.py:248
  17.1 0.2 %base.1 = (f32[256,128]{1,0:T(8,128)S(1)}, bf16[256,512]{1,0:T(8,128)(2,1)S(1)}, bf16[256,512]{1,0:T(8,128)(2,1)S(1)}, f32[256,128]{1,0:T(8,128)S(1)}) custom-call(f32[256,128]{1,0:T(8,128)S(1)} %get-tuple-element.27.rhs_ref, f32[256,256]{1,0:T(8,128)S(1)} %get-tuple-element.28.near_ref, f32[256,128]{1,0:T(8,128)S(1)} %get-tuple-element.29.x_ref, ...), custom_call_target="tpu_custom_call" | custom-call | tf_op jit(solution)/shard_map/base/pallas_call | solution.py:176
  17.4 0.3 %own.1.base_ref = f32[256,128]{1,0:T(8,128)S(1)} custom-call(f32[128,128]{1,0:T(8,128)S(1)} %collective-permute-done.2.got_ref, f32[256,128]{1,0:T(8,128)S(1)} %get-tuple-element.24.part_ref._, f32[384,384]{1,0:T(8,128)S(1)} %get-tuple-element.21.schur_ref, bf16[256,384]{1,0:T(8,128)(2,1)S(1)} %get-tuple-element.25.sel_ref, ...), custom_call_target="tpu_custom_call" | custom-call | tf_op jit(solution)/shard_map/own/pallas_call | solution.py:176
  17.7 0.0 all-to-all-done
  17.7 0.3 %far.1.base_ref = f32[256,128]{1,0:T(8,128)S(1)} custom-call(f32[512,128]{1,0:T(8,128)S(1)} %bitcast.7, bf16[256,512]{1,0:T(8,128)(2,1)S(1)} %get-tuple-element.32.hi_ref, bf16[256,512]{1,0:T(8,128)(2,1)S(1)} %get-tuple-element.33.lo_ref, f32[256,128]{1,0:T(8,128)S(1)} %own.1.base_ref), custom_call_target="tpu_custom_call" | custom-call | tf_op jit(solution)/shard_map/far/pallas_call | solution.py:176
  18.0 0.0 collective-permute-done.3.back_ref
  18.1 0.0 collective-permute-done.1.pay_ref
  18.1 1.1 %final.1 = (f32[256,128]{1,0:T(8,128)}, f32[256,128]{1,0:T(8,128)}) custom-call(f32[256,128]{1,0:T(8,128)S(1)} %collective-permute-done.1.pay_ref, f32[128,128]{1,0:T(8,128)S(1)} %get-tuple-element.23.out_b_ref, f32[128,128]{1,0:T(8,128)S(1)} %collective-permute-done.3.back_ref, bf16[256,384]{1,0:T(8,128)(2,1)S(1)} %get-tuple-element.25.sel_ref, ...), custom_call_target="tpu_custom_call" | custom-call | tf_op jit(solution)/shard_map/final/pallas_call | solution.py:176
Async XLA Ops:
  2.9 14.9 %all-to-all-start = ((f32[16,32,128]{2,1,0:T(8,128)}), f32[16,32,128]{2,1,0:T(8,128)S(1)}, u32[]{:S(2)}, u32[]{:S(2)}) async-start(f32[16,32,128]{2,1,0:T(8,128)} %get-tuple-element.26), calls=%async_computation | async-start | bytes 524288 | tf_op jit(solution)/shard_map/all_to_all | solution.py:237
  7.6 1.3 %collective-permute-start = (f32[128,128]{1,0:T(8,128)S(1)}, f32[128,128]{1,0:T(8,128)S(1)}, u32[]{:S(2)}, u32[]{:S(2)}) collective-permute-start(f32[128,128]{1,0:T(8,128)S(1)} %get-tuple-element.19), channel_id=1, source_target_pairs={{0,1},{1,0},{2,3},{3,2},{4,5},{5,4},{6,7},{7,6},{8,9},{9,8},{10,11... | collective-permute-start | bytes 196616 | tf_op jit(solution)/shard_map/ppermute | solution.py:238
  7.9 4.5 %collective-permute-start.2 = (f32[128,128]{1,0:T(8,128)S(1)}, f32[128,128]{1,0:T(8,128)S(1)}, u32[]{:S(2)}, u32[]{:S(2)}) collective-permute-start(f32[128,128]{1,0:T(8,128)S(1)} %get-tuple-element.23.out_b_ref), channel_id=1, source_target_pairs={{1,2},{2,1},{3,4},{4,3},{5,6},{6,5},{7,8},{8,7},{9,10},{10,9},{11,... | collective-permute-start | bytes 196616 | tf_op jit(solution)/shard_map/ppermute | solution.py:239
  9.1 9.0 %collective-permute-start.1 = (f32[256,128]{1,0:T(8,128)S(1)}, f32[256,128]{1,0:T(8,128)S(1)}, u32[]{:S(2)}, u32[]{:S(2)}) collective-permute-start(f32[256,128]{1,0:T(8,128)S(1)} %get-tuple-element.22), channel_id=1, source_target_pairs={{1,2},{2,1},{3,4},{4,3},{5,6},{6,5},{7,8},{8,7},{9,10},{10,9},{11,... | collective-permute-start | bytes 393224 | tf_op jit(solution)/shard_map/ppermute | solution.py:243
  12.6 5.4 %collective-permute-start.3 = (f32[128,128]{1,0:T(8,128)S(1)}, f32[128,128]{1,0:T(8,128)S(1)}, u32[]{:S(2)}, u32[]{:S(2)}) collective-permute-start(f32[128,128]{1,0:T(8,128)S(1)} %force.1), channel_id=1, source_target_pairs={{0,1},{1,0},{2,3},{3,2},{4,5},{5,4},{6,7},{7,6},{8,9},{9,8},{10,11... | collective-permute-start | bytes 196616 | tf_op jit(solution)/shard_map/ppermute | solution.py:248

commit v8 on v7

--- a/solution.py
+++ b/solution.py
@@ -45,16 +45,11 @@
     return lax.axis_index("wide") % 2 == 1
 
 
-def lead(size):
+def group_order(size):
     pairs = size // 2
-    return (2 * (pairs // 2 + math.isqrt(pairs) // 2) + 1) % size
-
-
-def turned(hbm, ref, by):
-    rest = hbm.shape[0] - by
-    if by == 0:
-        return [(hbm, ref)]
-    return [(hbm.at[pl.ds(by, rest)], ref.at[pl.ds(0, rest)]), (hbm.at[pl.ds(0, by)], ref.at[pl.ds(rest, by)])]
+    first = 2 * (pairs // 2 + math.isqrt(pairs) // 2) + 1
+    stride = 5 if math.gcd(5, size) == 1 else 1
+    return [(first + stride * i) % size for i in range(size)]
 
 
 def tiles_at_once(tiles, top):
@@ -67,11 +62,10 @@
     n_rows, loads = x_ref.shape
     face = rows_ref.shape[2]
     tiles, top, _ = v_ref.shape
-    first = lead(tiles)
-    early = [(x_hbm, x_ref), (rank_hbm, rank_ref)] + turned(v_hbm, v_ref, first)
+    order = group_order(tiles)
+    early = [(x_hbm, x_ref), (rank_hbm, rank_ref), (v_hbm, v_ref)]
     middle = [(rows_hbm, rows_ref), (count_hbm, count_ref)]
-    late = [(schur_hbm, schur_ref)] + turned(u_hbm, u_ref, first * top)
-    late += [(near_hbm, near_ref), (rhs_hbm, rhs_ref), (p_hbm, p_ref)]
+    late = [(schur_hbm, schur_ref), (u_hbm, u_ref), (near_hbm, near_ref), (rhs_hbm, rhs_ref), (p_hbm, p_ref)]
     moves = [pltpu.make_async_copy(src, dst, sems.at[i]) for i, (src, dst) in enumerate(early + middle + late)]
     for move in moves:
         move.start()
@@ -87,11 +81,11 @@
         return pltpu.make_async_copy(coeff_ref.at[span], coeff_hbm.at[span], out_sems.at[s])
 
     for s in range(tiles // step):
-        part = v_ref[s * step : (s + 1) * step].reshape(step * top, n_rows)
+        chosen = order[s * step : (s + 1) * step]
+        part = jnp.concatenate([v_ref[tile] for tile in chosen], axis=0)
         out = product(part, x_wide).reshape(step, top, loads)
-        for t in range(step):
-            at = s * step + t
-            coeff_ref[at] = jnp.where(k < rank_ref[(at + first) % tiles], out[t], 0.0)
+        for t, tile in enumerate(chosen):
+            coeff_ref[s * step + t] = jnp.where(k < rank_ref[tile], out[t], 0.0)
         out_move(s).start()
     for move in moves[len(early) : -len(late)]:
         move.wait()
@@ -139,7 +133,9 @@
 def base_kernel(rhs_ref, near_ref, x_ref, u_ref, p_ref, _, base_ref, hi_ref, lo_ref, scale_ref):
     n_rows, loads = x_ref.shape
     base_ref[...] = rhs_ref[...] - product(near_ref[...], wide_halves(x_ref[...]))
-    hi_ref[...], lo_ref[...] = halves(u_ref[...].T)
+    tiles, top, _ = u_ref.shape
+    u = jnp.concatenate([u_ref[tile] for tile in group_order(tiles)], axis=0)
+    hi_ref[...], lo_ref[...] = halves(u.T)
     scale_ref[...] = jnp.broadcast_to(p_ref[...], (loads, n_rows)).T
 
 
@@ -208,7 +204,7 @@
         send_count.reshape(3),
         tile_rank.reshape(tiles),
         schur,
-        u_basis.reshape(tiles * top, n_rows),
+        u_basis,
         near_block,
         rhs,
         precond.reshape(1, n_rows),
@@ -228,13 +224,14 @@
             pltpu.SMEM((3,), jnp.int32),
             pltpu.SMEM((tiles,), jnp.int32),
             pltpu.VMEM((tiles, top, loads), f32),
-            pltpu.SemaphoreType.DMA((len(arrays) + 2,)),
+            pltpu.SemaphoreType.DMA((len(arrays),)),
             pltpu.SemaphoreType.DMA((steps,)),
         ],
         [pltpu.HBM] + [pltpu.VMEM] * 10,
     )
-    order = [(i + lead(size)) % size for i in range(size)]
-    gathered = lax.all_to_all(coeff, "wide", split_axis=0, concat_axis=0, tiled=True, axis_index_groups=[order])
+    gathered = lax.all_to_all(
+        coeff, "wide", split_axis=0, concat_axis=0, tiled=True, axis_index_groups=[group_order(size)]
+    )
     in_a = lax.ppermute(out_a, "wide", inside)
     got = lax.ppermute(out_b, ("groups", "wide"), across)
     pay, part = call(

time: 19.4 us -> 19.3 us (level)
  no operation moved by 1% of the time
where the time goes in v8:
time: 19.3 us; the launch traced here: 19.1 us
  starting transfers between devices  10.7 us (55%)
  Pallas kernels  4.59 us (24%)
  waiting for transfers between devices  3.1 us (16%)
  between operations  0.7 us (4%)
    all_to_all x1, starting transfers between devices, body(): lax.all_to_all(coeff, 'wide', split_axis=0, concat_axis=0, tiled=True, ax...  4.61 us
    pallas_call x7, Pallas kernels, call(): pl.pallas_call(kernel, out_shape=tuple((space(s, t) for space, (s, t) in...  4.59 us
    ppermute x1, starting transfers between devices, body(): back = lax.ppermute(f_a, 'wide', inside)  4.39 us
    ppermute x1, waiting for transfers between devices, body(): got = lax.ppermute(out_b, ('groups', 'wide'), across)  2.54 us
    ppermute x1, starting transfers between devices, body(): sums = lax.ppermute(pay, ('groups', 'wide'), across)  0.91 us
    ppermute x1, waiting for transfers between devices, body(): in_a = lax.ppermute(out_a, 'wide', inside)  0.54 us
    ppermute x1, starting transfers between devices, body(): in_a = lax.ppermute(out_a, 'wide', inside)  0.43 us
  transfers between devices with their start and end apart: 5, of which 2 were waited for; matrix products, arithmetic and copies ran while one was open for 0% of the time, Pallas kernels for 7%

profile of v8, /device:TPU:19, one launch (start us, length us, event | category | flops | bytes accessed | tf_op | source)
XLA Modules:
  0.0 19.1 jit_solution(1132850423251368017)
XLA Ops:
  0.6 2.2 %send.1 = (f32[16,32,128]{2,1,0:T(8,128)}, f32[128,128]{1,0:T(8,128)S(1)}, f32[128,128]{1,0:T(8,128)S(1)}, f32[128,128]{1,0:T(8,128)S(1)}, bf16[256,384]{1,0:T(8...) custom-call(f32[256,128]{1,0:T(8,128)} %x_hbm.1, ...), custom_call_target="tpu_custom_call" | custom-call | tf_op jit(solution)/shard_map/send/pallas_call | solution.py:172
  2.8 4.6 %all-to-all-start = ((f32[16,32,128]{2,1,0:T(8,128)}), f32[16,32,128]{2,1,0:T(8,128)S(1)}, u32[]{:S(2)}, u32[]{:S(2)}) async-start(f32[16,32,128]{2,1,0:T(8,128)} %get-tuple-element.26), calls=%async_computation | async-start | bytes 524288 | tf_op jit(solution)/shard_map/all_to_all | solution.py:232
  7.4 0.4 %collective-permute-start = (f32[128,128]{1,0:T(8,128)S(1)}, f32[128,128]{1,0:T(8,128)S(1)}, u32[]{:S(2)}, u32[]{:S(2)}) collective-permute-start(f32[128,128]{1,0:T(8,128)S(1)} %get-tuple-element.19), channel_id=1, source_target_pairs={{0,1},{1,0},{2,3},{3,2},{4,5},{5,4},{6,7},{7,6},{8,9},{9,8},{10,11... | collective-permute-start | bytes 196616 | tf_op jit(solution)/shard_map/ppermute | solution.py:235
  7.9 0.4 %collective-permute-start.2 = (f32[128,128]{1,0:T(8,128)S(1)}, f32[128,128]{1,0:T(8,128)S(1)}, u32[]{:S(2)}, u32[]{:S(2)}) collective-permute-start(f32[128,128]{1,0:T(8,128)S(1)} %get-tuple-element.23.out_b_ref), channel_id=1, source_target_pairs={{1,2},{2,1},{3,4},{4,3},{5,6},{6,5},{7,8},{8,7},{9,10},{10,9},{11,... | collective-permute-start | bytes 196616 | tf_op jit(solution)/shard_map/ppermute | solution.py:236
  8.2 0.5 %collective-permute-done.a_ref = f32[128,128]{1,0:T(8,128)S(1)} collective-permute-done((f32[128,128]{1,0:T(8,128)S(1)}, f32[128,128]{1,0:T(8,128)S(1)}, u32[]{:S(2)}, u32[]{:S(2)}) %collective-permute-start) | collective-permute-done | bytes 65568 | tf_op jit(solution)/shard_map/ppermute | solution.py:235
  8.8 0.3 %across.1 = (f32[256,128]{1,0:T(8,128)S(1)}, f32[256,128]{1,0:T(8,128)S(1)}) custom-call(f32[128,128]{1,0:T(8,128)S(1)} %collective-permute-done.a_ref, f32[128,128]{1,0:T(8,128)S(1)} %get-tuple-element.20.m_ref, f32[384,384]{1,0:T(8,128)S(1)} %get-tuple-element.21.schur_ref), custom_call_target="tpu_custom_call" | custom-call | tf_op jit(solution)/shard_map/across/pallas_call | solution.py:172
  9.0 0.9 %collective-permute-start.1 = (f32[256,128]{1,0:T(8,128)S(1)}, f32[256,128]{1,0:T(8,128)S(1)}, u32[]{:S(2)}, u32[]{:S(2)}) collective-permute-start(f32[256,128]{1,0:T(8,128)S(1)} %get-tuple-element.22), channel_id=1, source_target_pairs={{1,2},{2,1},{3,4},{4,3},{5,6},{6,5},{7,8},{8,7},{9,10},{10,9},{11,... | collective-permute-start | bytes 393224 | tf_op jit(solution)/shard_map/ppermute | solution.py:240
  9.9 2.5 %collective-permute-done.2.got_ref = f32[128,128]{1,0:T(8,128)S(1)} collective-permute-done((f32[128,128]{1,0:T(8,128)S(1)}, f32[128,128]{1,0:T(8,128)S(1)}, u32[]{:S(2)}, u32[]{:S(2)}) %collective-permute-start.2) | collective-permute-done | bytes 65568 | tf_op jit(solution)/shard_map/ppermute | solution.py:236
  12.5 0.2 force.1
  12.7 4.4 %collective-permute-start.3 = (f32[128,128]{1,0:T(8,128)S(1)}, f32[128,128]{1,0:T(8,128)S(1)}, u32[]{:S(2)}, u32[]{:S(2)}) collective-permute-start(f32[128,128]{1,0:T(8,128)S(1)} %force.1), channel_id=1, source_target_pairs={{0,1},{1,0},{2,3},{3,2},{4,5},{5,4},{6,7},{7,6},{8,9},{9,8},{10,11... | collective-permute-start | bytes 196616 | tf_op jit(solution)/shard_map/ppermute | solution.py:245
  17.1 0.2 %base.1 = (f32[256,128]{1,0:T(8,128)S(1)}, bf16[256,512]{1,0:T(8,128)(2,1)S(1)}, bf16[256,512]{1,0:T(8,128)(2,1)S(1)}, f32[256,128]{1,0:T(8,128)S(1)}) custom-call(f32[256,128]{1,0:T(8,128)S(1)} %get-tuple-element.27.rhs_ref, f32[256,256]{1,0:T(8,128)S(1)} %get-tuple-element.28.near_ref, f32[256,128]{1,0:T(8,128)S(1)} %get-tuple-element.29.x_ref, ...), custom_call_target="tpu_custom_call" | custom-call | tf_op jit(solution)/shard_map/base/pallas_call | solution.py:172
  17.3 0.3 %own.1.base_ref = f32[256,128]{1,0:T(8,128)S(1)} custom-call(f32[128,128]{1,0:T(8,128)S(1)} %collective-permute-done.2.got_ref, f32[256,128]{1,0:T(8,128)S(1)} %get-tuple-element.24.part_ref._, f32[384,384]{1,0:T(8,128)S(1)} %get-tuple-element.21.schur_ref, bf16[256,384]{1,0:T(8,128)(2,1)S(1)} %get-tuple-element.25.sel_ref, ...), custom_call_target="tpu_custom_call" | custom-call | tf_op jit(solution)/shard_map/own/pallas_call | solution.py:172
  17.7 0.0 all-to-all-done
  17.7 0.3 %far.1.base_ref = f32[256,128]{1,0:T(8,128)S(1)} custom-call(f32[512,128]{1,0:T(8,128)S(1)} %bitcast.6, bf16[256,512]{1,0:T(8,128)(2,1)S(1)} %get-tuple-element.32.hi_ref, bf16[256,512]{1,0:T(8,128)(2,1)S(1)} %get-tuple-element.33.lo_ref, f32[256,128]{1,0:T(8,128)S(1)} %own.1.base_ref), custom_call_target="tpu_custom_call" | custom-call | tf_op jit(solution)/shard_map/far/pallas_call | solution.py:172
  18.0 0.0 collective-permute-done.3.back_ref
  18.0 0.0 collective-permute-done.1.pay_ref
  18.0 1.1 %final.1 = (f32[256,128]{1,0:T(8,128)}, f32[256,128]{1,0:T(8,128)}) custom-call(f32[256,128]{1,0:T(8,128)S(1)} %collective-permute-done.1.pay_ref, f32[128,128]{1,0:T(8,128)S(1)} %get-tuple-element.23.out_b_ref, f32[128,128]{1,0:T(8,128)S(1)} %collective-permute-done.3.back_ref, bf16[256,384]{1,0:T(8,128)(2,1)S(1)} %get-tuple-element.25.sel_ref, ...), custom_call_target="tpu_custom_call" | custom-call | tf_op jit(solution)/shard_map/final/pallas_call | solution.py:172
Async XLA Ops:
  2.8 14.8 %all-to-all-start = ((f32[16,32,128]{2,1,0:T(8,128)}), f32[16,32,128]{2,1,0:T(8,128)S(1)}, u32[]{:S(2)}, u32[]{:S(2)}) async-start(f32[16,32,128]{2,1,0:T(8,128)} %get-tuple-element.26), calls=%async_computation | async-start | bytes 524288 | tf_op jit(solution)/shard_map/all_to_all | solution.py:232
  7.4 1.3 %collective-permute-start = (f32[128,128]{1,0:T(8,128)S(1)}, f32[128,128]{1,0:T(8,128)S(1)}, u32[]{:S(2)}, u32[]{:S(2)}) collective-permute-start(f32[128,128]{1,0:T(8,128)S(1)} %get-tuple-element.19), channel_id=1, source_target_pairs={{0,1},{1,0},{2,3},{3,2},{4,5},{5,4},{6,7},{7,6},{8,9},{9,8},{10,11... | collective-permute-start | bytes 196616 | tf_op jit(solution)/shard_map/ppermute | solution.py:235
  7.9 4.6 %collective-permute-start.2 = (f32[128,128]{1,0:T(8,128)S(1)}, f32[128,128]{1,0:T(8,128)S(1)}, u32[]{:S(2)}, u32[]{:S(2)}) collective-permute-start(f32[128,128]{1,0:T(8,128)S(1)} %get-tuple-element.23.out_b_ref), channel_id=1, source_target_pairs={{1,2},{2,1},{3,4},{4,3},{5,6},{6,5},{7,8},{8,7},{9,10},{10,9},{11,... | collective-permute-start | bytes 196616 | tf_op jit(solution)/shard_map/ppermute | solution.py:236
  9.0 9.0 %collective-permute-start.1 = (f32[256,128]{1,0:T(8,128)S(1)}, f32[256,128]{1,0:T(8,128)S(1)}, u32[]{:S(2)}, u32[]{:S(2)}) collective-permute-start(f32[256,128]{1,0:T(8,128)S(1)} %get-tuple-element.22), channel_id=1, source_target_pairs={{1,2},{2,1},{3,4},{4,3},{5,6},{6,5},{7,8},{8,7},{9,10},{10,9},{11,... | collective-permute-start | bytes 393224 | tf_op jit(solution)/shard_map/ppermute | solution.py:240
  12.7 5.3 %collective-permute-start.3 = (f32[128,128]{1,0:T(8,128)S(1)}, f32[128,128]{1,0:T(8,128)S(1)}, u32[]{:S(2)}, u32[]{:S(2)}) collective-permute-start(f32[128,128]{1,0:T(8,128)S(1)} %force.1), channel_id=1, source_target_pairs={{0,1},{1,0},{2,3},{3,2},{4,5},{5,4},{6,7},{7,6},{8,9},{9,8},{10,11... | collective-permute-start | bytes 196616 | tf_op jit(solution)/shard_map/ppermute | solution.py:245

commit v9 on v8

--- a/solution.py
+++ b/solution.py
@@ -57,7 +57,7 @@
 
 
 def send_kernel(x_hbm, v_hbm, rows_hbm, count_hbm, rank_hbm, schur_hbm, u_hbm, near_hbm, rhs_hbm, p_hbm,
-                coeff_hbm, a_ref, m_ref, b_ref, sel_ref, x_ref, schur_ref, u_ref, near_ref, rhs_ref, p_ref,
+                coeff_hbm, a_ref, m_ref, b_ref, corner_ref, sel_ref, x_ref, schur_ref, u_ref, near_ref, rhs_ref, p_ref,
                 v_ref, rows_ref, count_ref, rank_ref, coeff_ref, sems, out_sems):
     n_rows, loads = x_ref.shape
     face = rows_ref.shape[2]
@@ -104,6 +104,8 @@
         out_move(s).wait()
     for move in moves[-len(late) :]:
         move.wait()
+    last = pl.ds(place(odd, 2, face), face)
+    corner_ref[...] = schur_ref[last, last]
 
 
 def place(odd, spot, face):
@@ -115,9 +117,7 @@
 def across_kernel(a_ref, m_ref, schur_ref, pay_ref, part_ref):
     odd = is_odd()
     face = a_ref.shape[0]
-    last = pl.ds(place(odd, 2, face), face)
     known = jnp.concatenate([wide_halves(a_ref[...]), wide_halves(m_ref[...])], axis=0)
-    pay_ref[face:] = schur_ref[last, last]
     for spot in (2, 0, 1):
         rows = pl.ds(place(odd, spot, face), face)
         block = jnp.concatenate(
@@ -125,7 +125,7 @@
         )
         out = product(block, known)
         if spot == 2:
-            pay_ref[:face] = out
+            pay_ref[...] = out
         else:
             part_ref[spot * face : (spot + 1) * face] = out
 
@@ -146,23 +146,24 @@
     fa_ref[...] = part_ref[:face] + product(block, wide_halves(got_ref[...]))
 
 
-def own_kernel(got_ref, part_ref, schur_ref, sel_ref, base_ref, next_ref):
+def own_kernel(got_ref, corner_ref, out_b_ref, part_ref, schur_ref, sel_ref, base_ref, next_ref):
     odd = is_odd()
     face = got_ref.shape[0]
     block = schur_ref[face : 2 * face, pl.ds(place(odd, 2, face), face)]
     own = part_ref[face:] + product(block, wide_halves(got_ref[...]))
-    next_ref[...] = base_ref[...] - fold(dot(sel_ref[:, face : 2 * face], wide_halves(own)))
+    back = product(corner_ref[...], wide_halves(out_b_ref[...]))
+    both = jnp.concatenate([wide_halves(own), wide_halves(back)], axis=0)
+    next_ref[...] = base_ref[...] - fold(dot(sel_ref[:, face:], both))
 
 
 def far_kernel(coeff_ref, hi_ref, lo_ref, base_ref, next_ref):
     next_ref[...] = base_ref[...] - split_product(hi_ref[...], lo_ref[...], wide_halves(coeff_ref[...]))
 
 
-def final_kernel(pay_ref, out_b_ref, back_ref, sel_ref, base_ref, x_ref, scale_ref, up_ref, res_ref):
+def final_kernel(sum_ref, back_ref, sel_ref, base_ref, x_ref, scale_ref, up_ref, res_ref):
     face = back_ref.shape[0]
     a = dot(sel_ref[:, :face], wide_halves(back_ref[...]))
-    b = pay_ref[:face] + product(pay_ref[face:], wide_halves(out_b_ref[...]))
-    b = dot(sel_ref[:, 2 * face :], wide_halves(b))
+    b = dot(sel_ref[:, 2 * face :], wide_halves(sum_ref[...]))
     res = base_ref[...] - fold(a + b)
     res_ref[...] = res
     up_ref[...] = x_ref[...] + scale_ref[...] * res
@@ -210,14 +211,14 @@
         precond.reshape(1, n_rows),
     )
     square = lambda a: (a.shape, a.dtype)
-    coeff, out_a, out_m, out_b, sel, x, schur, u, near, rhs, p = call(
+    coeff, out_a, out_m, out_b, corner, sel, x, schur, u, near, rhs, p = call(
         send_kernel,
         "send",
-        [((tiles, top, loads), f32), block, block, block, ((n_rows, 3 * face), bf16), field]
+        [((tiles, top, loads), f32), block, block, block, ((face, face), f32), ((n_rows, 3 * face), bf16), field]
         + [square(arrays[i]) for i in (5, 6, 7, 8, 9)],
         [pltpu.with_memory_space_constraint(a, pltpu.HBM) for a in arrays],
         [HBM] * len(arrays),
-        [HBM] + [VMEM] * 10,
+        [HBM] + [VMEM] * 11,
         [
             pltpu.VMEM((tiles, top, n_rows), f32),
             pltpu.VMEM((3, 1, face), jnp.int32),
@@ -227,29 +228,28 @@
             pltpu.SemaphoreType.DMA((len(arrays),)),
             pltpu.SemaphoreType.DMA((steps,)),
         ],
-        [pltpu.HBM] + [pltpu.VMEM] * 10,
+        [pltpu.HBM] + [pltpu.VMEM] * 11,
     )
     gathered = lax.all_to_all(
         coeff, "wide", split_axis=0, concat_axis=0, tiled=True, axis_index_groups=[group_order(size)]
     )
     in_a = lax.ppermute(out_a, "wide", inside)
     got = lax.ppermute(out_b, ("groups", "wide"), across)
-    pay, part = call(
-        across_kernel, "across", [((2 * face, loads), f32)] * 2, (in_a, out_m, schur)
-    )
+    corner = lax.ppermute(corner, ("groups", "wide"), across)
+    pay, part = call(across_kernel, "across", [block, ((2 * face, loads), f32)], (in_a, out_m, schur))
     sums = lax.ppermute(pay, ("groups", "wide"), across)
     base, u_hi, u_lo, scale = call(
         base_kernel, "base", [field, factor, factor, field], (rhs, near, x, u, p, part)
     )
     (f_a,) = call(force_kernel, "force", [block], (got, part, schur))
     back = lax.ppermute(f_a, "wide", inside)
-    (base,) = call(own_kernel, "own", [field], (got, part, schur, sel, base))
+    (base,) = call(own_kernel, "own", [field], (got, corner, out_b, part, schur, sel, base))
     (base,) = call(far_kernel, "far", [field], (gathered.reshape(tiles * top, loads), u_hi, u_lo, base))
     return call(
         final_kernel,
         "final",
         [field, field],
-        (sums, out_b, back, sel, base, x, scale),
+        (sums, back, sel, base, x, scale),
         spaces=[jax.ShapeDtypeStruct] * 2,
     )
 

time: 19.3 us -> 19.2 us (level)
  starting transfers between devices: 10.7 us -> 11.6 us
  waiting for transfers between devices: 3.1 us -> 2.2 us
    ppermute x0 -> x1, starting transfers between devices: none -> 1.39 us  [body(): corner = lax.ppermute(corner, ('groups', 'wide'), across)]
    ppermute x1, waiting for transfers between devices: 0.54 us -> 0.01 us  [body(): in_a = lax.ppermute(out_a, 'wide', inside)]
    ppermute x1, starting transfers between devices: 0.91 us -> 0.42 us  [body(): sums = lax.ppermute(pay, ('groups', 'wide'), across)]
    ppermute x1, waiting for transfers between devices: 2.54 us -> 2.19 us  [body(): got = lax.ppermute(out_b, ('groups', 'wide'), across)]
  transfers between devices with their start and end apart: 5 -> 6, of which waited for: 2 -> 1; matrix products, arithmetic and copies ran while one was open for 0% -> 0% of each run, Pallas kernels for 7% -> 7%
where the time goes in v9:
time: 19.2 us; the launch traced here: 19 us
  starting transfers between devices  11.6 us (60%)
  Pallas kernels  4.46 us (23%)
  waiting for transfers between devices  2.2 us (11%)
  between operations  0.7 us (4%)
    all_to_all x1, starting transfers between devices, body(): lax.all_to_all(coeff, 'wide', split_axis=0, concat_axis=0, tiled=True, ax...  4.61 us
    pallas_call x7, Pallas kernels, call(): pl.pallas_call(kernel, out_shape=tuple((space(s, t) for space, (s, t) in...  4.46 us
    ppermute x1, starting transfers between devices, body(): back = lax.ppermute(f_a, 'wide', inside)  4.39 us
    ppermute x1, waiting for transfers between devices, body(): got = lax.ppermute(out_b, ('groups', 'wide'), across)  2.19 us
    ppermute x1, starting transfers between devices, body(): corner = lax.ppermute(corner, ('groups', 'wide'), across)  1.39 us
    ppermute x1, starting transfers between devices, body(): in_a = lax.ppermute(out_a, 'wide', inside)  0.43 us
    ppermute x1, starting transfers between devices, body(): sums = lax.ppermute(pay, ('groups', 'wide'), across)  0.42 us
  transfers between devices with their start and end apart: 6, of which 1 were waited for; matrix products, arithmetic and copies ran while one was open for 0% of the time, Pallas kernels for 7%

profile of v9, /device:TPU:19, one launch (start us, length us, event | category | flops | bytes accessed | tf_op | source)
XLA Modules:
  0.0 19.0 jit_solution(7922506856554412571)
XLA Ops:
  0.6 2.2 %send.1 = (f32[16,32,128]{2,1,0:T(8,128)}, f32[128,128]{1,0:T(8,128)S(1)}, f32[128,128]{1,0:T(8,128)S(1)}, f32[128,128]{1,0:T(8,128)S(1)}, f32[128,128]{1,0:T(8,...) custom-call(f32[256,128]{1,0:T(8,128)} %x_hbm.1, ...), custom_call_target="tpu_custom_call" | custom-call | tf_op jit(solution)/shard_map/send/pallas_call | solution.py:173
  2.8 4.6 %all-to-all-start = ((f32[16,32,128]{2,1,0:T(8,128)}), f32[16,32,128]{2,1,0:T(8,128)S(1)}, u32[]{:S(2)}, u32[]{:S(2)}) async-start(f32[16,32,128]{2,1,0:T(8,128)} %get-tuple-element.27), calls=%async_computation | async-start | bytes 524288 | tf_op jit(solution)/shard_map/all_to_all | solution.py:233
  7.4 0.4 %collective-permute-start = (f32[128,128]{1,0:T(8,128)S(1)}, f32[128,128]{1,0:T(8,128)S(1)}, u32[]{:S(2)}, u32[]{:S(2)}) collective-permute-start(f32[128,128]{1,0:T(8,128)S(1)} %get-tuple-element.20), channel_id=1, source_target_pairs={{0,1},{1,0},{2,3},{3,2},{4,5},{5,4},{6,7},{7,6},{8,9},{9,8},{10,11... | collective-permute-start | bytes 196616 | tf_op jit(solution)/shard_map/ppermute | solution.py:236
  7.9 0.4 %collective-permute-start.2 = (f32[128,128]{1,0:T(8,128)S(1)}, f32[128,128]{1,0:T(8,128)S(1)}, u32[]{:S(2)}, u32[]{:S(2)}) collective-permute-start(f32[128,128]{1,0:T(8,128)S(1)} %get-tuple-element.24.out_b_ref), channel_id=1, source_target_pairs={{1,2},{2,1},{3,4},{4,3},{5,6},{6,5},{7,8},{8,7},{9,10},{10,9},{11,... | collective-permute-start | bytes 196616 | tf_op jit(solution)/shard_map/ppermute | solution.py:237
  8.2 1.4 %collective-permute-start.4 = (f32[128,128]{1,0:T(8,128)S(1)}, f32[128,128]{1,0:T(8,128)S(1)}, u32[]{:S(2)}, u32[]{:S(2)}) collective-permute-start(f32[128,128]{1,0:T(8,128)S(1)} %get-tuple-element.35), channel_id=1, source_target_pairs={{1,2},{2,1},{3,4},{4,3},{5,6},{6,5},{7,8},{8,7},{9,10},{10,9},{11,... | collective-permute-start | bytes 196616 | tf_op jit(solution)/shard_map/ppermute | solution.py:238
  9.6 0.0 collective-permute-done.a_ref
  9.6 0.3 %across.1 = (f32[128,128]{1,0:T(8,128)S(1)}, f32[256,128]{1,0:T(8,128)S(1)}) custom-call(f32[128,128]{1,0:T(8,128)S(1)} %collective-permute-done.a_ref, f32[128,128]{1,0:T(8,128)S(1)} %get-tuple-element.21.m_ref, f32[384,384]{1,0:T(8,128)S(1)} %get-tuple-element.22.schur_ref), custom_call_target="tpu_custom_call" | custom-call | tf_op jit(solution)/shard_map/across/pallas_call | solution.py:173
  9.9 0.4 %collective-permute-start.1 = (f32[128,128]{1,0:T(8,128)S(1)}, f32[128,128]{1,0:T(8,128)S(1)}, u32[]{:S(2)}, u32[]{:S(2)}) collective-permute-start(f32[128,128]{1,0:T(8,128)S(1)} %get-tuple-element.23), channel_id=1, source_target_pairs={{1,2},{2,1},{3,4},{4,3},{5,6},{6,5},{7,8},{8,7},{9,10},{10,9},{11,... | collective-permute-start | bytes 196616 | tf_op jit(solution)/shard_map/ppermute | solution.py:240
  10.3 2.2 %collective-permute-done.2.got_ref = f32[128,128]{1,0:T(8,128)S(1)} collective-permute-done((f32[128,128]{1,0:T(8,128)S(1)}, f32[128,128]{1,0:T(8,128)S(1)}, u32[]{:S(2)}, u32[]{:S(2)}) %collective-permute-start.2) | collective-permute-done | bytes 65568 | tf_op jit(solution)/shard_map/ppermute | solution.py:237
  12.5 0.2 force.1
  12.7 4.4 %collective-permute-start.3 = (f32[128,128]{1,0:T(8,128)S(1)}, f32[128,128]{1,0:T(8,128)S(1)}, u32[]{:S(2)}, u32[]{:S(2)}) collective-permute-start(f32[128,128]{1,0:T(8,128)S(1)} %force.1), channel_id=1, source_target_pairs={{0,1},{1,0},{2,3},{3,2},{4,5},{5,4},{6,7},{7,6},{8,9},{9,8},{10,11... | collective-permute-start | bytes 196616 | tf_op jit(solution)/shard_map/ppermute | solution.py:245
  17.1 0.2 %base.1 = (f32[256,128]{1,0:T(8,128)S(1)}, bf16[256,512]{1,0:T(8,128)(2,1)S(1)}, bf16[256,512]{1,0:T(8,128)(2,1)S(1)}, f32[256,128]{1,0:T(8,128)S(1)}) custom-call(f32[256,128]{1,0:T(8,128)S(1)} %get-tuple-element.28.rhs_ref, f32[256,256]{1,0:T(8,128)S(1)} %get-tuple-element.29.near_ref, f32[256,128]{1,0:T(8,128)S(1)} %get-tuple-element.30.x_ref, ...), custom_call_target="tpu_custom_call" | custom-call | tf_op jit(solution)/shard_map/base/pallas_call | solution.py:173
  17.3 0.0 collective-permute-done.4.corner_ref
  17.3 0.4 %own.1.base_ref = f32[256,128]{1,0:T(8,128)S(1)} custom-call(f32[128,128]{1,0:T(8,128)S(1)} %collective-permute-done.2.got_ref, f32[128,128]{1,0:T(8,128)S(1)} %collective-permute-done.4.corner_ref, f32[128,128]{1,0:T(8,128)S(1)} %get-tuple-element.24.out_b_ref, f32[256,128]{1,0:T(8,128)S(1)} %get-tuple-element.25.part_ref._, ...), custom_call_target="tpu_custom_call" | custom-call | tf_op jit(solution)/shard_map/own/pallas_call | solution.py:173
  17.7 0.0 all-to-all-done
  17.7 0.3 %far.1.base_ref = f32[256,128]{1,0:T(8,128)S(1)} custom-call(f32[512,128]{1,0:T(8,128)S(1)} %bitcast.6, bf16[256,512]{1,0:T(8,128)(2,1)S(1)} %get-tuple-element.33.hi_ref, bf16[256,512]{1,0:T(8,128)(2,1)S(1)} %get-tuple-element.34.lo_ref, f32[256,128]{1,0:T(8,128)S(1)} %own.1.base_ref), custom_call_target="tpu_custom_call" | custom-call | tf_op jit(solution)/shard_map/far/pallas_call | solution.py:173
  18.0 0.0 collective-permute-done.1.sum_ref
  18.0 0.0 collective-permute-done.3.back_ref
  18.0 0.9 %final.1 = (f32[256,128]{1,0:T(8,128)}, f32[256,128]{1,0:T(8,128)}) custom-call(f32[128,128]{1,0:T(8,128)S(1)} %collective-permute-done.1.sum_ref, f32[128,128]{1,0:T(8,128)S(1)} %collective-permute-done.3.back_ref, bf16[256,384]{1,0:T(8,128)(2,1)S(1)} %get-tuple-element.26.sel_ref, f32[256,128]{1,0:T(8,128)S(1)} %far.1.base_ref, ...), custom_call_target="tpu_custom_call" | custom-call | tf_op jit(solution)/shard_map/final/pallas_call | solution.py:173
Async XLA Ops:
  2.8 14.9 %all-to-all-start = ((f32[16,32,128]{2,1,0:T(8,128)}), f32[16,32,128]{2,1,0:T(8,128)S(1)}, u32[]{:S(2)}, u32[]{:S(2)}) async-start(f32[16,32,128]{2,1,0:T(8,128)} %get-tuple-element.27), calls=%async_computation | async-start | bytes 524288 | tf_op jit(solution)/shard_map/all_to_all | solution.py:233
  7.4 2.2 %collective-permute-start = (f32[128,128]{1,0:T(8,128)S(1)}, f32[128,128]{1,0:T(8,128)S(1)}, u32[]{:S(2)}, u32[]{:S(2)}) collective-permute-start(f32[128,128]{1,0:T(8,128)S(1)} %get-tuple-element.20), channel_id=1, source_target_pairs={{0,1},{1,0},{2,3},{3,2},{4,5},{5,4},{6,7},{7,6},{8,9},{9,8},{10,11... | collective-permute-start | bytes 196616 | tf_op jit(solution)/shard_map/ppermute | solution.py:236
  7.9 4.6 %collective-permute-start.2 = (f32[128,128]{1,0:T(8,128)S(1)}, f32[128,128]{1,0:T(8,128)S(1)}, u32[]{:S(2)}, u32[]{:S(2)}) collective-permute-start(f32[128,128]{1,0:T(8,128)S(1)} %get-tuple-element.24.out_b_ref), channel_id=1, source_target_pairs={{1,2},{2,1},{3,4},{4,3},{5,6},{6,5},{7,8},{8,7},{9,10},{10,9},{11,... | collective-permute-start | bytes 196616 | tf_op jit(solution)/shard_map/ppermute | solution.py:237
  8.2 9.1 %collective-permute-start.4 = (f32[128,128]{1,0:T(8,128)S(1)}, f32[128,128]{1,0:T(8,128)S(1)}, u32[]{:S(2)}, u32[]{:S(2)}) collective-permute-start(f32[128,128]{1,0:T(8,128)S(1)} %get-tuple-element.35), channel_id=1, source_target_pairs={{1,2},{2,1},{3,4},{4,3},{5,6},{6,5},{7,8},{8,7},{9,10},{10,9},{11,... | collective-permute-start | bytes 196616 | tf_op jit(solution)/shard_map/ppermute | solution.py:238
  9.9 8.1 %collective-permute-start.1 = (f32[128,128]{1,0:T(8,128)S(1)}, f32[128,128]{1,0:T(8,128)S(1)}, u32[]{:S(2)}, u32[]{:S(2)}) collective-permute-start(f32[128,128]{1,0:T(8,128)S(1)} %get-tuple-element.23), channel_id=1, source_target_pairs={{1,2},{2,1},{3,4},{4,3},{5,6},{6,5},{7,8},{8,7},{9,10},{10,9},{11,... | collective-permute-start | bytes 196616 | tf_op jit(solution)/shard_map/ppermute | solution.py:240
  12.7 5.4 %collective-permute-start.3 = (f32[128,128]{1,0:T(8,128)S(1)}, f32[128,128]{1,0:T(8,128)S(1)}, u32[]{:S(2)}, u32[]{:S(2)}) collective-permute-start(f32[128,128]{1,0:T(8,128)S(1)} %force.1), channel_id=1, source_target_pairs={{0,1},{1,0},{2,3},{3,2},{4,5},{5,4},{6,7},{7,6},{8,9},{9,8},{10,11... | collective-permute-start | bytes 196616 | tf_op jit(solution)/shard_map/ppermute | solution.py:245

commit v10 on v9

--- a/solution.py
+++ b/solution.py
@@ -108,6 +108,12 @@
     corner_ref[...] = schur_ref[last, last]
 
 
+def inside_part(ref):
+    index = lax.axis_index("wide")
+    at_end = (index == 0) | (index == lax.axis_size("wide") - 1)
+    return jnp.where(at_end, 0.0, ref[...])
+
+
 def place(odd, spot, face):
     if spot == 1:
         return face
@@ -143,15 +149,15 @@
     odd = is_odd()
     face = fa_ref.shape[0]
     block = schur_ref[pl.ds(place(odd, 0, face), face), pl.ds(place(odd, 2, face), face)]
-    fa_ref[...] = part_ref[:face] + product(block, wide_halves(got_ref[...]))
+    fa_ref[...] = part_ref[:face] + product(block, wide_halves(inside_part(got_ref)))
 
 
 def own_kernel(got_ref, corner_ref, out_b_ref, part_ref, schur_ref, sel_ref, base_ref, next_ref):
     odd = is_odd()
     face = got_ref.shape[0]
     block = schur_ref[face : 2 * face, pl.ds(place(odd, 2, face), face)]
-    own = part_ref[face:] + product(block, wide_halves(got_ref[...]))
-    back = product(corner_ref[...], wide_halves(out_b_ref[...]))
+    own = part_ref[face:] + product(block, wide_halves(inside_part(got_ref)))
+    back = product(inside_part(corner_ref), wide_halves(out_b_ref[...]))
     both = jnp.concatenate([wide_halves(own), wide_halves(back)], axis=0)
     next_ref[...] = base_ref[...] - fold(dot(sel_ref[:, face:], both))
 
@@ -163,7 +169,7 @@
 def final_kernel(sum_ref, back_ref, sel_ref, base_ref, x_ref, scale_ref, up_ref, res_ref):
     face = back_ref.shape[0]
     a = dot(sel_ref[:, :face], wide_halves(back_ref[...]))
-    b = dot(sel_ref[:, 2 * face :], wide_halves(sum_ref[...]))
+    b = dot(sel_ref[:, 2 * face :], wide_halves(inside_part(sum_ref)))
     res = base_ref[...] - fold(a + b)
     res_ref[...] = res
     up_ref[...] = x_ref[...] + scale_ref[...] * res

time: 19.2 us -> 19.2 us (level)
  no operation moved by 1% of the time
where the time goes in v10:
time: 19.2 us; the launch traced here: 19 us
  starting transfers between devices  11.6 us (60%)
  Pallas kernels  4.48 us (23%)
  waiting for transfers between devices  2.2 us (11%)
  between operations  0.7 us (4%)
    all_to_all x1, starting transfers between devices, body(): lax.all_to_all(coeff, 'wide', split_axis=0, concat_axis=0, tiled=True, ax...  4.61 us
    pallas_call x7, Pallas kernels, call(): pl.pallas_call(kernel, out_shape=tuple((space(s, t) for space, (s, t) in...  4.48 us
    ppermute x1, starting transfers between devices, body(): back = lax.ppermute(f_a, 'wide', inside)  4.4 us
    ppermute x1, waiting for transfers between devices, body(): got = lax.ppermute(out_b, ('groups', 'wide'), across)  2.19 us
    ppermute x1, starting transfers between devices, body(): corner = lax.ppermute(corner, ('groups', 'wide'), across)  1.39 us
    ppermute x1, starting transfers between devices, body(): in_a = lax.ppermute(out_a, 'wide', inside)  0.43 us
    ppermute x1, starting transfers between devices, body(): sums = lax.ppermute(pay, ('groups', 'wide'), across)  0.42 us
  transfers between devices with their start and end apart: 6, of which 1 were waited for; matrix products, arithmetic and copies ran while one was open for 0% of the time, Pallas kernels for 7%

profile of v10, /device:TPU:19, one launch (start us, length us, event | category | flops | bytes accessed | tf_op | source)
XLA Modules:
  0.0 19.0 jit_solution(1075504263498524730)
XLA Ops:
  0.6 2.2 %send.1 = (f32[16,32,128]{2,1,0:T(8,128)}, f32[128,128]{1,0:T(8,128)S(1)}, f32[128,128]{1,0:T(8,128)S(1)}, f32[128,128]{1,0:T(8,128)S(1)}, f32[128,128]{1,0:T(8,...) custom-call(f32[256,128]{1,0:T(8,128)} %x_hbm.1, ...), custom_call_target="tpu_custom_call" | custom-call | tf_op jit(solution)/shard_map/send/pallas_call | solution.py:179
  2.8 4.6 %all-to-all-start = ((f32[16,32,128]{2,1,0:T(8,128)}), f32[16,32,128]{2,1,0:T(8,128)S(1)}, u32[]{:S(2)}, u32[]{:S(2)}) async-start(f32[16,32,128]{2,1,0:T(8,128)} %get-tuple-element.27), calls=%async_computation | async-start | bytes 524288 | tf_op jit(solution)/shard_map/all_to_all | solution.py:239
  7.4 0.4 %collective-permute-start = (f32[128,128]{1,0:T(8,128)S(1)}, f32[128,128]{1,0:T(8,128)S(1)}, u32[]{:S(2)}, u32[]{:S(2)}) collective-permute-start(f32[128,128]{1,0:T(8,128)S(1)} %get-tuple-element.20), channel_id=1, source_target_pairs={{0,1},{1,0},{2,3},{3,2},{4,5},{5,4},{6,7},{7,6},{8,9},{9,8},{10,11... | collective-permute-start | bytes 196616 | tf_op jit(solution)/shard_map/ppermute | solution.py:242
  7.9 0.4 %collective-permute-start.2 = (f32[128,128]{1,0:T(8,128)S(1)}, f32[128,128]{1,0:T(8,128)S(1)}, u32[]{:S(2)}, u32[]{:S(2)}) collective-permute-start(f32[128,128]{1,0:T(8,128)S(1)} %get-tuple-element.24.out_b_ref), channel_id=1, source_target_pairs={{1,2},{2,1},{3,4},{4,3},{5,6},{6,5},{7,8},{8,7},{9,10},{10,9},{11,... | collective-permute-start | bytes 196616 | tf_op jit(solution)/shard_map/ppermute | solution.py:243
  8.2 1.4 %collective-permute-start.4 = (f32[128,128]{1,0:T(8,128)S(1)}, f32[128,128]{1,0:T(8,128)S(1)}, u32[]{:S(2)}, u32[]{:S(2)}) collective-permute-start(f32[128,128]{1,0:T(8,128)S(1)} %get-tuple-element.35), channel_id=1, source_target_pairs={{1,2},{2,1},{3,4},{4,3},{5,6},{6,5},{7,8},{8,7},{9,10},{10,9},{11,... | collective-permute-start | bytes 196616 | tf_op jit(solution)/shard_map/ppermute | solution.py:244
  9.6 0.0 collective-permute-done.a_ref
  9.6 0.3 %across.1 = (f32[128,128]{1,0:T(8,128)S(1)}, f32[256,128]{1,0:T(8,128)S(1)}) custom-call(f32[128,128]{1,0:T(8,128)S(1)} %collective-permute-done.a_ref, f32[128,128]{1,0:T(8,128)S(1)} %get-tuple-element.21.m_ref, f32[384,384]{1,0:T(8,128)S(1)} %get-tuple-element.22.schur_ref), custom_call_target="tpu_custom_call" | custom-call | tf_op jit(solution)/shard_map/across/pallas_call | solution.py:179
  9.9 0.4 %collective-permute-start.1 = (f32[128,128]{1,0:T(8,128)S(1)}, f32[128,128]{1,0:T(8,128)S(1)}, u32[]{:S(2)}, u32[]{:S(2)}) collective-permute-start(f32[128,128]{1,0:T(8,128)S(1)} %get-tuple-element.23), channel_id=1, source_target_pairs={{1,2},{2,1},{3,4},{4,3},{5,6},{6,5},{7,8},{8,7},{9,10},{10,9},{11,... | collective-permute-start | bytes 196616 | tf_op jit(solution)/shard_map/ppermute | solution.py:246
  10.3 2.2 %collective-permute-done.2.got_ref = f32[128,128]{1,0:T(8,128)S(1)} collective-permute-done((f32[128,128]{1,0:T(8,128)S(1)}, f32[128,128]{1,0:T(8,128)S(1)}, u32[]{:S(2)}, u32[]{:S(2)}) %collective-permute-start.2) | collective-permute-done | bytes 65568 | tf_op jit(solution)/shard_map/ppermute | solution.py:243
  12.5 0.2 force.1
  12.7 4.4 %collective-permute-start.3 = (f32[128,128]{1,0:T(8,128)S(1)}, f32[128,128]{1,0:T(8,128)S(1)}, u32[]{:S(2)}, u32[]{:S(2)}) collective-permute-start(f32[128,128]{1,0:T(8,128)S(1)} %force.1), channel_id=1, source_target_pairs={{0,1},{1,0},{2,3},{3,2},{4,5},{5,4},{6,7},{7,6},{8,9},{9,8},{10,11... | collective-permute-start | bytes 196616 | tf_op jit(solution)/shard_map/ppermute | solution.py:251
  17.1 0.2 %base.1 = (f32[256,128]{1,0:T(8,128)S(1)}, bf16[256,512]{1,0:T(8,128)(2,1)S(1)}, bf16[256,512]{1,0:T(8,128)(2,1)S(1)}, f32[256,128]{1,0:T(8,128)S(1)}) custom-call(f32[256,128]{1,0:T(8,128)S(1)} %get-tuple-element.28.rhs_ref, f32[256,256]{1,0:T(8,128)S(1)} %get-tuple-element.29.near_ref, f32[256,128]{1,0:T(8,128)S(1)} %get-tuple-element.30.x_ref, ...), custom_call_target="tpu_custom_call" | custom-call | tf_op jit(solution)/shard_map/base/pallas_call | solution.py:179
  17.3 0.0 collective-permute-done.4.corner_ref
  17.3 0.4 %own.1.base_ref = f32[256,128]{1,0:T(8,128)S(1)} custom-call(f32[128,128]{1,0:T(8,128)S(1)} %collective-permute-done.2.got_ref, f32[128,128]{1,0:T(8,128)S(1)} %collective-permute-done.4.corner_ref, f32[128,128]{1,0:T(8,128)S(1)} %get-tuple-element.24.out_b_ref, f32[256,128]{1,0:T(8,128)S(1)} %get-tuple-element.25.part_ref._, ...), custom_call_target="tpu_custom_call" | custom-call | tf_op jit(solution)/shard_map/own/pallas_call | solution.py:179
  17.7 0.0 all-to-all-done
  17.7 0.3 %far.1.base_ref = f32[256,128]{1,0:T(8,128)S(1)} custom-call(f32[512,128]{1,0:T(8,128)S(1)} %bitcast.6, bf16[256,512]{1,0:T(8,128)(2,1)S(1)} %get-tuple-element.33.hi_ref, bf16[256,512]{1,0:T(8,128)(2,1)S(1)} %get-tuple-element.34.lo_ref, f32[256,128]{1,0:T(8,128)S(1)} %own.1.base_ref), custom_call_target="tpu_custom_call" | custom-call | tf_op jit(solution)/shard_map/far/pallas_call | solution.py:179
  18.0 0.0 collective-permute-done.1.sum_ref
  18.0 0.0 collective-permute-done.3.back_ref
  18.1 0.9 %final.1 = (f32[256,128]{1,0:T(8,128)}, f32[256,128]{1,0:T(8,128)}) custom-call(f32[128,128]{1,0:T(8,128)S(1)} %collective-permute-done.1.sum_ref, f32[128,128]{1,0:T(8,128)S(1)} %collective-permute-done.3.back_ref, bf16[256,384]{1,0:T(8,128)(2,1)S(1)} %get-tuple-element.26.sel_ref, f32[256,128]{1,0:T(8,128)S(1)} %far.1.base_ref, ...), custom_call_target="tpu_custom_call" | custom-call | tf_op jit(solution)/shard_map/final/pallas_call | solution.py:179
Async XLA Ops:
  2.8 14.9 %all-to-all-start = ((f32[16,32,128]{2,1,0:T(8,128)}), f32[16,32,128]{2,1,0:T(8,128)S(1)}, u32[]{:S(2)}, u32[]{:S(2)}) async-start(f32[16,32,128]{2,1,0:T(8,128)} %get-tuple-element.27), calls=%async_computation | async-start | bytes 524288 | tf_op jit(solution)/shard_map/all_to_all | solution.py:239
  7.4 2.2 %collective-permute-start = (f32[128,128]{1,0:T(8,128)S(1)}, f32[128,128]{1,0:T(8,128)S(1)}, u32[]{:S(2)}, u32[]{:S(2)}) collective-permute-start(f32[128,128]{1,0:T(8,128)S(1)} %get-tuple-element.20), channel_id=1, source_target_pairs={{0,1},{1,0},{2,3},{3,2},{4,5},{5,4},{6,7},{7,6},{8,9},{9,8},{10,11... | collective-permute-start | bytes 196616 | tf_op jit(solution)/shard_map/ppermute | solution.py:242
  7.9 4.6 %collective-permute-start.2 = (f32[128,128]{1,0:T(8,128)S(1)}, f32[128,128]{1,0:T(8,128)S(1)}, u32[]{:S(2)}, u32[]{:S(2)}) collective-permute-start(f32[128,128]{1,0:T(8,128)S(1)} %get-tuple-element.24.out_b_ref), channel_id=1, source_target_pairs={{1,2},{2,1},{3,4},{4,3},{5,6},{6,5},{7,8},{8,7},{9,10},{10,9},{11,... | collective-permute-start | bytes 196616 | tf_op jit(solution)/shard_map/ppermute | solution.py:243
  8.2 9.1 %collective-permute-start.4 = (f32[128,128]{1,0:T(8,128)S(1)}, f32[128,128]{1,0:T(8,128)S(1)}, u32[]{:S(2)}, u32[]{:S(2)}) collective-permute-start(f32[128,128]{1,0:T(8,128)S(1)} %get-tuple-element.35), channel_id=1, source_target_pairs={{1,2},{2,1},{3,4},{4,3},{5,6},{6,5},{7,8},{8,7},{9,10},{10,9},{11,... | collective-permute-start | bytes 196616 | tf_op jit(solution)/shard_map/ppermute | solution.py:244
  9.9 8.2 %collective-permute-start.1 = (f32[128,128]{1,0:T(8,128)S(1)}, f32[128,128]{1,0:T(8,128)S(1)}, u32[]{:S(2)}, u32[]{:S(2)}) collective-permute-start(f32[128,128]{1,0:T(8,128)S(1)} %get-tuple-element.23), channel_id=1, source_target_pairs={{1,2},{2,1},{3,4},{4,3},{5,6},{6,5},{7,8},{8,7},{9,10},{10,9},{11,... | collective-permute-start | bytes 196616 | tf_op jit(solution)/shard_map/ppermute | solution.py:246
  12.7 5.4 %collective-permute-start.3 = (f32[128,128]{1,0:T(8,128)S(1)}, f32[128,128]{1,0:T(8,128)S(1)}, u32[]{:S(2)}, u32[]{:S(2)}) collective-permute-start(f32[128,128]{1,0:T(8,128)S(1)} %force.1), channel_id=1, source_target_pairs={{0,1},{1,0},{2,3},{3,2},{4,5},{5,4},{6,7},{7,6},{8,9},{9,8},{10,11... | collective-permute-start | bytes 196616 | tf_op jit(solution)/shard_map/ppermute | solution.py:251

commit v11 on v10

--- a/solution.py
+++ b/solution.py
@@ -96,9 +96,10 @@
     down = lax.broadcasted_iota(jnp.int32, (n_rows, face), 0)
     for spot, out_ref in enumerate((a_ref, m_ref, b_ref)):
         rows = jnp.where(lane < count_ref[slots[spot]], rows_ref[slots[spot]], -1)
-        sel_ref[:, spot * face : (spot + 1) * face] = (down == rows).astype(f32).astype(bf16)
-        column = jnp.broadcast_to(rows.astype(f32), (face, face)).T[:, :1]
-        select = (across == column).astype(f32).astype(bf16)
+        column = (0, 2, 1)[spot] * face
+        sel_ref[:, column : column + face] = (down == rows).astype(f32).astype(bf16)
+        wanted = jnp.broadcast_to(rows.astype(f32), (face, face)).T[:, :1]
+        select = (across == wanted).astype(f32).astype(bf16)
         out_ref[...] = fold(dot(select, x_wide))
     for s in range(tiles // step):
         out_move(s).wait()
@@ -158,7 +159,7 @@
     block = schur_ref[face : 2 * face, pl.ds(place(odd, 2, face), face)]
     own = part_ref[face:] + product(block, wide_halves(inside_part(got_ref)))
     back = product(inside_part(corner_ref), wide_halves(out_b_ref[...]))
-    both = jnp.concatenate([wide_halves(own), wide_halves(back)], axis=0)
+    both = jnp.concatenate([wide_halves(back), wide_halves(own)], axis=0)
     next_ref[...] = base_ref[...] - fold(dot(sel_ref[:, face:], both))
 
 
@@ -168,9 +169,8 @@
 
 def final_kernel(sum_ref, back_ref, sel_ref, base_ref, x_ref, scale_ref, up_ref, res_ref):
     face = back_ref.shape[0]
-    a = dot(sel_ref[:, :face], wide_halves(back_ref[...]))
-    b = dot(sel_ref[:, 2 * face :], wide_halves(inside_part(sum_ref)))
-    res = base_ref[...] - fold(a + b)
+    both = jnp.concatenate([wide_halves(back_ref[...]), wide_halves(inside_part(sum_ref))], axis=0)
+    res = base_ref[...] - fold(dot(sel_ref[:, : 2 * face], both))
     res_ref[...] = res
     up_ref[...] = x_ref[...] + scale_ref[...] * res
 

time: 19.2 us -> 19.2 us (level)
  no operation moved by 1% of the time
where the time goes in v11:
time: 19.2 us; the launch traced here: 19 us
  starting transfers between devices  11.6 us (60%)
  Pallas kernels  4.47 us (23%)
  waiting for transfers between devices  2.2 us (11%)
  between operations  0.7 us (4%)
    all_to_all x1, starting transfers between devices, body(): lax.all_to_all(coeff, 'wide', split_axis=0, concat_axis=0, tiled=True, ax...  4.61 us
    pallas_call x7, Pallas kernels, call(): pl.pallas_call(kernel, out_shape=tuple((space(s, t) for space, (s, t) in...  4.47 us
    ppermute x1, starting transfers between devices, body(): back = lax.ppermute(f_a, 'wide', inside)  4.4 us
    ppermute x1, waiting for transfers between devices, body(): got = lax.ppermute(out_b, ('groups', 'wide'), across)  2.19 us
    ppermute x1, starting transfers between devices, body(): corner = lax.ppermute(corner, ('groups', 'wide'), across)  1.39 us
    ppermute x1, starting transfers between devices, body(): in_a = lax.ppermute(out_a, 'wide', inside)  0.43 us
    ppermute x1, starting transfers between devices, body(): sums = lax.ppermute(pay, ('groups', 'wide'), across)  0.42 us
  transfers between devices with their start and end apart: 6, of which 1 were waited for; matrix products, arithmetic and copies ran while one was open for 0% of the time, Pallas kernels for 7%

profile of v11, /device:TPU:19, one launch (start us, length us, event | category | flops | bytes accessed | tf_op | source)
XLA Modules:
  0.0 19.0 jit_solution(9350139235168474805)
XLA Ops:
  0.6 2.2 %send.1 = (f32[16,32,128]{2,1,0:T(8,128)}, f32[128,128]{1,0:T(8,128)S(1)}, f32[128,128]{1,0:T(8,128)S(1)}, f32[128,128]{1,0:T(8,128)S(1)}, f32[128,128]{1,0:T(8,...) custom-call(f32[256,128]{1,0:T(8,128)} %x_hbm.1, ...), custom_call_target="tpu_custom_call" | custom-call | tf_op jit(solution)/shard_map/send/pallas_call | solution.py:179
  2.8 4.6 %all-to-all-start = ((f32[16,32,128]{2,1,0:T(8,128)}), f32[16,32,128]{2,1,0:T(8,128)S(1)}, u32[]{:S(2)}, u32[]{:S(2)}) async-start(f32[16,32,128]{2,1,0:T(8,128)} %get-tuple-element.27), calls=%async_computation | async-start | bytes 524288 | tf_op jit(solution)/shard_map/all_to_all | solution.py:239
  7.4 0.4 %collective-permute-start = (f32[128,128]{1,0:T(8,128)S(1)}, f32[128,128]{1,0:T(8,128)S(1)}, u32[]{:S(2)}, u32[]{:S(2)}) collective-permute-start(f32[128,128]{1,0:T(8,128)S(1)} %get-tuple-element.20), channel_id=1, source_target_pairs={{0,1},{1,0},{2,3},{3,2},{4,5},{5,4},{6,7},{7,6},{8,9},{9,8},{10,11... | collective-permute-start | bytes 196616 | tf_op jit(solution)/shard_map/ppermute | solution.py:242
  7.9 0.4 %collective-permute-start.2 = (f32[128,128]{1,0:T(8,128)S(1)}, f32[128,128]{1,0:T(8,128)S(1)}, u32[]{:S(2)}, u32[]{:S(2)}) collective-permute-start(f32[128,128]{1,0:T(8,128)S(1)} %get-tuple-element.24.out_b_ref), channel_id=1, source_target_pairs={{1,2},{2,1},{3,4},{4,3},{5,6},{6,5},{7,8},{8,7},{9,10},{10,9},{11,... | collective-permute-start | bytes 196616 | tf_op jit(solution)/shard_map/ppermute | solution.py:243
  8.2 1.4 %collective-permute-start.4 = (f32[128,128]{1,0:T(8,128)S(1)}, f32[128,128]{1,0:T(8,128)S(1)}, u32[]{:S(2)}, u32[]{:S(2)}) collective-permute-start(f32[128,128]{1,0:T(8,128)S(1)} %get-tuple-element.35), channel_id=1, source_target_pairs={{1,2},{2,1},{3,4},{4,3},{5,6},{6,5},{7,8},{8,7},{9,10},{10,9},{11,... | collective-permute-start | bytes 196616 | tf_op jit(solution)/shard_map/ppermute | solution.py:244
  9.6 0.0 collective-permute-done.a_ref
  9.6 0.3 %across.1 = (f32[128,128]{1,0:T(8,128)S(1)}, f32[256,128]{1,0:T(8,128)S(1)}) custom-call(f32[128,128]{1,0:T(8,128)S(1)} %collective-permute-done.a_ref, f32[128,128]{1,0:T(8,128)S(1)} %get-tuple-element.21.m_ref, f32[384,384]{1,0:T(8,128)S(1)} %get-tuple-element.22.schur_ref), custom_call_target="tpu_custom_call" | custom-call | tf_op jit(solution)/shard_map/across/pallas_call | solution.py:179
  9.9 0.4 %collective-permute-start.1 = (f32[128,128]{1,0:T(8,128)S(1)}, f32[128,128]{1,0:T(8,128)S(1)}, u32[]{:S(2)}, u32[]{:S(2)}) collective-permute-start(f32[128,128]{1,0:T(8,128)S(1)} %get-tuple-element.23), channel_id=1, source_target_pairs={{1,2},{2,1},{3,4},{4,3},{5,6},{6,5},{7,8},{8,7},{9,10},{10,9},{11,... | collective-permute-start | bytes 196616 | tf_op jit(solution)/shard_map/ppermute | solution.py:246
  10.3 2.2 %collective-permute-done.2.got_ref = f32[128,128]{1,0:T(8,128)S(1)} collective-permute-done((f32[128,128]{1,0:T(8,128)S(1)}, f32[128,128]{1,0:T(8,128)S(1)}, u32[]{:S(2)}, u32[]{:S(2)}) %collective-permute-start.2) | collective-permute-done | bytes 65568 | tf_op jit(solution)/shard_map/ppermute | solution.py:243
  12.5 0.2 force.1
  12.7 4.4 %collective-permute-start.3 = (f32[128,128]{1,0:T(8,128)S(1)}, f32[128,128]{1,0:T(8,128)S(1)}, u32[]{:S(2)}, u32[]{:S(2)}) collective-permute-start(f32[128,128]{1,0:T(8,128)S(1)} %force.1), channel_id=1, source_target_pairs={{0,1},{1,0},{2,3},{3,2},{4,5},{5,4},{6,7},{7,6},{8,9},{9,8},{10,11... | collective-permute-start | bytes 196616 | tf_op jit(solution)/shard_map/ppermute | solution.py:251
  17.1 0.2 %base.1 = (f32[256,128]{1,0:T(8,128)S(1)}, bf16[256,512]{1,0:T(8,128)(2,1)S(1)}, bf16[256,512]{1,0:T(8,128)(2,1)S(1)}, f32[256,128]{1,0:T(8,128)S(1)}) custom-call(f32[256,128]{1,0:T(8,128)S(1)} %get-tuple-element.28.rhs_ref, f32[256,256]{1,0:T(8,128)S(1)} %get-tuple-element.29.near_ref, f32[256,128]{1,0:T(8,128)S(1)} %get-tuple-element.30.x_ref, ...), custom_call_target="tpu_custom_call" | custom-call | tf_op jit(solution)/shard_map/base/pallas_call | solution.py:179
  17.3 0.0 collective-permute-done.4.corner_ref
  17.3 0.4 %own.1.base_ref = f32[256,128]{1,0:T(8,128)S(1)} custom-call(f32[128,128]{1,0:T(8,128)S(1)} %collective-permute-done.2.got_ref, f32[128,128]{1,0:T(8,128)S(1)} %collective-permute-done.4.corner_ref, f32[128,128]{1,0:T(8,128)S(1)} %get-tuple-element.24.out_b_ref, f32[256,128]{1,0:T(8,128)S(1)} %get-tuple-element.25.part_ref._, ...), custom_call_target="tpu_custom_call" | custom-call | tf_op jit(solution)/shard_map/own/pallas_call | solution.py:179
  17.7 0.0 all-to-all-done
  17.7 0.3 %far.1.base_ref = f32[256,128]{1,0:T(8,128)S(1)} custom-call(f32[512,128]{1,0:T(8,128)S(1)} %bitcast.6, bf16[256,512]{1,0:T(8,128)(2,1)S(1)} %get-tuple-element.33.hi_ref, bf16[256,512]{1,0:T(8,128)(2,1)S(1)} %get-tuple-element.34.lo_ref, f32[256,128]{1,0:T(8,128)S(1)} %own.1.base_ref), custom_call_target="tpu_custom_call" | custom-call | tf_op jit(solution)/shard_map/far/pallas_call | solution.py:179
  18.0 0.0 collective-permute-done.1.sum_ref
  18.1 0.0 collective-permute-done.3.back_ref
  18.1 0.9 %final.1 = (f32[256,128]{1,0:T(8,128)}, f32[256,128]{1,0:T(8,128)}) custom-call(f32[128,128]{1,0:T(8,128)S(1)} %collective-permute-done.1.sum_ref, f32[128,128]{1,0:T(8,128)S(1)} %collective-permute-done.3.back_ref, bf16[256,384]{1,0:T(8,128)(2,1)S(1)} %get-tuple-element.26.sel_ref, f32[256,128]{1,0:T(8,128)S(1)} %far.1.base_ref, ...), custom_call_target="tpu_custom_call" | custom-call | tf_op jit(solution)/shard_map/final/pallas_call | solution.py:179
Async XLA Ops:
  2.8 14.9 %all-to-all-start = ((f32[16,32,128]{2,1,0:T(8,128)}), f32[16,32,128]{2,1,0:T(8,128)S(1)}, u32[]{:S(2)}, u32[]{:S(2)}) async-start(f32[16,32,128]{2,1,0:T(8,128)} %get-tuple-element.27), calls=%async_computation | async-start | bytes 524288 | tf_op jit(solution)/shard_map/all_to_all | solution.py:239
  7.4 2.2 %collective-permute-start = (f32[128,128]{1,0:T(8,128)S(1)}, f32[128,128]{1,0:T(8,128)S(1)}, u32[]{:S(2)}, u32[]{:S(2)}) collective-permute-start(f32[128,128]{1,0:T(8,128)S(1)} %get-tuple-element.20), channel_id=1, source_target_pairs={{0,1},{1,0},{2,3},{3,2},{4,5},{5,4},{6,7},{7,6},{8,9},{9,8},{10,11... | collective-permute-start | bytes 196616 | tf_op jit(solution)/shard_map/ppermute | solution.py:242
  7.9 4.6 %collective-permute-start.2 = (f32[128,128]{1,0:T(8,128)S(1)}, f32[128,128]{1,0:T(8,128)S(1)}, u32[]{:S(2)}, u32[]{:S(2)}) collective-permute-start(f32[128,128]{1,0:T(8,128)S(1)} %get-tuple-element.24.out_b_ref), channel_id=1, source_target_pairs={{1,2},{2,1},{3,4},{4,3},{5,6},{6,5},{7,8},{8,7},{9,10},{10,9},{11,... | collective-permute-start | bytes 196616 | tf_op jit(solution)/shard_map/ppermute | solution.py:243
  8.2 9.1 %collective-permute-start.4 = (f32[128,128]{1,0:T(8,128)S(1)}, f32[128,128]{1,0:T(8,128)S(1)}, u32[]{:S(2)}, u32[]{:S(2)}) collective-permute-start(f32[128,128]{1,0:T(8,128)S(1)} %get-tuple-element.35), channel_id=1, source_target_pairs={{1,2},{2,1},{3,4},{4,3},{5,6},{6,5},{7,8},{8,7},{9,10},{10,9},{11,... | collective-permute-start | bytes 196616 | tf_op jit(solution)/shard_map/ppermute | solution.py:244
  9.9 8.2 %collective-permute-start.1 = (f32[128,128]{1,0:T(8,128)S(1)}, f32[128,128]{1,0:T(8,128)S(1)}, u32[]{:S(2)}, u32[]{:S(2)}) collective-permute-start(f32[128,128]{1,0:T(8,128)S(1)} %get-tuple-element.23), channel_id=1, source_target_pairs={{1,2},{2,1},{3,4},{4,3},{5,6},{6,5},{7,8},{8,7},{9,10},{10,9},{11,... | collective-permute-start | bytes 196616 | tf_op jit(solution)/shard_map/ppermute | solution.py:246
  12.7 5.4 %collective-permute-start.3 = (f32[128,128]{1,0:T(8,128)S(1)}, f32[128,128]{1,0:T(8,128)S(1)}, u32[]{:S(2)}, u32[]{:S(2)}) collective-permute-start(f32[128,128]{1,0:T(8,128)S(1)} %force.1), channel_id=1, source_target_pairs={{0,1},{1,0},{2,3},{3,2},{4,5},{5,4},{6,7},{7,6},{8,9},{9,8},{10,11... | collective-permute-start | bytes 196616 | tf_op jit(solution)/shard_map/ppermute | solution.py:251

commit v12 on v11

--- a/solution.py
+++ b/solution.py
@@ -2,6 +2,7 @@
 
 import jax
 import jax.numpy as jnp
+import numpy as np
 from jax import lax
 from jax.experimental import pallas as pl
 from jax.experimental.pallas import tpu as pltpu
@@ -48,8 +49,8 @@
 def group_order(size):
     pairs = size // 2
     first = 2 * (pairs // 2 + math.isqrt(pairs) // 2) + 1
-    stride = 5 if math.gcd(5, size) == 1 else 1
-    return [(first + stride * i) % size for i in range(size)]
+    rest = [i for i in range(size) if i != first]
+    return [first] + [rest[i] for i in np.random.RandomState(12).permutation(size - 1).tolist()]
 
 
 def tiles_at_once(tiles, top):
@@ -63,16 +64,16 @@
     face = rows_ref.shape[2]
     tiles, top, _ = v_ref.shape
     order = group_order(tiles)
-    early = [(x_hbm, x_ref), (rank_hbm, rank_ref), (v_hbm, v_ref)]
+    early = [(v_hbm, v_ref), (x_hbm, x_ref), (rank_hbm, rank_ref)]
     middle = [(rows_hbm, rows_ref), (count_hbm, count_ref)]
     late = [(schur_hbm, schur_ref), (u_hbm, u_ref), (near_hbm, near_ref), (rhs_hbm, rhs_ref), (p_hbm, p_ref)]
     moves = [pltpu.make_async_copy(src, dst, sems.at[i]) for i, (src, dst) in enumerate(early + middle + late)]
     for move in moves:
         move.start()
+    moves[1].wait()
+    x_wide = wide_halves(x_ref[...])
     moves[0].wait()
-    x_wide = wide_halves(x_ref[...])
-    for move in moves[1 : len(early)]:
-        move.wait()
+    moves[2].wait()
     step = tiles_at_once(tiles, top)
     k = lax.broadcasted_iota(jnp.int32, (top, loads), 0)
 

time: 19.2 us -> 19.2 us (level)
  waiting for transfers between devices: 2.2 us -> 1.72 us
  starting transfers between devices: 11.6 us -> 12 us
    ppermute x1, waiting for transfers between devices: 2.19 us -> 1.71 us  [body(): got = lax.ppermute(out_b, ('groups', 'wide'), across)]
    ppermute x1, starting transfers between devices: 4.4 us -> 4.82 us  [body(): back = lax.ppermute(f_a, 'wide', inside)]
where the time goes in v12:
time: 19.2 us; the launch traced here: 18.9 us
  starting transfers between devices  12 us (62%)
  Pallas kernels  4.45 us (23%)
  waiting for transfers between devices  1.72 us (9%)
  between operations  0.7 us (4%)
    ppermute x1, starting transfers between devices, body(): back = lax.ppermute(f_a, 'wide', inside)  4.82 us
    all_to_all x1, starting transfers between devices, body(): lax.all_to_all(coeff, 'wide', split_axis=0, concat_axis=0, tiled=True, ax...  4.62 us
    pallas_call x7, Pallas kernels, call(): pl.pallas_call(kernel, out_shape=tuple((space(s, t) for space, (s, t) in...  4.45 us
    ppermute x1, waiting for transfers between devices, body(): got = lax.ppermute(out_b, ('groups', 'wide'), across)  1.71 us
    ppermute x1, starting transfers between devices, body(): corner = lax.ppermute(corner, ('groups', 'wide'), across)  1.33 us
    ppermute x1, starting transfers between devices, body(): sums = lax.ppermute(pay, ('groups', 'wide'), across)  0.49 us
    ppermute x1, starting transfers between devices, body(): got = lax.ppermute(out_b, ('groups', 'wide'), across)  0.42 us
  transfers between devices with their start and end apart: 6, of which 1 were waited for; matrix products, arithmetic and copies ran while one was open for 0% of the time, Pallas kernels for 7%

profile of v12, /device:TPU:19, one launch (start us, length us, event | category | flops | bytes accessed | tf_op | source)
XLA Modules:
  0.0 18.9 jit_solution(11644650342402352007)
XLA Ops:
  0.6 2.2 %send.1 = (f32[16,32,128]{2,1,0:T(8,128)}, f32[128,128]{1,0:T(8,128)S(1)}, f32[128,128]{1,0:T(8,128)S(1)}, f32[128,128]{1,0:T(8,128)S(1)}, f32[128,128]{1,0:T(8,...) custom-call(f32[256,128]{1,0:T(8,128)} %x_hbm.1, ...), custom_call_target="tpu_custom_call" | custom-call | tf_op jit(solution)/shard_map/send/pallas_call | solution.py:180
  2.8 4.6 %all-to-all-start = ((f32[16,32,128]{2,1,0:T(8,128)}), f32[16,32,128]{2,1,0:T(8,128)S(1)}, u32[]{:S(2)}, u32[]{:S(2)}) async-start(f32[16,32,128]{2,1,0:T(8,128)} %get-tuple-element.27), calls=%async_computation | async-start | bytes 524288 | tf_op jit(solution)/shard_map/all_to_all | solution.py:240
  7.4 0.4 %collective-permute-start = (f32[128,128]{1,0:T(8,128)S(1)}, f32[128,128]{1,0:T(8,128)S(1)}, u32[]{:S(2)}, u32[]{:S(2)}) collective-permute-start(f32[128,128]{1,0:T(8,128)S(1)} %get-tuple-element.20), channel_id=1, source_target_pairs={{0,1},{1,0},{2,3},{3,2},{4,5},{5,4},{6,7},{7,6},{8,9},{9,8},{10,11... | collective-permute-start | bytes 196616 | tf_op jit(solution)/shard_map/ppermute | solution.py:243
  7.8 0.4 %collective-permute-start.2 = (f32[128,128]{1,0:T(8,128)S(1)}, f32[128,128]{1,0:T(8,128)S(1)}, u32[]{:S(2)}, u32[]{:S(2)}) collective-permute-start(f32[128,128]{1,0:T(8,128)S(1)} %get-tuple-element.24.out_b_ref), channel_id=1, source_target_pairs={{1,2},{2,1},{3,4},{4,3},{5,6},{6,5},{7,8},{8,7},{9,10},{10,9},{11,... | collective-permute-start | bytes 196616 | tf_op jit(solution)/shard_map/ppermute | solution.py:244
  8.2 1.3 %collective-permute-start.4 = (f32[128,128]{1,0:T(8,128)S(1)}, f32[128,128]{1,0:T(8,128)S(1)}, u32[]{:S(2)}, u32[]{:S(2)}) collective-permute-start(f32[128,128]{1,0:T(8,128)S(1)} %get-tuple-element.35), channel_id=1, source_target_pairs={{1,2},{2,1},{3,4},{4,3},{5,6},{6,5},{7,8},{8,7},{9,10},{10,9},{11,... | collective-permute-start | bytes 196616 | tf_op jit(solution)/shard_map/ppermute | solution.py:245
  9.5 0.0 collective-permute-done.a_ref
  9.5 0.3 %across.1 = (f32[128,128]{1,0:T(8,128)S(1)}, f32[256,128]{1,0:T(8,128)S(1)}) custom-call(f32[128,128]{1,0:T(8,128)S(1)} %collective-permute-done.a_ref, f32[128,128]{1,0:T(8,128)S(1)} %get-tuple-element.21.m_ref, f32[384,384]{1,0:T(8,128)S(1)} %get-tuple-element.22.schur_ref), custom_call_target="tpu_custom_call" | custom-call | tf_op jit(solution)/shard_map/across/pallas_call | solution.py:180
  9.8 0.5 %collective-permute-start.1 = (f32[128,128]{1,0:T(8,128)S(1)}, f32[128,128]{1,0:T(8,128)S(1)}, u32[]{:S(2)}, u32[]{:S(2)}) collective-permute-start(f32[128,128]{1,0:T(8,128)S(1)} %get-tuple-element.23), channel_id=1, source_target_pairs={{1,2},{2,1},{3,4},{4,3},{5,6},{6,5},{7,8},{8,7},{9,10},{10,9},{11,... | collective-permute-start | bytes 196616 | tf_op jit(solution)/shard_map/ppermute | solution.py:247
  10.3 1.7 %collective-permute-done.2.got_ref = f32[128,128]{1,0:T(8,128)S(1)} collective-permute-done((f32[128,128]{1,0:T(8,128)S(1)}, f32[128,128]{1,0:T(8,128)S(1)}, u32[]{:S(2)}, u32[]{:S(2)}) %collective-permute-start.2) | collective-permute-done | bytes 65568 | tf_op jit(solution)/shard_map/ppermute | solution.py:244
  12.0 0.2 force.1
  12.2 4.8 %collective-permute-start.3 = (f32[128,128]{1,0:T(8,128)S(1)}, f32[128,128]{1,0:T(8,128)S(1)}, u32[]{:S(2)}, u32[]{:S(2)}) collective-permute-start(f32[128,128]{1,0:T(8,128)S(1)} %force.1), channel_id=1, source_target_pairs={{0,1},{1,0},{2,3},{3,2},{4,5},{5,4},{6,7},{7,6},{8,9},{9,8},{10,11... | collective-permute-start | bytes 196616 | tf_op jit(solution)/shard_map/ppermute | solution.py:252
  17.0 0.2 %base.1 = (f32[256,128]{1,0:T(8,128)S(1)}, bf16[256,512]{1,0:T(8,128)(2,1)S(1)}, bf16[256,512]{1,0:T(8,128)(2,1)S(1)}, f32[256,128]{1,0:T(8,128)S(1)}) custom-call(f32[256,128]{1,0:T(8,128)S(1)} %get-tuple-element.28.rhs_ref, f32[256,256]{1,0:T(8,128)S(1)} %get-tuple-element.29.near_ref, f32[256,128]{1,0:T(8,128)S(1)} %get-tuple-element.30.x_ref, ...), custom_call_target="tpu_custom_call" | custom-call | tf_op jit(solution)/shard_map/base/pallas_call | solution.py:180
  17.2 0.0 collective-permute-done.4.corner_ref
  17.3 0.4 %own.1.base_ref = f32[256,128]{1,0:T(8,128)S(1)} custom-call(f32[128,128]{1,0:T(8,128)S(1)} %collective-permute-done.2.got_ref, f32[128,128]{1,0:T(8,128)S(1)} %collective-permute-done.4.corner_ref, f32[128,128]{1,0:T(8,128)S(1)} %get-tuple-element.24.out_b_ref, f32[256,128]{1,0:T(8,128)S(1)} %get-tuple-element.25.part_ref._, ...), custom_call_target="tpu_custom_call" | custom-call | tf_op jit(solution)/shard_map/own/pallas_call | solution.py:180
  17.7 0.0 all-to-all-done
  17.7 0.3 %far.1.base_ref = f32[256,128]{1,0:T(8,128)S(1)} custom-call(f32[512,128]{1,0:T(8,128)S(1)} %bitcast.6, bf16[256,512]{1,0:T(8,128)(2,1)S(1)} %get-tuple-element.33.hi_ref, bf16[256,512]{1,0:T(8,128)(2,1)S(1)} %get-tuple-element.34.lo_ref, f32[256,128]{1,0:T(8,128)S(1)} %own.1.base_ref), custom_call_target="tpu_custom_call" | custom-call | tf_op jit(solution)/shard_map/far/pallas_call | solution.py:180
  18.0 0.0 collective-permute-done.1.sum_ref
  18.0 0.0 collective-permute-done.3.back_ref
  18.0 0.9 %final.1 = (f32[256,128]{1,0:T(8,128)}, f32[256,128]{1,0:T(8,128)}) custom-call(f32[128,128]{1,0:T(8,128)S(1)} %collective-permute-done.1.sum_ref, f32[128,128]{1,0:T(8,128)S(1)} %collective-permute-done.3.back_ref, bf16[256,384]{1,0:T(8,128)(2,1)S(1)} %get-tuple-element.26.sel_ref, f32[256,128]{1,0:T(8,128)S(1)} %far.1.base_ref, ...), custom_call_target="tpu_custom_call" | custom-call | tf_op jit(solution)/shard_map/final/pallas_call | solution.py:180
Async XLA Ops:
  2.8 14.9 %all-to-all-start = ((f32[16,32,128]{2,1,0:T(8,128)}), f32[16,32,128]{2,1,0:T(8,128)S(1)}, u32[]{:S(2)}, u32[]{:S(2)}) async-start(f32[16,32,128]{2,1,0:T(8,128)} %get-tuple-element.27), calls=%async_computation | async-start | bytes 524288 | tf_op jit(solution)/shard_map/all_to_all | solution.py:240
  7.4 2.1 %collective-permute-start = (f32[128,128]{1,0:T(8,128)S(1)}, f32[128,128]{1,0:T(8,128)S(1)}, u32[]{:S(2)}, u32[]{:S(2)}) collective-permute-start(f32[128,128]{1,0:T(8,128)S(1)} %get-tuple-element.20), channel_id=1, source_target_pairs={{0,1},{1,0},{2,3},{3,2},{4,5},{5,4},{6,7},{7,6},{8,9},{9,8},{10,11... | collective-permute-start | bytes 196616 | tf_op jit(solution)/shard_map/ppermute | solution.py:243
  7.8 4.2 %collective-permute-start.2 = (f32[128,128]{1,0:T(8,128)S(1)}, f32[128,128]{1,0:T(8,128)S(1)}, u32[]{:S(2)}, u32[]{:S(2)}) collective-permute-start(f32[128,128]{1,0:T(8,128)S(1)} %get-tuple-element.24.out_b_ref), channel_id=1, source_target_pairs={{1,2},{2,1},{3,4},{4,3},{5,6},{6,5},{7,8},{8,7},{9,10},{10,9},{11,... | collective-permute-start | bytes 196616 | tf_op jit(solution)/shard_map/ppermute | solution.py:244
  8.2 9.0 %collective-permute-start.4 = (f32[128,128]{1,0:T(8,128)S(1)}, f32[128,128]{1,0:T(8,128)S(1)}, u32[]{:S(2)}, u32[]{:S(2)}) collective-permute-start(f32[128,128]{1,0:T(8,128)S(1)} %get-tuple-element.35), channel_id=1, source_target_pairs={{1,2},{2,1},{3,4},{4,3},{5,6},{6,5},{7,8},{8,7},{9,10},{10,9},{11,... | collective-permute-start | bytes 196616 | tf_op jit(solution)/shard_map/ppermute | solution.py:245
  9.8 8.2 %collective-permute-start.1 = (f32[128,128]{1,0:T(8,128)S(1)}, f32[128,128]{1,0:T(8,128)S(1)}, u32[]{:S(2)}, u32[]{:S(2)}) collective-permute-start(f32[128,128]{1,0:T(8,128)S(1)} %get-tuple-element.23), channel_id=1, source_target_pairs={{1,2},{2,1},{3,4},{4,3},{5,6},{6,5},{7,8},{8,7},{9,10},{10,9},{11,... | collective-permute-start | bytes 196616 | tf_op jit(solution)/shard_map/ppermute | solution.py:247
  12.2 5.8 %collective-permute-start.3 = (f32[128,128]{1,0:T(8,128)S(1)}, f32[128,128]{1,0:T(8,128)S(1)}, u32[]{:S(2)}, u32[]{:S(2)}) collective-permute-start(f32[128,128]{1,0:T(8,128)S(1)} %force.1), channel_id=1, source_target_pairs={{0,1},{1,0},{2,3},{3,2},{4,5},{5,4},{6,7},{7,6},{8,9},{9,8},{10,11... | collective-permute-start | bytes 196616 | tf_op jit(solution)/shard_map/ppermute | solution.py:252

commit v13 on v12

--- a/solution.py
+++ b/solution.py
@@ -147,7 +147,7 @@
     scale_ref[...] = jnp.broadcast_to(p_ref[...], (loads, n_rows)).T
 
 
-def force_kernel(got_ref, part_ref, schur_ref, fa_ref):
+def force_kernel(got_ref, part_ref, schur_ref, _, fa_ref):
     odd = is_odd()
     face = fa_ref.shape[0]
     block = schur_ref[pl.ds(place(odd, 0, face), face), pl.ds(place(odd, 2, face), face)]
@@ -248,7 +248,7 @@
     base, u_hi, u_lo, scale = call(
         base_kernel, "base", [field, factor, factor, field], (rhs, near, x, u, p, part)
     )
-    (f_a,) = call(force_kernel, "force", [block], (got, part, schur))
+    (f_a,) = call(force_kernel, "force", [block], (got, part, schur, base))
     back = lax.ppermute(f_a, "wide", inside)
     (base,) = call(own_kernel, "own", [field], (got, corner, out_b, part, schur, sel, base))
     (base,) = call(far_kernel, "far", [field], (gathered.reshape(tiles * top, loads), u_hi, u_lo, base))

time: 19.2 us -> 19.2 us (level)
    ppermute x1, waiting for transfers between devices: 1.71 us -> 1.46 us  [body(): got = lax.ppermute(out_b, ('groups', 'wide'), across)]
  transfers between devices with their start and end apart: 6 -> 6, of which waited for: 1 -> 2; matrix products, arithmetic and copies ran while one was open for 0% -> 0% of each run, Pallas kernels for 7% -> 7%
where the time goes in v13:
time: 19.2 us; the launch traced here: 18.8 us
  starting transfers between devices  12 us (62%)
  Pallas kernels  4.44 us (23%)
  waiting for transfers between devices  1.65 us (9%)
  between operations  0.69 us (4%)
    ppermute x1, starting transfers between devices, body(): back = lax.ppermute(f_a, 'wide', inside)  4.82 us
    all_to_all x1, starting transfers between devices, body(): lax.all_to_all(coeff, 'wide', split_axis=0, concat_axis=0, tiled=True, ax...  4.62 us
    pallas_call x7, Pallas kernels, call(): pl.pallas_call(kernel, out_shape=tuple((space(s, t) for space, (s, t) in...  4.44 us
    ppermute x1, waiting for transfers between devices, body(): got = lax.ppermute(out_b, ('groups', 'wide'), across)  1.46 us
    ppermute x1, starting transfers between devices, body(): corner = lax.ppermute(corner, ('groups', 'wide'), across)  1.33 us
    ppermute x1, starting transfers between devices, body(): sums = lax.ppermute(pay, ('groups', 'wide'), across)  0.48 us
    ppermute x1, starting transfers between devices, body(): got = lax.ppermute(out_b, ('groups', 'wide'), across)  0.42 us
  transfers between devices with their start and end apart: 6, of which 2 were waited for; matrix products, arithmetic and copies ran while one was open for 0% of the time, Pallas kernels for 7%

profile of v13, /device:TPU:19, one launch (start us, length us, event | category | flops | bytes accessed | tf_op | source)
XLA Modules:
  0.0 18.8 jit_solution(9375531284807277867)
XLA Ops:
  0.6 2.2 %send.1 = (f32[16,32,128]{2,1,0:T(8,128)}, f32[128,128]{1,0:T(8,128)S(1)}, f32[128,128]{1,0:T(8,128)S(1)}, f32[128,128]{1,0:T(8,128)S(1)}, f32[128,128]{1,0:T(8,...) custom-call(f32[256,128]{1,0:T(8,128)} %x_hbm.1, ...), custom_call_target="tpu_custom_call" | custom-call | tf_op jit(solution)/shard_map/send/pallas_call | solution.py:180
  2.8 4.6 %all-to-all-start = ((f32[16,32,128]{2,1,0:T(8,128)}), f32[16,32,128]{2,1,0:T(8,128)S(1)}, u32[]{:S(2)}, u32[]{:S(2)}) async-start(f32[16,32,128]{2,1,0:T(8,128)} %get-tuple-element.33), calls=%async_computation | async-start | bytes 524288 | tf_op jit(solution)/shard_map/all_to_all | solution.py:240
  7.4 0.4 %collective-permute-start = (f32[128,128]{1,0:T(8,128)S(1)}, f32[128,128]{1,0:T(8,128)S(1)}, u32[]{:S(2)}, u32[]{:S(2)}) collective-permute-start(f32[128,128]{1,0:T(8,128)S(1)} %get-tuple-element.20), channel_id=1, source_target_pairs={{0,1},{1,0},{2,3},{3,2},{4,5},{5,4},{6,7},{7,6},{8,9},{9,8},{10,11... | collective-permute-start | bytes 196616 | tf_op jit(solution)/shard_map/ppermute | solution.py:243
  7.8 0.4 %collective-permute-start.2 = (f32[128,128]{1,0:T(8,128)S(1)}, f32[128,128]{1,0:T(8,128)S(1)}, u32[]{:S(2)}, u32[]{:S(2)}) collective-permute-start(f32[128,128]{1,0:T(8,128)S(1)} %get-tuple-element.24.out_b_ref), channel_id=1, source_target_pairs={{1,2},{2,1},{3,4},{4,3},{5,6},{6,5},{7,8},{8,7},{9,10},{10,9},{11,... | collective-permute-start | bytes 196616 | tf_op jit(solution)/shard_map/ppermute | solution.py:244
  8.2 1.3 %collective-permute-start.4 = (f32[128,128]{1,0:T(8,128)S(1)}, f32[128,128]{1,0:T(8,128)S(1)}, u32[]{:S(2)}, u32[]{:S(2)}) collective-permute-start(f32[128,128]{1,0:T(8,128)S(1)} %get-tuple-element.36), channel_id=1, source_target_pairs={{1,2},{2,1},{3,4},{4,3},{5,6},{6,5},{7,8},{8,7},{9,10},{10,9},{11,... | collective-permute-start | bytes 196616 | tf_op jit(solution)/shard_map/ppermute | solution.py:245
  9.5 0.0 collective-permute-done.a_ref
  9.5 0.3 %across.1 = (f32[128,128]{1,0:T(8,128)S(1)}, f32[256,128]{1,0:T(8,128)S(1)}) custom-call(f32[128,128]{1,0:T(8,128)S(1)} %collective-permute-done.a_ref, f32[128,128]{1,0:T(8,128)S(1)} %get-tuple-element.21.m_ref, f32[384,384]{1,0:T(8,128)S(1)} %get-tuple-element.22.schur_ref), custom_call_target="tpu_custom_call" | custom-call | tf_op jit(solution)/shard_map/across/pallas_call | solution.py:180
  9.8 0.5 %collective-permute-start.1 = (f32[128,128]{1,0:T(8,128)S(1)}, f32[128,128]{1,0:T(8,128)S(1)}, u32[]{:S(2)}, u32[]{:S(2)}) collective-permute-start(f32[128,128]{1,0:T(8,128)S(1)} %get-tuple-element.23), channel_id=1, source_target_pairs={{1,2},{2,1},{3,4},{4,3},{5,6},{6,5},{7,8},{8,7},{9,10},{10,9},{11,... | collective-permute-start | bytes 196616 | tf_op jit(solution)/shard_map/ppermute | solution.py:247
  10.3 0.2 %base.1 = (f32[256,128]{1,0:T(8,128)S(1)}, bf16[256,512]{1,0:T(8,128)(2,1)S(1)}, bf16[256,512]{1,0:T(8,128)(2,1)S(1)}, f32[256,128]{1,0:T(8,128)S(1)}) custom-call(f32[256,128]{1,0:T(8,128)S(1)} %get-tuple-element.26.rhs_ref, f32[256,256]{1,0:T(8,128)S(1)} %get-tuple-element.27.near_ref, f32[256,128]{1,0:T(8,128)S(1)} %get-tuple-element.28.x_ref, ...), custom_call_target="tpu_custom_call" | custom-call | tf_op jit(solution)/shard_map/base/pallas_call | solution.py:180
  10.5 1.5 %collective-permute-done.2.got_ref = f32[128,128]{1,0:T(8,128)S(1)} collective-permute-done((f32[128,128]{1,0:T(8,128)S(1)}, f32[128,128]{1,0:T(8,128)S(1)}, u32[]{:S(2)}, u32[]{:S(2)}) %collective-permute-start.2) | collective-permute-done | bytes 65568 | tf_op jit(solution)/shard_map/ppermute | solution.py:244
  12.0 0.2 force.1
  12.2 4.8 %collective-permute-start.3 = (f32[128,128]{1,0:T(8,128)S(1)}, f32[128,128]{1,0:T(8,128)S(1)}, u32[]{:S(2)}, u32[]{:S(2)}) collective-permute-start(f32[128,128]{1,0:T(8,128)S(1)} %force.1), channel_id=1, source_target_pairs={{0,1},{1,0},{2,3},{3,2},{4,5},{5,4},{6,7},{7,6},{8,9},{9,8},{10,11... | collective-permute-start | bytes 196616 | tf_op jit(solution)/shard_map/ppermute | solution.py:252
  17.0 0.0 collective-permute-done.4.corner_ref
  17.0 0.4 %own.1.base_ref = f32[256,128]{1,0:T(8,128)S(1)} custom-call(f32[128,128]{1,0:T(8,128)S(1)} %collective-permute-done.2.got_ref, f32[128,128]{1,0:T(8,128)S(1)} %collective-permute-done.4.corner_ref, f32[128,128]{1,0:T(8,128)S(1)} %get-tuple-element.24.out_b_ref, f32[256,128]{1,0:T(8,128)S(1)} %get-tuple-element.25._.part_ref, ...), custom_call_target="tpu_custom_call" | custom-call | tf_op jit(solution)/shard_map/own/pallas_call | solution.py:180
  17.4 0.0 all-to-all-done
  17.4 0.3 %far.1.base_ref = f32[256,128]{1,0:T(8,128)S(1)} custom-call(f32[512,128]{1,0:T(8,128)S(1)} %bitcast.6, bf16[256,512]{1,0:T(8,128)(2,1)S(1)} %get-tuple-element.34.hi_ref, bf16[256,512]{1,0:T(8,128)(2,1)S(1)} %get-tuple-element.35.lo_ref, f32[256,128]{1,0:T(8,128)S(1)} %own.1.base_ref), custom_call_target="tpu_custom_call" | custom-call | tf_op jit(solution)/shard_map/far/pallas_call | solution.py:180
  17.7 0.0 collective-permute-done.1.sum_ref
  17.7 0.2 collective-permute-done.3.back_ref
  17.9 0.9 %final.1 = (f32[256,128]{1,0:T(8,128)}, f32[256,128]{1,0:T(8,128)}) custom-call(f32[128,128]{1,0:T(8,128)S(1)} %collective-permute-done.1.sum_ref, f32[128,128]{1,0:T(8,128)S(1)} %collective-permute-done.3.back_ref, bf16[256,384]{1,0:T(8,128)(2,1)S(1)} %get-tuple-element.32.sel_ref, f32[256,128]{1,0:T(8,128)S(1)} %far.1.base_ref, ...), custom_call_target="tpu_custom_call" | custom-call | tf_op jit(solution)/shard_map/final/pallas_call | solution.py:180
Async XLA Ops:
  2.8 14.6 %all-to-all-start = ((f32[16,32,128]{2,1,0:T(8,128)}), f32[16,32,128]{2,1,0:T(8,128)S(1)}, u32[]{:S(2)}, u32[]{:S(2)}) async-start(f32[16,32,128]{2,1,0:T(8,128)} %get-tuple-element.33), calls=%async_computation | async-start | bytes 524288 | tf_op jit(solution)/shard_map/all_to_all | solution.py:240
  7.4 2.1 %collective-permute-start = (f32[128,128]{1,0:T(8,128)S(1)}, f32[128,128]{1,0:T(8,128)S(1)}, u32[]{:S(2)}, u32[]{:S(2)}) collective-permute-start(f32[128,128]{1,0:T(8,128)S(1)} %get-tuple-element.20), channel_id=1, source_target_pairs={{0,1},{1,0},{2,3},{3,2},{4,5},{5,4},{6,7},{7,6},{8,9},{9,8},{10,11... | collective-permute-start | bytes 196616 | tf_op jit(solution)/shard_map/ppermute | solution.py:243
  7.8 4.2 %collective-permute-start.2 = (f32[128,128]{1,0:T(8,128)S(1)}, f32[128,128]{1,0:T(8,128)S(1)}, u32[]{:S(2)}, u32[]{:S(2)}) collective-permute-start(f32[128,128]{1,0:T(8,128)S(1)} %get-tuple-element.24.out_b_ref), channel_id=1, source_target_pairs={{1,2},{2,1},{3,4},{4,3},{5,6},{6,5},{7,8},{8,7},{9,10},{10,9},{11,... | collective-permute-start | bytes 196616 | tf_op jit(solution)/shard_map/ppermute | solution.py:244
  8.2 8.8 %collective-permute-start.4 = (f32[128,128]{1,0:T(8,128)S(1)}, f32[128,128]{1,0:T(8,128)S(1)}, u32[]{:S(2)}, u32[]{:S(2)}) collective-permute-start(f32[128,128]{1,0:T(8,128)S(1)} %get-tuple-element.36), channel_id=1, source_target_pairs={{1,2},{2,1},{3,4},{4,3},{5,6},{6,5},{7,8},{8,7},{9,10},{10,9},{11,... | collective-permute-start | bytes 196616 | tf_op jit(solution)/shard_map/ppermute | solution.py:245
  9.8 7.9 %collective-permute-start.1 = (f32[128,128]{1,0:T(8,128)S(1)}, f32[128,128]{1,0:T(8,128)S(1)}, u32[]{:S(2)}, u32[]{:S(2)}) collective-permute-start(f32[128,128]{1,0:T(8,128)S(1)} %get-tuple-element.23), channel_id=1, source_target_pairs={{1,2},{2,1},{3,4},{4,3},{5,6},{6,5},{7,8},{8,7},{9,10},{10,9},{11,... | collective-permute-start | bytes 196616 | tf_op jit(solution)/shard_map/ppermute | solution.py:247
  12.2 5.7 %collective-permute-start.3 = (f32[128,128]{1,0:T(8,128)S(1)}, f32[128,128]{1,0:T(8,128)S(1)}, u32[]{:S(2)}, u32[]{:S(2)}) collective-permute-start(f32[128,128]{1,0:T(8,128)S(1)} %force.1), channel_id=1, source_target_pairs={{0,1},{1,0},{2,3},{3,2},{4,5},{5,4},{6,7},{7,6},{8,9},{9,8},{10,11... | collective-permute-start | bytes 196616 | tf_op jit(solution)/shard_map/ppermute | solution.py:252
